TPU v7x, 32 devices: a whole 2x2x4 slice. The times are simulated.
32 devices in a mesh: dp: 8 (over z, y), cent: 4 (over x, core).
Axes of the slice: x: 2, y: 2, z: 4, core: 2. Of those that a mesh axis runs over, the one named last changes fastest.
Arguments:
- frames: bfloat16 [32768, 1024], P(('dp', 'cent')), may hold values from -6 to 6
- video_length: int32 [32, 128], P(('dp', 'cent')), may hold values from 1 to 16, 1024 in all within a row
- video_owner: int32 [32, 128], P(('dp', 'cent')), may hold values from 0 to 7, as said below
- video_cluster: int32 [32, 128], P(('dp', 'cent')), may hold values from 0 to 255
- frame_code: int32 [32768], P(('dp', 'cent')), may hold values from 0 to 511, as said below
- old_coarse: bfloat16 [2048, 1024], P('dp'), may hold values from -6 to 6
- old_codes: float32 [512, 1024], P(('dp', 'cent')), may hold values from -6 to 6
Outputs:
- new_coarse: float32 [2048, 1024], P(('dp', 'cent'))
- new_codes: float32 [512, 1024], P(('dp', 'cent'))
Inputs may be any that keep to these rules, and one draw needn't show every extreme that they name: `video_owner`: each device's row of 128 videos names one index of dp at most 32 times; in every draw some index of dp is named exactly 32 times in every device's row. `frame_code`: among each device's 1024 frames at most 256 have codes in one block of 64 codes (codes b * 64 to (b + 1) * 64 - 1); in every draw some block gets exactly 256 from every device.
All inputs are finite; a program needn't handle non-finite values.
Results may differ from a plain program's by a relative error of at most 0.0015.
Values may be sent and summed in bfloat16 or wider, within the bound.
No kernel may reach another device: no remote copies, remote signals or barrier semaphores. Data moves between devices by JAX's collectives and lax.ppermute only.
A program may use at most 64 MiB of HBM per device.

v0:
```python
import jax
import jax.numpy as jnp
from jax import lax
from jax.sharding import PartitionSpec as P

code_prior = 16.0


def owner_slots(target, target_count, capacity):
    matches = (target[:, None] == jnp.arange(target_count, dtype=jnp.int32)[None, :]).astype(
        jnp.int32
    )
    before = jnp.cumsum(matches, axis=0) - matches
    slot_rank = jnp.sum(before * matches, axis=1)
    return target * capacity + slot_rank


def invert_slots(slot_list, slot_total):
    item_index = jnp.arange(slot_list.shape[0], dtype=jnp.int32)
    source = jnp.zeros((slot_total,), jnp.int32).at[slot_list].set(item_index)
    filled = jnp.zeros((slot_total,), jnp.int32).at[slot_list].set(1)
    return (source, filled)


def body(frames, video_length, video_owner, video_cluster, frame_code, old_coarse, old_codes):
    dp_count = lax.axis_size("dp")
    cent_count = lax.axis_size("cent")
    frame_count, features = frames.shape
    video_count = video_length.shape[1]
    coarse_rows = old_coarse.shape[0]
    code_share = old_codes.shape[0]
    code_block = code_share * cent_count
    cap_video = max(2, 2 * video_count // dp_count)
    cap_frame = max(2, 2 * frame_count // dp_count)
    lengths = video_length[0]
    target = video_owner[0]
    cluster = video_cluster[0]
    video_ends = jnp.cumsum(lengths)
    video_starts = video_ends - lengths
    position = jnp.arange(frame_count, dtype=jnp.int32)
    member = (
        (position[None, :] >= video_starts[:, None]) & (position[None, :] < video_ends[:, None])
    ).astype(jnp.bfloat16)
    video_sums = jnp.dot(member, frames, preferred_element_type=jnp.float32)
    pooled = (video_sums / lengths[:, None].astype(jnp.float32)).astype(jnp.bfloat16)
    video_slot = owner_slots(target, dp_count, cap_video)
    source, filled = invert_slots(video_slot, dp_count * cap_video)
    send_rows = jnp.where(filled[:, None] > 0, pooled[source], jnp.zeros((), jnp.bfloat16))
    send_codes = jnp.where(filled > 0, cluster[source], -1)
    got_rows, got_codes = (
        lax.all_to_all(
            send_rows.reshape(dp_count, cap_video, features),
            "dp",
            split_axis=0,
            concat_axis=0,
            tiled=True,
        ),
        lax.all_to_all(
            send_codes.reshape(dp_count, cap_video), "dp", split_axis=0, concat_axis=0, tiled=True
        ),
    )
    got_rows = got_rows.reshape(-1, features)
    got_codes = got_codes.reshape(-1)
    table_index = jnp.arange(coarse_rows, dtype=jnp.int32)
    coarse_pick = (got_codes[None, :] == table_index[:, None]).astype(jnp.bfloat16)
    coarse_sum = jnp.dot(coarse_pick, got_rows, preferred_element_type=jnp.float32)
    coarse_count = jnp.sum(coarse_pick.astype(jnp.float32), axis=1)
    quarter = coarse_rows // cent_count
    part_sum, part_count = (
        lax.psum_scatter(coarse_sum, "cent", scatter_dimension=0, tiled=True),
        lax.psum_scatter(coarse_count, "cent", scatter_dimension=0, tiled=True),
    )
    first_row = lax.axis_index("cent") * quarter
    old_part = lax.dynamic_slice_in_dim(old_coarse, first_row, quarter, 0).astype(jnp.float32)
    new_coarse = (part_sum + old_part) / (part_count[:, None] + 1.0)
    anchor_table = lax.all_gather(new_coarse.astype(jnp.bfloat16), "cent", axis=0, tiled=True)
    slot_anchor = jnp.dot(coarse_pick.T, anchor_table, preferred_element_type=jnp.float32).astype(
        jnp.bfloat16
    )
    returned = lax.all_to_all(
        slot_anchor.reshape(dp_count, cap_video, features),
        "dp",
        split_axis=0,
        concat_axis=0,
        tiled=True,
    )
    video_anchor = returned.reshape(-1, features)[video_slot]
    frame_anchor = jnp.dot(member.T, video_anchor, preferred_element_type=jnp.float32)
    residual = (frames - frame_anchor).astype(jnp.bfloat16)
    code_target = frame_code // code_block
    code_offset = frame_code - code_target * code_block
    frame_slot = owner_slots(code_target, dp_count, cap_frame)
    source, filled = invert_slots(frame_slot, dp_count * cap_frame)
    slot_rows = jnp.where(filled[:, None] > 0, residual[source], jnp.zeros((), jnp.bfloat16))
    slot_codes = jnp.where(filled > 0, code_offset[source], -1)
    code_rows, code_ids = (
        lax.all_to_all(
            slot_rows.reshape(dp_count, cap_frame, features),
            "dp",
            split_axis=0,
            concat_axis=0,
            tiled=True,
        ),
        lax.all_to_all(
            slot_codes.reshape(dp_count, cap_frame), "dp", split_axis=0, concat_axis=0, tiled=True
        ),
    )
    code_index = jnp.arange(code_block, dtype=jnp.int32)
    code_pick = (code_ids.reshape(-1)[None, :] == code_index[:, None]).astype(jnp.bfloat16)
    code_sum = jnp.dot(
        code_pick, code_rows.reshape(-1, features), preferred_element_type=jnp.float32
    )
    code_count = jnp.sum(code_pick.astype(jnp.float32), axis=1)
    own_sum, own_count = (
        lax.psum_scatter(code_sum, "cent", scatter_dimension=0, tiled=True),
        lax.psum_scatter(code_count, "cent", scatter_dimension=0, tiled=True),
    )
    new_codes = (own_sum + code_prior * old_codes) / (own_count[:, None] + code_prior)
    return (new_coarse, new_codes)


def solution(mesh):
    placed = (
        P(("dp", "cent"), None),
        P(("dp", "cent"), None),
        P(("dp", "cent"), None),
        P(("dp", "cent"), None),
        P(("dp", "cent")),
        P("dp", None),
        P(("dp", "cent"), None),
    )
    return jax.shard_map(
        body,
        mesh=mesh,
        in_specs=placed,
        out_specs=(P(("dp", "cent"), None), P(("dp", "cent"), None)),
        check_vma=False,
    )
```

profile of v0, /device:TPU:0, one launch (start us, length us, event | category | flops | bytes accessed | tf_op | source)
XLA Modules:
  0.0 256.1 jit_solution(5853091058785813855)
XLA Ops:
  7.2 0.0 copy-start
  7.2 0.7 fusion.15
  7.9 0.2 reduce_window_sum.33
  8.1 0.8 select_reduce_fusion
  8.9 0.7 fusion.27
  9.6 1.0 scatter_custom_fusion.1
  10.6 1.0 scatter_custom_fusion
  11.6 0.0 copy-done
  11.6 1.9 gather_fusion
  13.5 0.7 all_to_all.21
  14.2 7.3 %all-to-all-start = ((s32[8,1,32]{2,1,0:T(1,128)}), s32[8,1,32]{2,1,0:T(1,128)S(1)}, u32[]{:S(2)}, u32[]{:S(2)}) async-start(s32[8,1,32]{2,1,0:T(1,128)} %all_to_all.21), calls=%async_computation | async-start | bytes 8192 | tf_op jit(solution)/shard_map/all_to_all | solution.py:58
  21.5 0.7 bitcast_convert_fusion
  22.1 0.8 copy.12
  22.9 0.2 reduce-window.14
  23.1 0.1 reduce.1
  23.2 0.7 bitcast_subtract_fusion
  23.8 0.1 broadcast_in_dim.71
  23.9 2.1 fusion
  26.0 0.0 copy-start.2
  26.0 1.2 gather_fusion.1
  27.2 0.9 broadcast_select_fusion.1
  28.1 0.0 all-to-all-done
  28.1 6.0 %all-to-all-start.1 = ((bf16[8,32,1024]{2,1,0:T(8,128)(2,1)}), bf16[8,32,1024]{2,1,0:T(8,128)(2,1)S(1)}, u32[]{:S(2)}, u32[]{:S(2)}) async-start(bf16[8,32,1024]{2,1,0:T(8,128)(2,1)} %broadcast_select_fusion.1), calls=%async_computation.1 | async-start | bytes 1048576 | tf_op jit(solution)/shard_map/all_to_all | solution.py:51
  34.1 0.0 reduce-scatter.3.cloned.1.call-start
  34.1 0.5 broadcast.160
  34.7 0.7 reduce.6
  35.3 0.1 eq.72
  35.4 12.7 %all-to-all-done.1 = bf16[8,32,1024]{2,1,0:T(8,128)(2,1)S(1)} async-done(((bf16[8,32,1024]{2,1,0:T(8,128)(2,1)}), bf16[8,32,1024]{2,1,0:T(8,128)(2,1)S(1)}, u32[]{:S(2)}, u32[]{:S(2)}) %all-to-all-start.1) | async-done | bytes 524320 | tf_op jit(solution)/shard_map/all_to_all | solution.py:51
  48.1 1.3 fusion.12
  49.4 0.0 reduce-scatter.3.cloned.1.call-update
  49.4 0.0 copy-done.2
  49.4 2.3 reduce-window.18
  51.7 0.3 slice_reduce_fusion
  52.0 0.2 reduce-window.19
  52.2 0.1 add_bitcast_fusion
  52.3 4.3 %scatter_custom_fusion.2 = s32[2048]{0:T(1024)S(1)} fusion(s32[1024]{0:T(1024)S(1)} %get-tuple-element.10, s32[1024]{0:T(1024)S(1)} %ne.14, s32[]{:T(128)} %constant.17.clone.1), kind=kCustom, calls=%fused_computation.63 | custom fusion | bytes 8196 | tf_op jit(solution)/shard_map/scatter | solution.py:21
  56.6 4.3 %scatter_custom_fusion.3 = s32[2048]{0:T(1024)S(1)} fusion(s32[1024]{0:T(1024)S(1)} %get-tuple-element.10, s32[1024]{0:T(1024)S(1)} %iota.29, s32[]{:T(128)} %constant.17.clone.1), kind=kCustom, calls=%fused_computation.60 | custom fusion | bytes 8196 | tf_op jit(solution)/shard_map/scatter | solution.py:20
  61.0 0.0 copy-start.3
  61.0 8.6 %gather_fusion.2 = s32[2048]{0:T(1024)S(1)} fusion(s32[1024]{0:T(1024)S(1)} %get-tuple-element.11, s32[2048]{0:T(1024)S(1)} %fusion.20), kind=kCustom, calls=%fused_computation.2 | custom fusion | bytes 24576 | tf_op jit(solution)/shard_map/gather | solution.py:95
  69.6 0.6 broadcast_select_fusion.2
  70.2 3.6 %all-to-all-start.2 = ((s32[8,1,256]{2,1,0:T(1,128)}), s32[8,1,256]{2,1,0:T(1,128)S(1)}, u32[]{:S(2)}, u32[]{:S(2)}) async-start(s32[8,1,256]{2,1,0:T(1,128)} %bitcast.11), calls=%async_computation.3 | async-start | bytes 16384 | tf_op jit(solution)/shard_map/all_to_all | solution.py:104
  73.8 0.0 copy-done.3
  73.8 0.6 dynamic-slice
  75.0 0.1 convert_reduce_fusion.1
  75.1 5.2 %all-to-all-done.2 = s32[8,1,256]{2,1,0:T(1,128)S(1)} async-done(((s32[8,1,256]{2,1,0:T(1,128)}), s32[8,1,256]{2,1,0:T(1,128)S(1)}, u32[]{:S(2)}, u32[]{:S(2)}) %all-to-all-start.2) | async-done | bytes 8224 | tf_op jit(solution)/shard_map/all_to_all | solution.py:104
  80.3 0.2 convert_reduce_fusion
  80.5 5.7 %all-reduce.2 = (f32[256]{0:T(256)S(1)}, f32[64]{0:T(128)S(1)}) all-reduce(f32[256]{0:T(256)S(1)} %convert_reduce_fusion.1, f32[64]{0:T(128)S(1)} %convert_reduce_fusion), channel_id=3, replica_groups=mesh['dp'=8,'cent'=4] {'cent'}, use_global_device_ids=true, to_apply=%region_7.8.clone | all-reduce | flops 320 | bytes 2560
  86.1 0.1 dynamic-slice_add_fusion.1
  86.2 1.8 fusion.33
  88.0 7.4 %all_gather.3 = bf16[256,1024]{1,0:T(8,128)(2,1)S(1)} all-gather(bf16[64,1024]{1,0:T(8,128)(2,1)S(1)} %get-tuple-element.4), channel_id=1, replica_groups=mesh['dp'=8,'cent'=4] {'cent'}, dimensions={0}, use_global_device_ids=true | all-gather | bytes 655360 | tf_op jit(solution)/shard_map/all_gather | solution.py:76
  95.4 1.1 convolution_convert_fusion
  96.5 3.5 %all-to-all-start.3 = ((bf16[8,32,1024]{2,1,0:T(8,128)(2,1)}), bf16[8,32,1024]{2,1,0:T(8,128)(2,1)S(1)}, u32[]{:S(2)}, u32[]{:S(2)}) async-start(bf16[8,32,1024]{2,1,0:T(8,128)(2,1)} %bitcast.13), calls=%async_computation.4 | async-start | bytes 1048576 | tf_op jit(solution)/shard_map/all_to_all | solution.py:80
  100.0 0.0 reduce-scatter.5.cloned.1.call-start
  100.1 15.1 %all-to-all-done.3 = bf16[8,32,1024]{2,1,0:T(8,128)(2,1)S(1)} async-done(((bf16[8,32,1024]{2,1,0:T(8,128)(2,1)}), bf16[8,32,1024]{2,1,0:T(8,128)(2,1)S(1)}, u32[]{:S(2)}, u32[]{:S(2)}) %all-to-all-start.3) | async-done | bytes 524320 | tf_op jit(solution)/shard_map/all_to_all | solution.py:80
  115.2 0.9 gather_fusion.3
  116.1 2.4 subtract_convert_fusion
  118.5 9.7 %gather_fusion.4 = bf16[2048,1024]{1,0:T(8,128)(2,1)} fusion(bf16[1024,1024]{1,0:T(8,128)(2,1)S(1)} %subtract_convert_fusion, s32[2048]{0:T(1024)S(1)} %fusion.20), kind=kCustom, calls=%fused_computation.4 | custom fusion | bytes 8396800 | tf_op jit(solution)/shard_map/gather | solution.py:94
  128.2 2.5 broadcast_select_fusion
  130.7 96.8 %all_to_all.33 = bf16[8,256,1024]{2,1,0:T(8,128)(2,1)S(1)} all-to-all(bf16[8,256,1024]{2,1,0:T(8,128)(2,1)S(1)} %broadcast_select_fusion), channel_id=1, replica_groups=mesh['dp'=8,'cent'=4] {'dp'}, dimensions={0} | all-to-all | bytes 8388608 | tf_op jit(solution)/shard_map/all_to_all | solution.py:97
  227.4 1.5 fusion.2
  229.0 0.0 reduce-scatter.5.cloned.1.call-update
  229.6 0.1 dynamic-slice_add_fusion
  229.7 18.0 %reduce-scatter.5.cloned.1.call-done = f32[16,1024]{1,0:T(8,128)} async-done(((f32[64,1024]{1,0:T(8,128)}), f32[16,1024]{1,0:T(8,128)}) %reduce-scatter.5.cloned.1.call-update) | async-done | bytes 65552 | tf_op jit(solution)/shard_map/reduce_scatter | solution.py:115
  247.7 1.5 add_divide_fusion.1
  (17 shorter events, 0.1 us)
Async XLA Ops:
  7.2 4.4 %copy-start = (s32[1,128]{1,0:T(1,128)S(1)}, s32[1,128]{1,0:T(1,128)}, u32[]{:S(2)}) copy-start(s32[1,128]{1,0:T(1,128)} %param.10) | copy-start | bytes 1540
  14.2 13.9 %all-to-all-start = ((s32[8,1,32]{2,1,0:T(1,128)}), s32[8,1,32]{2,1,0:T(1,128)S(1)}, u32[]{:S(2)}, u32[]{:S(2)}) async-start(s32[8,1,32]{2,1,0:T(1,128)} %all_to_all.21), calls=%async_computation | async-start | bytes 8192 | tf_op jit(solution)/shard_map/all_to_all | solution.py:58
  26.0 23.4 %copy-start.2 = (s32[1024]{0:T(1024)S(1)}, s32[1024]{0:T(1024)}, u32[]{:S(2)}) copy-start(s32[1024]{0:T(1024)} %param.11) | copy-start | bytes 12292
  28.1 20.0 %all-to-all-start.1 = ((bf16[8,32,1024]{2,1,0:T(8,128)(2,1)}), bf16[8,32,1024]{2,1,0:T(8,128)(2,1)S(1)}, u32[]{:S(2)}, u32[]{:S(2)}) async-start(bf16[8,32,1024]{2,1,0:T(8,128)(2,1)} %broadcast_select_fusion.1), calls=%async_computation.1 | async-start | bytes 1048576 | tf_op jit(solution)/shard_map/all_to_all | solution.py:51
  34.1 52.1 %reduce-scatter.3.cloned.1.call-start = ((), (), s32[]{:S(2)}) async-start(), calls=%async_computation.7 | async-start | bytes 1310720 | tf_op jit(solution)/shard_map/reduce_scatter | solution.py:70
  61.0 12.8 %copy-start.3 = (u32[32]{0:T(128)S(1)}, u32[32]{0:T(128)}, u32[]{:S(2)}) copy-start(u32[32]{0:T(128)} %constant.70) | copy-start | bytes 388
  70.2 10.1 %all-to-all-start.2 = ((s32[8,1,256]{2,1,0:T(1,128)}), s32[8,1,256]{2,1,0:T(1,128)S(1)}, u32[]{:S(2)}, u32[]{:S(2)}) async-start(s32[8,1,256]{2,1,0:T(1,128)} %bitcast.11), calls=%async_computation.3 | async-start | bytes 16384 | tf_op jit(solution)/shard_map/all_to_all | solution.py:104
  96.5 18.7 %all-to-all-start.3 = ((bf16[8,32,1024]{2,1,0:T(8,128)(2,1)}), bf16[8,32,1024]{2,1,0:T(8,128)(2,1)S(1)}, u32[]{:S(2)}, u32[]{:S(2)}) async-start(bf16[8,32,1024]{2,1,0:T(8,128)(2,1)} %bitcast.13), calls=%async_computation.4 | async-start | bytes 1048576 | tf_op jit(solution)/shard_map/all_to_all | solution.py:80
  100.0 147.6 %reduce-scatter.5.cloned.1.call-start = ((), (), s32[]{:S(2)}) async-start(), calls=%async_computation.8 | async-start | bytes 327680 | tf_op jit(solution)/shard_map/reduce_scatter | solution.py:115
  227.4 20.2 %copy-start.1 = (f32[16,1024]{1,0:T(8,128)S(1)}, f32[16,1024]{1,0:T(8,128)}, u32[]{:S(2)}) copy-start(f32[16,1024]{1,0:T(8,128)} %param.13) | copy-start | bytes 196612
Sparse Core Ops, SparseCore 0:
  49.5 23.9 reduce-scatter.2
  229.1 18.4 reduce-scatter.4
where the time goes:
time: 257 us; the launch traced here: 256 us
  blocking collectives  110 us (43%)
  waiting for transfers between devices  51 us (20%)
  local copies, waits for them, and re-layouts  35.8 us (14%)
  starting transfers between devices  20.5 us (8%)
  between operations  15.5 us (6%)
  other arithmetic  15 us (6%)
  matrix products  8.5 us (3%)
    all_to_all x1, blocking collectives, body(): lax.all_to_all(slot_rows.reshape(dp_count, cap_frame, features), 'dp', sp...  96.8 us
    reduce_scatter x1, waiting for transfers between devices, body(): lax.psum_scatter(code_sum, 'cent', scatter_dimension=0, tiled=True)  18 us
    all_to_all x1, waiting for transfers between devices, body(): lax.all_to_all(slot_anchor.reshape(dp_count, cap_video, features), 'dp',...  15.1 us
    all_to_all x1, waiting for transfers between devices, body(): lax.all_to_all(send_rows.reshape(dp_count, cap_video, features), 'dp', sp...  12.7 us
    gather x1, local copies, waits for them, and re-layouts, body(): residual[source]  9.67 us
    gather x1, local copies, waits for them, and re-layouts, body(): slot_codes = jnp.where(filled > 0, code_offset[source], -1)  8.58 us
    all_gather x1, blocking collectives, body(): lax.all_gather(new_coarse.astype(jnp.bfloat16), 'cent', axis=0, tiled=True)  7.4 us
    all_to_all x1, starting transfers between devices, body(): lax.all_to_all(send_codes.reshape(dp_count, cap_video), 'dp', split_axis=...  7.28 us
  transfers between devices with their start and end apart: 6, of which 4 were waited for; matrix products, arithmetic and copies ran while one was open for 12% of the time, Pallas kernels for 0%

commit v1 on v0

--- a/solution.py
+++ b/solution.py
@@ -1,9 +1,336 @@
+import functools
+
 import jax
 import jax.numpy as jnp
 from jax import lax
+from jax.experimental import pallas as pl
+from jax.experimental.pallas import tpu as pltpu
 from jax.sharding import PartitionSpec as P
 
 code_prior = 16.0
+LANES = 128
+EXACT = 256
+f32 = jnp.float32
+bf16 = jnp.bfloat16
+
+
+def iota(shape, axis):
+    return lax.broadcasted_iota(jnp.int32, shape, axis)
+
+
+def dot(left, right):
+    return jnp.dot(left, right, preferred_element_type=f32)
+
+
+def dot_rows(left, right):
+    return lax.dot_general(left, right, (((1,), (1,)), ((), ())), preferred_element_type=f32)
+
+
+def member_of_slots(length_ref, owner_ref, owners, capacity, frame_count):
+    videos = length_ref.shape[1]
+    slots = owners * capacity
+    lengths = length_ref[...].astype(f32)
+    owner = owner_ref[...]
+    match = (iota((owners, videos), 0) == owner).astype(f32)
+    earlier = (iota((videos, videos), 0) < iota((videos, videos), 1)).astype(bf16)
+    stacked = jnp.concatenate([match, jnp.broadcast_to(lengths, (8, videos))], axis=0)
+    before = dot(stacked.astype(bf16), earlier)
+    rank = jnp.sum(before[:owners] * match, axis=0, keepdims=True)
+    starts = before[owners : owners + 1]
+    slot = owner * capacity + rank.astype(jnp.int32)
+    video_of_slot = (iota((slots, videos), 0) == slot).astype(f32).astype(bf16)
+    high = jnp.floor(starts / 16.0) * 16.0
+    low = starts - high
+    tall = lambda row: jnp.broadcast_to(row, (LANES, videos)).astype(bf16)
+    start = dot_rows(video_of_slot, tall(high)) + dot_rows(video_of_slot, tall(low))
+    length = dot_rows(video_of_slot, tall(lengths))
+    first, last = start.astype(jnp.int32), (start + length).astype(jnp.int32)
+    member = jnp.concatenate(
+        [
+            (
+                (iota((slots, LANES), 1) + at >= first) & (iota((slots, LANES), 1) + at < last)
+            ).astype(f32)
+            for at in range(0, frame_count, LANES)
+        ],
+        axis=1,
+    ).astype(bf16)
+    return video_of_slot, first, length, member
+
+
+def code_matches(code_ref, code_total):
+    frame_count = code_ref.shape[1]
+    return (iota((code_total, frame_count), 0) == code_ref[...]).astype(f32).astype(bf16)
+
+
+def pool_kernel(sizes, length_ref, owner_ref, cluster_ref, code_ref, frames_hbm, send_ref, frames_ref, sem):
+    owners, cents, capacity, longest, code_total = sizes
+    copy = pltpu.make_async_copy(frames_hbm, frames_ref, sem)
+    copy.start()
+    me = lax.axis_index("cent")
+    frame_count, features = frames_hbm.shape
+    slots = owners * capacity
+    share = features // cents
+    video_of_slot, first, length, member = member_of_slots(
+        length_ref, owner_ref, owners, capacity, frame_count
+    )
+    code = (code_ref[...] - EXACT).astype(f32)
+    shifted = pltpu.roll(
+        jnp.broadcast_to(code, (longest, frame_count)),
+        frame_count - (longest - 1),
+        1,
+        stride=1,
+        stride_axis=0,
+    ).astype(bf16)
+    at_start = jnp.concatenate(
+        [
+            ((iota((slots, LANES), 1) + at == first) & (length > 0)).astype(f32)
+            for at in range(0, frame_count, LANES)
+        ],
+        axis=1,
+    ).astype(bf16)
+    slot_codes = dot_rows(shifted, at_start)
+    rows = lambda ref: jnp.broadcast_to(ref[...], (longest, ref.shape[1])).astype(f32).astype(bf16)
+    slot_length = dot_rows(rows(length_ref), video_of_slot)
+    slot_cluster = dot_rows(rows(cluster_ref), video_of_slot)
+    back = (longest - 1 - iota((longest, slots), 0)).astype(f32)
+    slot_codes = jnp.where(back < slot_length, slot_codes, 2.0 * EXACT).astype(bf16)
+    slot_cluster = jnp.where(slot_length > 0, slot_cluster, -1.0).astype(bf16)
+    lane = iota((slots, owners * LANES), 1)
+    place_owner, place_lane = lane // LANES, lane % LANES
+    wanted = iota((slots, owners * LANES), 0) - place_owner * capacity
+    code_lane = me * capacity
+    cluster_lane = lax.rem(me + 1, cents) * capacity
+    count_lane = lax.rem(me + 2, cents) * capacity
+    inside = (wanted >= 0) & (wanted < capacity)
+    place_codes = (inside & (place_lane == wanted + code_lane)).astype(f32).astype(bf16)
+    place_cluster = (inside & (place_lane == wanted + cluster_lane)).astype(f32).astype(bf16)
+    notes = dot(slot_codes, place_codes) + dot(slot_cluster, place_cluster)
+    counts = dot(code_matches(code_ref, code_total), jnp.ones((frame_count, LANES), bf16))
+    part = code_total // (owners * cents)
+    note_lane = iota((part, LANES), 1)
+    counted = (note_lane >= count_lane) & (note_lane < count_lane + capacity)
+    for owner in range(owners):
+        for cent in range(cents):
+            at = (owner * cents + cent) * part
+            note = jnp.where(
+                counted, counts[at : at + part], notes[:, owner * LANES : (owner + 1) * LANES]
+            )
+            send_ref[owner, cent, 2 * capacity :, :] = note.astype(bf16)
+    weight = 1.0 / jnp.maximum(length, 1.0)
+    copy.wait()
+    half = share // 2
+    for cent in range(cents):
+        sums = dot(member, frames_ref[:, cent * share : (cent + 1) * share])
+        for side in range(2):
+            pooled = (sums[:, side * half : (side + 1) * half] * weight).astype(bf16)
+            send_ref[:, cent, side * capacity : (side + 1) * capacity, :] = pooled.reshape(
+                owners, capacity, half
+            )
+
+
+def code_kernel(sizes, length_ref, owner_ref, code_ref, frames_hbm, pooled_ref, keep_ref, give_ref, frames_ref, sem):
+    owners, cents, capacity, longest, code_total = sizes
+    copy = pltpu.make_async_copy(frames_hbm, frames_ref, sem)
+    copy.start()
+    me = lax.axis_index("cent")
+    frame_count, features = frames_hbm.shape
+    share = features // cents
+    slots = owners * capacity
+    half = share // 2
+    _, _, _, member = member_of_slots(length_ref, owner_ref, owners, capacity, frame_count)
+    matches = code_matches(code_ref, code_total)
+    slot_counts = dot_rows(matches, member).astype(bf16)
+    copy.wait()
+    for step in range(cents):
+        cent = me ^ step
+        columns = pl.ds(pl.multiple_of(cent * share, share), share)
+        sums = dot(matches, frames_ref[:, columns])
+        for side in range(2):
+            pooled = pooled_ref[:, cent, side * capacity : (side + 1) * capacity, :].reshape(
+                slots, half
+            )
+            lanes = slice(side * half, (side + 1) * half)
+            centred = sums[:, lanes] - dot(slot_counts, pooled)
+            if step % 2:
+                give_ref[step // 2, :, lanes] = centred.astype(bf16)
+            else:
+                keep_ref[step // 2, :, lanes] = centred
+
+
+def owner_kernel(sizes, got_ref, old_hbm, keep_ref, near_ref, far_ref, code_ref, new_ref, count_ref, old_ref, sem):
+    owners, cents, capacity, longest, code_total = sizes
+    me = lax.axis_index("cent")
+    share = old_ref.shape[1]
+    copy = pltpu.make_async_copy(
+        old_hbm.at[:, pl.ds(pl.multiple_of(me * share, share), share)], old_ref, sem
+    )
+    copy.start()
+    clusters = old_ref.shape[0]
+    sources = owners * cents
+    segment = iota((longest, LANES), 1) // capacity
+    count = jnp.zeros((longest, LANES), f32)
+    picks, slot_counts = [], []
+    code_row = (iota((code_total, LANES), 0) - EXACT).astype(f32).astype(bf16)
+    cluster_row = iota((clusters, LANES), 0).astype(f32).astype(bf16)
+    for owner in range(owners):
+        codes = jnp.zeros((longest, LANES), f32)
+        cluster = jnp.zeros((longest, LANES), f32)
+        for cent in range(cents):
+            note = got_ref[owner * cents + cent, 2 * capacity :, :].astype(f32)
+            codes = jnp.where(segment == cent, note, codes)
+            cluster = jnp.where(segment == (cent + 1) % cents, note, cluster)
+            count = count + jnp.where(segment == (cent + 2) % cents, note, 0.0)
+        cluster = pltpu.roll(cluster, LANES - capacity, 1).astype(bf16)
+        codes = codes.astype(bf16)
+        picks.append((cluster_row == cluster[0:1]).astype(bf16))
+        held = jnp.zeros((code_total, LANES), bf16)
+        for row in range(longest):
+            held = held + (code_row == codes[row : row + 1]).astype(bf16)
+        slot_counts.append(held)
+    for step in range(cents.bit_length() - 1):
+        count = count + pltpu.roll(count, capacity << step, 1)
+    count_ref[...] = count
+    pick = jnp.concatenate(picks, axis=1)
+    slot_count = jnp.concatenate(slot_counts, axis=1)
+    rows = jnp.concatenate(
+        [
+            got_ref[:, side * capacity : (side + 1) * capacity, :].reshape(
+                sources * capacity, share // 2
+            )
+            for side in range(2)
+        ],
+        axis=1,
+    )
+    sums = dot(pick, rows)
+    number = dot(pick, jnp.ones((sources * capacity, LANES), bf16))
+    number = jnp.concatenate([number] * (share // LANES), axis=1)
+    copy.wait()
+    new = (sums + old_ref[...].astype(f32)) / (number + 1.0)
+    new_ref[...] = new
+    anchor = new.astype(bf16)
+    cluster_count = dot_rows(slot_count, pick)
+    high = jnp.floor(cluster_count * (1.0 / EXACT))
+    low = cluster_count - high * EXACT
+    moved = dot(low.astype(bf16), anchor) + EXACT * dot(high.astype(bf16), anchor)
+    total = keep_ref[0] + near_ref[0].astype(f32) + far_ref[...].astype(f32)
+    total = total + (dot(slot_count, rows) - moved)
+    code_ref[...] = total.astype(bf16)
+
+
+def finish_kernel(sizes, got_ref, count_ref, old_ref, out_ref):
+    owners, cents, capacity, longest, code_total = sizes
+    share = got_ref.shape[2]
+    prior = jnp.concatenate([count_ref[...] + code_prior] * (share // LANES), axis=1)
+    for cent in range(cents):
+        total = got_ref[cent].astype(f32)
+        for owner in range(1, owners):
+            total = total + got_ref[owner * cents + cent].astype(f32)
+        lanes = slice(cent * share, (cent + 1) * share)
+        out_ref[:, lanes] = (total + code_prior * old_ref[:, lanes]) / prior
+
+
+def coarse_kernel(cents, own_ref, near_ref, far_ref, out_ref):
+    me = lax.axis_index("cent")
+    rows = out_ref.shape[0]
+    share = own_ref.shape[1]
+    put = lambda step, value: out_ref.__setitem__(
+        (slice(None), pl.ds(pl.multiple_of((me ^ step) * share, share), share)), value
+    )
+    put(0, own_ref[pl.ds(pl.multiple_of(me * rows, rows), rows), :])
+    put(1, near_ref[0])
+    put(2, far_ref[0])
+    put(3, far_ref[1])
+
+
+def summed_body(frames, video_length, video_owner, video_cluster, frame_code, old_coarse, old_codes):
+    owners = lax.axis_size("dp")
+    cents = lax.axis_size("cent")
+    frame_count, features = frames.shape
+    videos = video_length.shape[1]
+    clusters = old_coarse.shape[0]
+    part = old_codes.shape[0]
+    code_total = part * owners * cents
+    capacity = max(2, 2 * videos // owners)
+    longest = 2 * frame_count // videos
+    share = features // cents
+    devices = owners * cents
+    sizes = (owners, cents, capacity, longest, code_total)
+    me = lax.axis_index("cent")
+    frame_code = frame_code.reshape(1, frame_count)
+    vmem = pl.BlockSpec(memory_space=pltpu.VMEM)
+    anywhere = pl.BlockSpec(memory_space=pl.ANY)
+    params = pltpu.CompilerParams(vmem_limit_bytes=32 * 1024 * 1024)
+    chunk = 2 * capacity + longest
+    swap = lambda array, bit: lax.ppermute(
+        array, "cent", [(index, index ^ bit) for index in range(cents)]
+    )
+    frames_scratch = [pltpu.VMEM((frame_count, features), bf16), pltpu.SemaphoreType.DMA]
+    send = pl.pallas_call(
+        functools.partial(pool_kernel, sizes),
+        out_shape=jax.ShapeDtypeStruct((owners, cents, chunk, share // 2), bf16),
+        in_specs=[vmem] * 4 + [anywhere],
+        out_specs=vmem,
+        scratch_shapes=frames_scratch,
+        compiler_params=params,
+        name="pool",
+    )(video_length, video_owner, video_cluster, frame_code, frames)
+    got = lax.all_to_all(
+        send.reshape(devices, chunk, share // 2), ("dp", "cent"), 0, 0, tiled=True
+    )
+    keep, give = pl.pallas_call(
+        functools.partial(code_kernel, sizes),
+        out_shape=(
+            jax.ShapeDtypeStruct((cents // 2, code_total, share), f32),
+            jax.ShapeDtypeStruct((cents // 2, code_total, share), bf16),
+        ),
+        in_specs=[vmem] * 3 + [anywhere, vmem],
+        out_specs=(vmem, vmem),
+        scratch_shapes=frames_scratch,
+        compiler_params=params,
+        cost_estimate=pl.CostEstimate(
+            flops=3 * code_total * frame_count * features,
+            bytes_accessed=6 * frame_count * features,
+            transcendentals=0,
+        ),
+        name="codes",
+    )(video_length, video_owner, frame_code, frames, send)
+    near = swap(give, 1)
+    far = swap((keep[1] + near[1].astype(f32)).astype(bf16), 2)
+    sums, new, count = pl.pallas_call(
+        functools.partial(owner_kernel, sizes),
+        out_shape=(
+            jax.ShapeDtypeStruct((code_total, share), bf16),
+            jax.ShapeDtypeStruct((clusters, share), f32),
+            jax.ShapeDtypeStruct((part, LANES), f32),
+        ),
+        in_specs=[vmem, anywhere, vmem, vmem, vmem],
+        out_specs=(vmem, vmem, vmem),
+        scratch_shapes=[pltpu.VMEM((clusters, share), bf16), pltpu.SemaphoreType.DMA],
+        compiler_params=params,
+        name="owner",
+    )(got, old_coarse, keep, near, far)
+    last = lax.all_to_all(sums.reshape(devices, part, share), ("dp", "cent"), 0, 0, tiled=True)
+    quarter = clusters // cents
+    rows_of = lambda step: lax.dynamic_slice_in_dim(new, (me ^ step) * quarter, quarter, 0)
+    beside = swap(jnp.stack([rows_of(1), rows_of(3)]), 1)
+    across = swap(jnp.stack([rows_of(2), beside[1]]), 2)
+    new_coarse = pl.pallas_call(
+        functools.partial(coarse_kernel, cents),
+        out_shape=jax.ShapeDtypeStruct((quarter, features), f32),
+        in_specs=[vmem] * 3,
+        out_specs=vmem,
+        compiler_params=params,
+        name="coarse",
+    )(new, beside, across)
+    new_codes = pl.pallas_call(
+        functools.partial(finish_kernel, sizes),
+        out_shape=jax.ShapeDtypeStruct((part, features), f32),
+        in_specs=[vmem] * 3,
+        out_specs=vmem,
+        compiler_params=params,
+        name="finish",
+    )(last, count, old_codes)
+    return new_coarse, new_codes
 
 
 def owner_slots(target, target_count, capacity):
@@ -22,7 +349,7 @@
     return (source, filled)
 
 
-def body(frames, video_length, video_owner, video_cluster, frame_code, old_coarse, old_codes):
+def routed_body(frames, video_length, video_owner, video_cluster, frame_code, old_coarse, old_codes):
     dp_count = lax.axis_size("dp")
     cent_count = lax.axis_size("cent")
     frame_count, features = frames.shape
@@ -119,6 +446,26 @@
     return (new_coarse, new_codes)
 
 
+def choose(mesh):
+    owners, cents = mesh.shape["dp"], mesh.shape["cent"]
+
+    def body(*arrays):
+        frame_count, features = arrays[0].shape
+        videos = arrays[1].shape[1]
+        part = arrays[6].shape[0]
+        small = (
+            part * owners * cents <= 2 * EXACT
+            and arrays[5].shape[0] <= EXACT
+            and cents == 4
+            and cents * max(2, 2 * videos // owners) == LANES
+            and part == 2 * frame_count // videos
+            and features % (2 * cents * LANES) == 0
+        )
+        return (summed_body if small else routed_body)(*arrays)
+
+    return body
+
+
 def solution(mesh):
     placed = (
         P(("dp", "cent"), None),
@@ -130,7 +477,7 @@
         P(("dp", "cent"), None),
     )
     return jax.shard_map(
-        body,
+        choose(mesh),
         mesh=mesh,
         in_specs=placed,
         out_specs=(P(("dp", "cent"), None), P(("dp", "cent"), None)),

time: 257 us -> 67.7 us (0.26)
  blocking collectives: 110 us -> 0 us
  waiting for transfers between devices: 51 us -> 17.8 us
  local copies, waits for them, and re-layouts: 35.8 us -> 5.88 us
  Pallas kernels: 0 us -> 26.2 us
  other arithmetic: 15 us -> 0.08 us
  between operations: 15.5 us -> 0.76 us
  matrix products: 8.5 us -> 0 us
  starting transfers between devices: 20.5 us -> 16.6 us
    all_to_all x1 -> x0, blocking collectives: 96.8 us -> none  [body(): lax.all_to_all(slot_rows.reshape(dp_count, cap_frame, features), 'dp', sp...]
    all_to_all x4 -> x2, waiting for transfers between devices: 33 us -> 1.02 us  [the longest x1 1.02 us: summed_body(): lax.all_to_all(sums.reshape(devices, part, share), ('dp', 'cent'), 0, 0,...]
    pallas_call x0 -> x5, Pallas kernels: none -> 26.2 us  [the longest x1 16.7 us: summed_body(): pl.pallas_call(functools.partial(owner_kernel, sizes), out_shape=(jax.Sha...]
    gather x5 -> x0, local copies, waits for them, and re-layouts: 22.1 us -> none  [the longest x1 9.67 us: body(): residual[source]]
    reduce_scatter x2 -> x0, waiting for transfers between devices: 18 us -> none  [the longest x1 18 us: body(): lax.psum_scatter(code_sum, 'cent', scatter_dimension=0, tiled=True)]
    ppermute x0 -> x4, waiting for transfers between devices: none -> 16.7 us  [summed_body(): lax.ppermute(array, 'cent', [(index, index ^ bit) for index in range(cent...]
    scatter x4 -> x0, local copies, waits for them, and re-layouts: 10.6 us -> none  [the longest x2 5.29 us: invert_slots(): filled = jnp.zeros((slot_total,), jnp.int32).at[slot_list].set(1)]
    dot_general x5 -> x0, matrix products: 8.5 us -> none  [the longest x1 2.42 us: body(): jnp.dot(member.T, video_anchor, preferred_element_type=jnp.float32)]
  transfers between devices with their start and end apart: 6 -> 6, of which waited for: 4 -> 5; matrix products, arithmetic and copies ran while one was open for 12% -> 0% of each run, Pallas kernels for 0% -> 8%
where the time goes in v1:
time: 67.7 us; the launch traced here: 67.3 us
  Pallas kernels  26.2 us (39%)
  waiting for transfers between devices  17.8 us (26%)
  starting transfers between devices  16.6 us (25%)
  local copies, waits for them, and re-layouts  5.88 us (9%)
  between operations  0.76 us (1%)
    ppermute x4, waiting for transfers between devices, summed_body(): lax.ppermute(array, 'cent', [(index, index ^ bit) for index in range(cent...  16.7 us
    pallas_call x1, Pallas kernels, summed_body(): pl.pallas_call(functools.partial(owner_kernel, sizes), out_shape=(jax.Sha...  16.7 us
    all_to_all x1, starting transfers between devices, summed_body(): lax.all_to_all(send.reshape(devices, chunk, share // 2), ('dp', 'cent'),...  7.3 us
    unnamed x22, local copies, waits for them, and re-layouts  5.85 us
    all_to_all x1, starting transfers between devices, summed_body(): lax.all_to_all(sums.reshape(devices, part, share), ('dp', 'cent'), 0, 0,...  5.04 us
    pallas_call x1, Pallas kernels, summed_body(): pl.pallas_call(functools.partial(code_kernel, sizes), out_shape=(jax.Shap...  4.43 us
    ppermute x4, starting transfers between devices, summed_body(): lax.ppermute(array, 'cent', [(index, index ^ bit) for index in range(cent...  4.29 us
    pallas_call x1, Pallas kernels, summed_body(): pl.pallas_call(functools.partial(pool_kernel, sizes), out_shape=jax.Shape...  3.72 us
  transfers between devices with their start and end apart: 6, of which 5 were waited for; matrix products, arithmetic and copies ran while one was open for 0% of the time, Pallas kernels for 8%

profile of v1, /device:TPU:0, one launch (start us, length us, event | category | flops | bytes accessed | tf_op | source)
XLA Modules:
  0.0 67.3 jit_solution(16232020811802984458)
XLA Ops:
  0.6 0.0 copy-start.8
  0.6 0.0 copy-start.10
  0.7 0.0 copy-start
  0.7 1.6 %copy-done = bf16[1024,1024]{1,0:T(8,128)(2,1)S(1)} copy-done((bf16[1024,1024]{1,0:T(8,128)(2,1)S(1)}, bf16[1024,1024]{1,0:T(8,128)(2,1)}, u32[]{:S(2)}) %copy-start) | copy-done | bytes 2097176
  2.3 0.0 copy-start.4
  2.3 0.7 %copy-done.4 = s32[1024]{0:T(1024)S(1)} copy-done((s32[1024]{0:T(1024)S(1)}, s32[1024]{0:T(1024)}, u32[]{:S(2)}) %copy-start.4) | copy-done | bytes 4120
  2.9 0.0 copy-start.6
  2.9 0.7 copy-done.6
  3.6 0.0 copy-start.7
  3.6 0.7 copy-done.7
  4.3 0.0 copy-start.9
  4.3 0.7 copy-done.9
  4.9 0.0 copy-start.5
  4.9 3.7 %pool.1.pooled_ref = bf16[8,4,80,128]{3,2,1,0:T(8,128)(2,1)} custom-call(s32[1,128]{1,0:T(1,128)S(1)} %copy-done.7, s32[1,128]{1,0:T(1,128)S(1)} %copy-done.9, s32[1,128]{1,0:T(1,128)S(1)} %copy-done.6, s32[1,1024]{1,0:T(1,128)S(1)} %bitcast.11, bf16[1024,1024]{1,0:T(8,128)(2,1)S(1)} %copy-done), custom_call_target="tpu_custom_call" | custom-call | tf_op jit(solution)/shard_map/pool/pallas_call | solution.py:268
  8.6 7.3 %all-to-all-start = ((bf16[32,80,128]{2,1,0:T(8,128)(2,1)}), bf16[32,80,128]{2,1,0:T(8,128)(2,1)S(1)}, u32[]{:S(2)}, u32[]{:S(2)}) async-start(bf16[32,80,128]{2,1,0:T(8,128)(2,1)} %bitcast.1), calls=%async_computation | async-start | bytes 1310720 | tf_op jit(solution)/shard_map/all_to_all | solution.py:277
  16.0 0.0 copy-done.8
  16.0 0.0 copy-done.10
  16.0 0.0 copy-done.5
  16.0 0.0 copy-start.1
  16.0 1.6 %copy-done.1 = bf16[1024,1024]{1,0:T(8,128)(2,1)S(1)} copy-done((bf16[1024,1024]{1,0:T(8,128)(2,1)S(1)}, bf16[1024,1024]{1,0:T(8,128)(2,1)}, u32[]{:S(2)}) %copy-start.1) | copy-done | bytes 2097176
  17.6 0.0 copy-start.2
  17.6 4.4 %codes.1 = (f32[2,512,256]{2,1,0:T(8,128)S(1)}, bf16[2,512,256]{2,1,0:T(8,128)(2,1)S(1)}) custom-call(s32[1,128]{1,0:T(1,128)S(1)} %copy-done.8, s32[1,128]{1,0:T(1,128)S(1)} %copy-done.10, s32[1,1024]{1,0:T(1,128)S(1)} %bitcast.12, bf16[1024,1024]{1,0:T(8,128)(2,1)S(1)} %copy-done.1, bf16[8,4,80,128]{3,2,1,0:T(8,128)(2,1)} %pool.1.pooled_ref), custom_call_target="tpu_custom_call" | custom-call | flops 1610612736 | bytes 6291456 | tf_op jit(solution)/shard_map/codes/pallas_call | solution.py:280
  22.0 0.3 collective-permute-start
  22.3 1.7 %collective-permute-done.near_ref = bf16[2,512,256]{2,1,0:T(8,128)(2,1)S(1)} collective-permute-done((bf16[2,512,256]{2,1,0:T(8,128)(2,1)S(1)}, bf16[2,512,256]{2,1,0:T(8,128)(2,1)S(1)}, u32[]{:S(2)}, u32[]{:S(2)}) %collective-permute-start) | collective-permute-done | bytes 524320 | tf_op jit(solution)/shard_map/ppermute | solution.py:264
  24.0 0.1 fusion
  24.0 1.8 %collective-permute-start.1 = (bf16[512,256]{1,0:T(8,128)(2,1)S(1)}, bf16[512,256]{1,0:T(8,128)(2,1)S(1)}, u32[]{:S(2)}, u32[]{:S(2)}) collective-permute-start(bf16[512,256]{1,0:T(8,128)(2,1)S(1)} %fusion), channel_id=1, source_target_pairs={{0,2},{1,3},{2,0},{3,1},{4,6},{5,7},{6,4},{7,5},{8,10},{9,11},{10,... | collective-permute-start | bytes 786440 | tf_op jit(solution)/shard_map/ppermute | solution.py:264
  25.9 0.0 copy-start.3
  25.9 8.4 %collective-permute-done.1.far_ref = bf16[512,256]{1,0:T(8,128)(2,1)S(1)} collective-permute-done((bf16[512,256]{1,0:T(8,128)(2,1)S(1)}, bf16[512,256]{1,0:T(8,128)(2,1)S(1)}, u32[]{:S(2)}, u32[]{:S(2)}) %collective-permute-start.1) | collective-permute-done | bytes 262176 | tf_op jit(solution)/shard_map/ppermute | solution.py:264
  34.3 0.0 all-to-all-done.got_ref
  34.3 0.0 copy-done.2
  34.3 16.7 %owner.1 = (bf16[512,256]{1,0:T(8,128)(2,1)}, f32[256,256]{1,0:T(8,128)S(1)}, f32[16,128]{1,0:T(8,128)S(1)}) custom-call(bf16[32,80,128]{2,1,0:T(8,128)(2,1)S(1)} %all-to-all-done.got_ref, bf16[256,1024]{1,0:T(8,128)(2,1)S(1)} %copy-done.2, f32[2,512,256]{2,1,0:T(8,128)S(1)} %get-tuple-element.7.keep_ref, ...), custom_call_target="tpu_custom_call" | custom-call | tf_op jit(solution)/shard_map/owner/pallas_call | solution.py:299
  51.0 5.0 %all-to-all-start.1 = ((bf16[32,16,256]{2,1,0:T(8,128)(2,1)}), bf16[32,16,256]{2,1,0:T(8,128)(2,1)S(1)}, u32[]{:S(2)}, u32[]{:S(2)}) async-start(bf16[32,16,256]{2,1,0:T(8,128)(2,1)} %bitcast.6), calls=%async_computation.1 | async-start | bytes 524288 | tf_op jit(solution)/shard_map/all_to_all | solution.py:312
  56.1 0.3 collective-permute-start.2
  56.4 1.1 %collective-permute-done.2.near_ref = f32[2,64,256]{2,1,0:T(8,128)S(1)} collective-permute-done((f32[2,64,256]{2,1,0:T(8,128)S(1)}, f32[2,64,256]{2,1,0:T(8,128)S(1)}, u32[]{:S(2)}, u32[]{:S(2)}) %collective-permute-start.2) | collective-permute-done | bytes 131104 | tf_op jit(solution)/shard_map/ppermute | solution.py:264
  57.5 1.8 %collective-permute-start.3 = (f32[2,64,256]{2,1,0:T(8,128)S(1)}, f32[2,64,256]{2,1,0:T(8,128)S(1)}, u32[]{:S(2)}, u32[]{:S(2)}) collective-permute-start(f32[2,64,256]{2,1,0:T(8,128)S(1)} %pad_maximum_fusion.1), channel_id=1, source_target_pairs={{0,2},{1,3},{2,0},{3,1},{4,6},{5,7},{6,4},{7,5},{8,10},{9,11},{10,... | collective-permute-start | bytes 393224 | tf_op jit(solution)/shard_map/ppermute | solution.py:264
  59.4 5.5 %collective-permute-done.3.far_ref = f32[2,64,256]{2,1,0:T(8,128)S(1)} collective-permute-done((f32[2,64,256]{2,1,0:T(8,128)S(1)}, f32[2,64,256]{2,1,0:T(8,128)S(1)}, u32[]{:S(2)}, u32[]{:S(2)}) %collective-permute-start.3) | collective-permute-done | bytes 131104 | tf_op jit(solution)/shard_map/ppermute | solution.py:264
  64.9 0.7 %coarse.1 = f32[64,1024]{1,0:T(8,128)} custom-call(f32[256,256]{1,0:T(8,128)S(1)} %get-tuple-element.9.own_ref, f32[2,64,256]{2,1,0:T(8,128)S(1)} %collective-permute-done.2.near_ref, f32[2,64,256]{2,1,0:T(8,128)S(1)} %collective-permute-done.3.far_ref), custom_call_target="tpu_custom_call" | custom-call | tf_op jit(solution)/shard_map/coarse/pallas_call | solution.py:317
  65.6 1.0 %all-to-all-done.1.got_ref = bf16[32,16,256]{2,1,0:T(8,128)(2,1)S(1)} async-done(((bf16[32,16,256]{2,1,0:T(8,128)(2,1)}), bf16[32,16,256]{2,1,0:T(8,128)(2,1)S(1)}, u32[]{:S(2)}, u32[]{:S(2)}) %all-to-all-start.1) | async-done | bytes 262176 | tf_op jit(solution)/shard_map/all_to_all | solution.py:312
  66.7 0.0 copy-done.3
  66.7 0.7 %finish.1 = f32[16,1024]{1,0:T(8,128)} custom-call(bf16[32,16,256]{2,1,0:T(8,128)(2,1)S(1)} %all-to-all-done.1.got_ref, f32[16,128]{1,0:T(8,128)S(1)} %get-tuple-element.11.count_ref, f32[16,1024]{1,0:T(8,128)S(1)} %copy-done.3), custom_call_target="tpu_custom_call" | custom-call | tf_op jit(solution)/shard_map/finish/pallas_call | solution.py:325
  (4 shorter events, 0.1 us)
Async XLA Ops:
  0.6 15.3 %copy-start.8 = (s32[1,128]{1,0:T(1,128)S(1)}, s32[1,128]{1,0:T(1,128)}, u32[]{:S(2)}) copy-start(s32[1,128]{1,0:T(1,128)} %length_ref.3) | copy-start | bytes 1540
  0.6 15.3 %copy-start.10 = (s32[1,128]{1,0:T(1,128)S(1)}, s32[1,128]{1,0:T(1,128)}, u32[]{:S(2)}) copy-start(s32[1,128]{1,0:T(1,128)} %owner_ref.3) | copy-start | bytes 1540
  0.7 1.6 %copy-start = (bf16[1024,1024]{1,0:T(8,128)(2,1)S(1)}, bf16[1024,1024]{1,0:T(8,128)(2,1)}, u32[]{:S(2)}) copy-start(bf16[1024,1024]{1,0:T(8,128)(2,1)} %frames_hbm.3) | copy-start | bytes 6291460
  2.3 0.7 %copy-start.4 = (s32[1024]{0:T(1024)S(1)}, s32[1024]{0:T(1024)}, u32[]{:S(2)}) copy-start(s32[1024]{0:T(1024)} %param.11) | copy-start | bytes 12292
  2.9 0.7 copy-start.6
  3.6 0.7 copy-start.7
  4.3 0.7 copy-start.9
  4.9 11.1 %copy-start.5 = (s32[1024]{0:T(1024)S(1)}, s32[1024]{0:T(1024)}, u32[]{:S(2)}) copy-start(s32[1024]{0:T(1024)} %param.11) | copy-start | bytes 12292
  8.6 25.7 %all-to-all-start = ((bf16[32,80,128]{2,1,0:T(8,128)(2,1)}), bf16[32,80,128]{2,1,0:T(8,128)(2,1)S(1)}, u32[]{:S(2)}, u32[]{:S(2)}) async-start(bf16[32,80,128]{2,1,0:T(8,128)(2,1)} %bitcast.1), calls=%async_computation | async-start | bytes 1310720 | tf_op jit(solution)/shard_map/all_to_all | solution.py:277
  16.0 1.6 %copy-start.1 = (bf16[1024,1024]{1,0:T(8,128)(2,1)S(1)}, bf16[1024,1024]{1,0:T(8,128)(2,1)}, u32[]{:S(2)}) copy-start(bf16[1024,1024]{1,0:T(8,128)(2,1)} %frames_hbm.3) | copy-start | bytes 6291460
  17.6 16.8 %copy-start.2 = (bf16[256,1024]{1,0:T(8,128)(2,1)S(1)}, bf16[256,1024]{1,0:T(8,128)(2,1)}, u32[]{:S(2)}) copy-start(bf16[256,1024]{1,0:T(8,128)(2,1)} %old_hbm.1) | copy-start | bytes 1572868
  22.0 2.0 %collective-permute-start = (bf16[2,512,256]{2,1,0:T(8,128)(2,1)S(1)}, bf16[2,512,256]{2,1,0:T(8,128)(2,1)S(1)}, u32[]{:S(2)}, u32[]{:S(2)}) collective-permute-start(bf16[2,512,256]{2,1,0:T(8,128)(2,1)S(1)} %get-tuple-element.8), channel_id=1, source_target_pairs={{0,1},{1,0},{2,3},{3,2},{4,5},{5,4},{6,7},{7,6},{8,9},{9,8},{10,11... | collective-permute-start | bytes 1572872 | tf_op jit(solution)/shard_map/ppermute | solution.py:264
  24.0 10.3 %collective-permute-start.1 = (bf16[512,256]{1,0:T(8,128)(2,1)S(1)}, bf16[512,256]{1,0:T(8,128)(2,1)S(1)}, u32[]{:S(2)}, u32[]{:S(2)}) collective-permute-start(bf16[512,256]{1,0:T(8,128)(2,1)S(1)} %fusion), channel_id=1, source_target_pairs={{0,2},{1,3},{2,0},{3,1},{4,6},{5,7},{6,4},{7,5},{8,10},{9,11},{10,... | collective-permute-start | bytes 786440 | tf_op jit(solution)/shard_map/ppermute | solution.py:264
  25.9 40.8 %copy-start.3 = (f32[16,1024]{1,0:T(8,128)S(1)}, f32[16,1024]{1,0:T(8,128)}, u32[]{:S(2)}) copy-start(f32[16,1024]{1,0:T(8,128)} %old_ref.1) | copy-start | bytes 196612
  51.0 15.6 %all-to-all-start.1 = ((bf16[32,16,256]{2,1,0:T(8,128)(2,1)}), bf16[32,16,256]{2,1,0:T(8,128)(2,1)S(1)}, u32[]{:S(2)}, u32[]{:S(2)}) async-start(bf16[32,16,256]{2,1,0:T(8,128)(2,1)} %bitcast.6), calls=%async_computation.1 | async-start | bytes 524288 | tf_op jit(solution)/shard_map/all_to_all | solution.py:312
  56.1 1.4 %collective-permute-start.2 = (f32[2,64,256]{2,1,0:T(8,128)S(1)}, f32[2,64,256]{2,1,0:T(8,128)S(1)}, u32[]{:S(2)}, u32[]{:S(2)}) collective-permute-start(f32[2,64,256]{2,1,0:T(8,128)S(1)} %pad_maximum_fusion), channel_id=1, source_target_pairs={{0,1},{1,0},{2,3},{3,2},{4,5},{5,4},{6,7},{7,6},{8,9},{9,8},{10,11... | collective-permute-start | bytes 393224 | tf_op jit(solution)/shard_map/ppermute | solution.py:264
  57.5 7.4 %collective-permute-start.3 = (f32[2,64,256]{2,1,0:T(8,128)S(1)}, f32[2,64,256]{2,1,0:T(8,128)S(1)}, u32[]{:S(2)}, u32[]{:S(2)}) collective-permute-start(f32[2,64,256]{2,1,0:T(8,128)S(1)} %pad_maximum_fusion.1), channel_id=1, source_target_pairs={{0,2},{1,3},{2,0},{3,1},{4,6},{5,7},{6,4},{7,5},{8,10},{9,11},{10,... | collective-permute-start | bytes 393224 | tf_op jit(solution)/shard_map/ppermute | solution.py:264

commit v2 on v1

--- a/solution.py
+++ b/solution.py
@@ -16,6 +16,20 @@
 
 def iota(shape, axis):
     return lax.broadcasted_iota(jnp.int32, shape, axis)
+
+
+def ones_where(mask):
+    return jnp.where(mask, jnp.ones((), bf16), jnp.zeros((), bf16))
+
+
+def fetch(sources, targets, sems):
+    copies = [
+        pltpu.make_async_copy(source, target, sems.at[at])
+        for at, (source, target) in enumerate(zip(sources, targets))
+    ]
+    for copy in copies:
+        copy.start()
+    return copies
 
 
 def dot(left, right):
@@ -62,12 +76,16 @@
     return (iota((code_total, frame_count), 0) == code_ref[...]).astype(f32).astype(bf16)
 
 
-def pool_kernel(sizes, length_ref, owner_ref, cluster_ref, code_ref, frames_hbm, send_ref, frames_ref, sem):
+def pool_kernel(sizes, length_hbm, owner_hbm, cluster_hbm, code_hbm, frames_hbm, send_ref, *scratch):
     owners, cents, capacity, longest, code_total = sizes
-    copy = pltpu.make_async_copy(frames_hbm, frames_ref, sem)
-    copy.start()
+    length_ref, owner_ref, cluster_ref, code_ref, frames_ref, sems = scratch
+    copies = fetch(
+        (length_hbm, owner_hbm, cluster_hbm, code_hbm, frames_hbm), scratch[:-1], sems
+    )
     me = lax.axis_index("cent")
     frame_count, features = frames_hbm.shape
+    for copy in copies[:-1]:
+        copy.wait()
     slots = owners * capacity
     share = features // cents
     video_of_slot, first, length, member = member_of_slots(
@@ -117,7 +135,7 @@
             )
             send_ref[owner, cent, 2 * capacity :, :] = note.astype(bf16)
     weight = 1.0 / jnp.maximum(length, 1.0)
-    copy.wait()
+    copies[-1].wait()
     half = share // 2
     for cent in range(cents):
         sums = dot(member, frames_ref[:, cent * share : (cent + 1) * share])
@@ -128,11 +146,13 @@
             )
 
 
-def code_kernel(sizes, length_ref, owner_ref, code_ref, frames_hbm, pooled_ref, keep_ref, give_ref, frames_ref, sem):
+def code_kernel(sizes, length_hbm, owner_hbm, code_hbm, frames_hbm, pooled_ref, keep_ref, give_ref, *scratch):
     owners, cents, capacity, longest, code_total = sizes
-    copy = pltpu.make_async_copy(frames_hbm, frames_ref, sem)
-    copy.start()
+    length_ref, owner_ref, code_ref, frames_ref, sems = scratch
+    copies = fetch((length_hbm, owner_hbm, code_hbm, frames_hbm), scratch[:-1], sems)
     me = lax.axis_index("cent")
+    for copy in copies[:-1]:
+        copy.wait()
     frame_count, features = frames_hbm.shape
     share = features // cents
     slots = owners * capacity
@@ -140,7 +160,7 @@
     _, _, _, member = member_of_slots(length_ref, owner_ref, owners, capacity, frame_count)
     matches = code_matches(code_ref, code_total)
     slot_counts = dot_rows(matches, member).astype(bf16)
-    copy.wait()
+    copies[-1].wait()
     for step in range(cents):
         cent = me ^ step
         columns = pl.ds(pl.multiple_of(cent * share, share), share)
@@ -157,63 +177,84 @@
                 keep_ref[step // 2, :, lanes] = centred
 
 
-def owner_kernel(sizes, got_ref, old_hbm, keep_ref, near_ref, far_ref, code_ref, new_ref, count_ref, old_ref, sem):
+def slot_rows(got_ref, capacity):
+    sources, _, half = got_ref.shape
+    return jnp.concatenate(
+        [
+            got_ref[:, side * capacity : (side + 1) * capacity, :].reshape(sources * capacity, half)
+            for side in range(2)
+        ],
+        axis=1,
+    )
+
+
+def cluster_picks(sizes, got_ref, clusters):
     owners, cents, capacity, longest, code_total = sizes
-    me = lax.axis_index("cent")
-    share = old_ref.shape[1]
-    copy = pltpu.make_async_copy(
-        old_hbm.at[:, pl.ds(pl.multiple_of(me * share, share), share)], old_ref, sem
-    )
-    copy.start()
-    clusters = old_ref.shape[0]
-    sources = owners * cents
     segment = iota((longest, LANES), 1) // capacity
-    count = jnp.zeros((longest, LANES), f32)
-    picks, slot_counts = [], []
-    code_row = (iota((code_total, LANES), 0) - EXACT).astype(f32).astype(bf16)
     cluster_row = iota((clusters, LANES), 0).astype(f32).astype(bf16)
+    picks = []
     for owner in range(owners):
-        codes = jnp.zeros((longest, LANES), f32)
         cluster = jnp.zeros((longest, LANES), f32)
         for cent in range(cents):
             note = got_ref[owner * cents + cent, 2 * capacity :, :].astype(f32)
+            cluster = jnp.where(segment == (cent + 1) % cents, note, cluster)
+        cluster = pltpu.roll(cluster, LANES - capacity, 1).astype(bf16)
+        picks.append(ones_where(cluster_row == cluster[0:1]))
+    return jnp.concatenate(picks, axis=1)
+
+
+def coarse_kernel(sizes, got_ref, old_hbm, across_ref, here_ref, beside_ref, anchor_ref, old_ref, new_ref, sems):
+    owners, cents, capacity, longest, code_total = sizes
+    me = lax.axis_index("cent")
+    clusters, share = old_ref.shape
+    columns = pl.ds(pl.multiple_of(me * share, share), share)
+    copies = fetch((old_hbm.at[:, columns],), (old_ref,), sems)
+    pick = cluster_picks(sizes, got_ref, clusters)
+    rows = slot_rows(got_ref, capacity)
+    sums = dot(pick, rows)
+    number = dot(pick, jnp.ones((rows.shape[0], LANES), bf16))
+    number = jnp.concatenate([number] * (share // LANES), axis=1)
+    copies[0].wait()
+    new = (sums + old_ref[...].astype(f32)) / (number + 1.0)
+    anchor_ref[...] = new.astype(bf16)
+    new_ref[...] = new
+    quarter = clusters // cents
+    rows_of = lambda step: new_ref[pl.ds(pl.multiple_of((me ^ step) * quarter, quarter), quarter), :]
+    across_ref[0] = rows_of(2)
+    across_ref[1] = rows_of(3)
+    here_ref[...] = rows_of(0)
+    beside_ref[...] = rows_of(1)
+
+
+def owner_kernel(sizes, got_ref, anchor_ref, keep_ref, near_ref, far_ref, code_ref, count_ref):
+    owners, cents, capacity, longest, code_total = sizes
+    segment = iota((longest, LANES), 1) // capacity
+    count = jnp.zeros((longest, LANES), f32)
+    slot_counts = []
+    code_row = (iota((code_total, LANES), 0) - EXACT).astype(f32).astype(bf16)
+    for owner in range(owners):
+        codes = jnp.zeros((longest, LANES), f32)
+        for cent in range(cents):
+            note = got_ref[owner * cents + cent, 2 * capacity :, :].astype(f32)
             codes = jnp.where(segment == cent, note, codes)
-            cluster = jnp.where(segment == (cent + 1) % cents, note, cluster)
             count = count + jnp.where(segment == (cent + 2) % cents, note, 0.0)
-        cluster = pltpu.roll(cluster, LANES - capacity, 1).astype(bf16)
         codes = codes.astype(bf16)
-        picks.append((cluster_row == cluster[0:1]).astype(bf16))
         held = jnp.zeros((code_total, LANES), bf16)
         for row in range(longest):
-            held = held + (code_row == codes[row : row + 1]).astype(bf16)
+            held = held + ones_where(code_row == codes[row : row + 1])
         slot_counts.append(held)
     for step in range(cents.bit_length() - 1):
         count = count + pltpu.roll(count, capacity << step, 1)
     count_ref[...] = count
-    pick = jnp.concatenate(picks, axis=1)
     slot_count = jnp.concatenate(slot_counts, axis=1)
-    rows = jnp.concatenate(
-        [
-            got_ref[:, side * capacity : (side + 1) * capacity, :].reshape(
-                sources * capacity, share // 2
-            )
-            for side in range(2)
-        ],
-        axis=1,
-    )
-    sums = dot(pick, rows)
-    number = dot(pick, jnp.ones((sources * capacity, LANES), bf16))
-    number = jnp.concatenate([number] * (share // LANES), axis=1)
-    copy.wait()
-    new = (sums + old_ref[...].astype(f32)) / (number + 1.0)
-    new_ref[...] = new
-    anchor = new.astype(bf16)
+    pick = cluster_picks(sizes, got_ref, anchor_ref.shape[0])
+    anchor = anchor_ref[...]
     cluster_count = dot_rows(slot_count, pick)
     high = jnp.floor(cluster_count * (1.0 / EXACT))
     low = cluster_count - high * EXACT
     moved = dot(low.astype(bf16), anchor) + EXACT * dot(high.astype(bf16), anchor)
     total = keep_ref[0] + near_ref[0].astype(f32) + far_ref[...].astype(f32)
-    total = total + (dot(slot_count, rows) - moved)
+    total = total + (dot(slot_count, slot_rows(got_ref, capacity)) - moved)
     code_ref[...] = total.astype(bf16)
 
 
@@ -229,17 +270,11 @@
         out_ref[:, lanes] = (total + code_prior * old_ref[:, lanes]) / prior
 
 
-def coarse_kernel(cents, own_ref, near_ref, far_ref, out_ref):
+def join_kernel(here_ref, across_ref, near_ref, far_ref, out_ref):
     me = lax.axis_index("cent")
-    rows = out_ref.shape[0]
-    share = own_ref.shape[1]
-    put = lambda step, value: out_ref.__setitem__(
-        (slice(None), pl.ds(pl.multiple_of((me ^ step) * share, share), share)), value
-    )
-    put(0, own_ref[pl.ds(pl.multiple_of(me * rows, rows), rows), :])
-    put(1, near_ref[0])
-    put(2, far_ref[0])
-    put(3, far_ref[1])
+    share = here_ref.shape[1]
+    for step, value in enumerate((here_ref[...], near_ref[...], across_ref[0], far_ref[...])):
+        out_ref[:, pl.ds(pl.multiple_of((me ^ step) * share, share), share)] = value
 
 
 def summed_body(frames, video_length, video_owner, video_cluster, frame_code, old_coarse, old_codes):
@@ -255,25 +290,27 @@
     share = features // cents
     devices = owners * cents
     sizes = (owners, cents, capacity, longest, code_total)
-    me = lax.axis_index("cent")
     frame_code = frame_code.reshape(1, frame_count)
     vmem = pl.BlockSpec(memory_space=pltpu.VMEM)
-    anywhere = pl.BlockSpec(memory_space=pl.ANY)
+    hbm = pl.BlockSpec(memory_space=pltpu.HBM)
     params = pltpu.CompilerParams(vmem_limit_bytes=32 * 1024 * 1024)
     chunk = 2 * capacity + longest
+    stay = lambda array: pltpu.with_memory_space_constraint(array, pltpu.HBM)
     swap = lambda array, bit: lax.ppermute(
         array, "cent", [(index, index ^ bit) for index in range(cents)]
     )
-    frames_scratch = [pltpu.VMEM((frame_count, features), bf16), pltpu.SemaphoreType.DMA]
+    row = lambda length: pltpu.VMEM((1, length), jnp.int32)
+    frames_scratch = [row(frame_count), pltpu.VMEM((frame_count, features), bf16)]
+    quarter = clusters // cents
     send = pl.pallas_call(
         functools.partial(pool_kernel, sizes),
         out_shape=jax.ShapeDtypeStruct((owners, cents, chunk, share // 2), bf16),
-        in_specs=[vmem] * 4 + [anywhere],
+        in_specs=[hbm] * 5,
         out_specs=vmem,
-        scratch_shapes=frames_scratch,
+        scratch_shapes=[row(videos)] * 3 + frames_scratch + [pltpu.SemaphoreType.DMA((5,))],
         compiler_params=params,
         name="pool",
-    )(video_length, video_owner, video_cluster, frame_code, frames)
+    )(*map(stay, (video_length, video_owner, video_cluster, frame_code, frames)))
     got = lax.all_to_all(
         send.reshape(devices, chunk, share // 2), ("dp", "cent"), 0, 0, tiled=True
     )
@@ -283,9 +320,9 @@
             jax.ShapeDtypeStruct((cents // 2, code_total, share), f32),
             jax.ShapeDtypeStruct((cents // 2, code_total, share), bf16),
         ),
-        in_specs=[vmem] * 3 + [anywhere, vmem],
+        in_specs=[hbm] * 4 + [vmem],
         out_specs=(vmem, vmem),
-        scratch_shapes=frames_scratch,
+        scratch_shapes=[row(videos)] * 2 + frames_scratch + [pltpu.SemaphoreType.DMA((4,))],
         compiler_params=params,
         cost_estimate=pl.CostEstimate(
             flops=3 * code_total * frame_count * features,
@@ -293,35 +330,54 @@
             transcendentals=0,
         ),
         name="codes",
-    )(video_length, video_owner, frame_code, frames, send)
+    )(*map(stay, (video_length, video_owner, frame_code, frames)), send)
     near = swap(give, 1)
     far = swap((keep[1] + near[1].astype(f32)).astype(bf16), 2)
-    sums, new, count = pl.pallas_call(
+    piece = jax.ShapeDtypeStruct((quarter, share), f32)
+    across, here, beside, anchor = pl.pallas_call(
+        functools.partial(coarse_kernel, sizes),
+        out_shape=(
+            jax.ShapeDtypeStruct((2, quarter, share), f32),
+            piece,
+            piece,
+            jax.ShapeDtypeStruct((clusters, share), bf16),
+        ),
+        in_specs=[vmem, hbm],
+        out_specs=(vmem,) * 4,
+        scratch_shapes=[
+            pltpu.VMEM((clusters, share), bf16),
+            pltpu.VMEM((clusters, share), f32),
+            pltpu.SemaphoreType.DMA((1,)),
+        ],
+        compiler_params=params,
+        name="coarse",
+    )(got, stay(old_coarse))
+    across = swap(across, 2)
+    sums, count = pl.pallas_call(
         functools.partial(owner_kernel, sizes),
         out_shape=(
             jax.ShapeDtypeStruct((code_total, share), bf16),
-            jax.ShapeDtypeStruct((clusters, share), f32),
             jax.ShapeDtypeStruct((part, LANES), f32),
         ),
-        in_specs=[vmem, anywhere, vmem, vmem, vmem],
-        out_specs=(vmem, vmem, vmem),
-        scratch_shapes=[pltpu.VMEM((clusters, share), bf16), pltpu.SemaphoreType.DMA],
+        in_specs=[vmem] * 5,
+        out_specs=(vmem, vmem),
         compiler_params=params,
+        cost_estimate=pl.CostEstimate(
+            flops=4 * code_total * devices * capacity * share,
+            bytes_accessed=6 * code_total * share,
+            transcendentals=0,
+        ),
         name="owner",
-    )(got, old_coarse, keep, near, far)
+    )(got, anchor, keep, near, far)
     last = lax.all_to_all(sums.reshape(devices, part, share), ("dp", "cent"), 0, 0, tiled=True)
-    quarter = clusters // cents
-    rows_of = lambda step: lax.dynamic_slice_in_dim(new, (me ^ step) * quarter, quarter, 0)
-    beside = swap(jnp.stack([rows_of(1), rows_of(3)]), 1)
-    across = swap(jnp.stack([rows_of(2), beside[1]]), 2)
     new_coarse = pl.pallas_call(
-        functools.partial(coarse_kernel, cents),
+        join_kernel,
         out_shape=jax.ShapeDtypeStruct((quarter, features), f32),
-        in_specs=[vmem] * 3,
+        in_specs=[vmem] * 4,
         out_specs=vmem,
         compiler_params=params,
-        name="coarse",
-    )(new, beside, across)
+        name="join",
+    )(here, across, swap(beside, 1), swap(across[1], 1))
     new_codes = pl.pallas_call(
         functools.partial(finish_kernel, sizes),
         out_shape=jax.ShapeDtypeStruct((part, features), f32),

time: 67.7 us -> 50.1 us (0.74)
  Pallas kernels: 26.2 us -> 15.5 us
  local copies, waits for them, and re-layouts: 5.88 us -> 0.01 us
  starting transfers between devices: 16.6 us -> 14.8 us
  waiting for transfers between devices: 17.8 us -> 18.7 us
    pallas_call x1, Pallas kernels: 16.7 us -> 3.33 us  [summed_body(): pl.pallas_call(functools.partial(owner_kernel, sizes), out_shape=(jax.Sha...]
    all_to_all x1, waiting for transfers between devices: 0.01 us -> 9.04 us  [summed_body(): lax.all_to_all(send.reshape(devices, chunk, share // 2), ('dp', 'cent'),...]
    ppermute x4 -> x5, waiting for transfers between devices: 16.7 us -> 9.08 us  [summed_body(): lax.ppermute(array, 'cent', [(index, index ^ bit) for index in range(cent...]
    unnamed x22 -> x2, local copies, waits for them, and re-layouts: 5.85 us -> 0.01 us
    all_to_all x1, starting transfers between devices: 5.04 us -> 3.51 us  [summed_body(): lax.all_to_all(sums.reshape(devices, part, share), ('dp', 'cent'), 0, 0,...]
    pallas_call x1 -> x2, Pallas kernels: 0.72 us -> 2.13 us  [the longest x1 1.4 us: summed_body(): pl.pallas_call(functools.partial(coarse_kernel, sizes), out_shape=(jax.Sh...]
    ppermute x4 -> x5, starting transfers between devices: 4.29 us -> 4 us  [summed_body(): lax.ppermute(array, 'cent', [(index, index ^ bit) for index in range(cent...]
  transfers between devices with their start and end apart: 6 -> 7, of which waited for: 5 -> 5; matrix products, arithmetic and copies ran while one was open for 0% -> 0% of each run, Pallas kernels for 8% -> 14%
where the time goes in v2:
time: 50.1 us; the launch traced here: 49.8 us
  waiting for transfers between devices  18.7 us (37%)
  Pallas kernels  15.5 us (31%)
  starting transfers between devices  14.8 us (30%)
  between operations  0.71 us (1%)
    ppermute x5, waiting for transfers between devices, summed_body(): lax.ppermute(array, 'cent', [(index, index ^ bit) for index in range(cent...  9.08 us
    all_to_all x1, waiting for transfers between devices, summed_body(): lax.all_to_all(send.reshape(devices, chunk, share // 2), ('dp', 'cent'),...  9.04 us
    all_to_all x1, starting transfers between devices, summed_body(): lax.all_to_all(send.reshape(devices, chunk, share // 2), ('dp', 'cent'),...  7.3 us
    pallas_call x1, Pallas kernels, summed_body(): pl.pallas_call(functools.partial(code_kernel, sizes), out_shape=(jax.Shap...  5 us
    pallas_call x1, Pallas kernels, summed_body(): pl.pallas_call(functools.partial(pool_kernel, sizes), out_shape=jax.Shape...  4.33 us
    ppermute x5, starting transfers between devices, summed_body(): lax.ppermute(array, 'cent', [(index, index ^ bit) for index in range(cent...  4 us
    all_to_all x1, starting transfers between devices, summed_body(): lax.all_to_all(sums.reshape(devices, part, share), ('dp', 'cent'), 0, 0,...  3.51 us
    pallas_call x1, Pallas kernels, summed_body(): pl.pallas_call(functools.partial(owner_kernel, sizes), out_shape=(jax.Sha...  3.33 us
  transfers between devices with their start and end apart: 7, of which 5 were waited for; matrix products, arithmetic and copies ran while one was open for 0% of the time, Pallas kernels for 14%

profile of v2, /device:TPU:0, one launch (start us, length us, event | category | flops | bytes accessed | tf_op | source)
XLA Modules:
  0.0 49.8 jit_solution(9909465317797555069)
XLA Ops:
  0.6 4.3 %pool.1.pooled_ref = bf16[8,4,80,128]{3,2,1,0:T(8,128)(2,1)} custom-call(s32[1,128]{1,0:T(1,128)} %length_hbm.3, s32[1,128]{1,0:T(1,128)} %owner_hbm.3, s32[1,128]{1,0:T(1,128)} %cluster_hbm.1, s32[1,1024]{1,0:T(1,128)} %bitcast.7, bf16[1024,1024]{1,0:T(8,128)(2,1)} %frames_hbm.3), custom_call_target="tpu_custom_call" | custom-call | tf_op jit(solution)/shard_map/pool/pallas_call | solution.py:305
  5.0 7.3 %all-to-all-start = ((bf16[32,80,128]{2,1,0:T(8,128)(2,1)}), bf16[32,80,128]{2,1,0:T(8,128)(2,1)S(1)}, u32[]{:S(2)}, u32[]{:S(2)}) async-start(bf16[32,80,128]{2,1,0:T(8,128)(2,1)} %bitcast.1), calls=%async_computation | async-start | bytes 1310720 | tf_op jit(solution)/shard_map/all_to_all | solution.py:314
  12.3 5.0 %codes.1 = (f32[2,512,256]{2,1,0:T(8,128)S(1)}, bf16[2,512,256]{2,1,0:T(8,128)(2,1)S(1)}) custom-call(s32[1,128]{1,0:T(1,128)} %length_hbm.3, s32[1,128]{1,0:T(1,128)} %owner_hbm.3, s32[1,1024]{1,0:T(1,128)} %bitcast.8, bf16[1024,1024]{1,0:T(8,128)(2,1)} %frames_hbm.3, bf16[8,4,80,128]{3,2,1,0:T(8,128)(2,1)} %pool.1.pooled_ref), custom_call_target="tpu_custom_call" | custom-call | flops 1610612736 | bytes 6291456 | tf_op jit(solution)/shard_map/codes/pallas_call | solution.py:317
  17.3 0.3 collective-permute-start.3
  17.6 1.7 %collective-permute-done.3.near_ref = bf16[2,512,256]{2,1,0:T(8,128)(2,1)S(1)} collective-permute-done((bf16[2,512,256]{2,1,0:T(8,128)(2,1)S(1)}, bf16[2,512,256]{2,1,0:T(8,128)(2,1)S(1)}, u32[]{:S(2)}, u32[]{:S(2)}) %collective-permute-start.3) | collective-permute-done | bytes 524320 | tf_op jit(solution)/shard_map/ppermute | solution.py:299
  19.3 0.1 fusion
  19.3 1.8 %collective-permute-start.4 = (bf16[512,256]{1,0:T(8,128)(2,1)S(1)}, bf16[512,256]{1,0:T(8,128)(2,1)S(1)}, u32[]{:S(2)}, u32[]{:S(2)}) collective-permute-start(bf16[512,256]{1,0:T(8,128)(2,1)S(1)} %fusion), channel_id=1, source_target_pairs={{0,2},{1,3},{2,0},{3,1},{4,6},{5,7},{6,4},{7,5},{8,10},{9,11},{10,... | collective-permute-start | bytes 786440 | tf_op jit(solution)/shard_map/ppermute | solution.py:299
  21.2 9.0 %all-to-all-done.got_ref = bf16[32,80,128]{2,1,0:T(8,128)(2,1)S(1)} async-done(((bf16[32,80,128]{2,1,0:T(8,128)(2,1)}), bf16[32,80,128]{2,1,0:T(8,128)(2,1)S(1)}, u32[]{:S(2)}, u32[]{:S(2)}) %all-to-all-start) | async-done | bytes 655392 | tf_op jit(solution)/shard_map/all_to_all | solution.py:314
  30.2 1.4 %coarse.1 = (f32[2,64,256]{2,1,0:T(8,128)S(1)}, f32[64,256]{1,0:T(8,128)S(1)}, f32[64,256]{1,0:T(8,128)S(1)}, bf16[256,256]{1,0:T(8,128)(2,1)S(1)}) custom-call(bf16[32,80,128]{2,1,0:T(8,128)(2,1)S(1)} %all-to-all-done.got_ref, bf16[256,1024]{1,0:T(8,128)(2,1)} %old_hbm.1), custom_call_target="tpu_custom_call" | custom-call | tf_op jit(solution)/shard_map/coarse/pallas_call | solution.py:337
  31.6 0.0 copy-start
  31.6 0.0 collective-permute-done.4.far_ref
  31.6 3.3 %owner.1 = (bf16[512,256]{1,0:T(8,128)(2,1)}, f32[16,128]{1,0:T(8,128)S(1)}) custom-call(bf16[32,80,128]{2,1,0:T(8,128)(2,1)S(1)} %all-to-all-done.got_ref, bf16[256,256]{1,0:T(8,128)(2,1)S(1)} %get-tuple-element.13.anchor_ref, f32[2,512,256]{2,1,0:T(8,128)S(1)} %get-tuple-element.14.keep_ref, bf16[2,512,256]{2,1,0:T(8,128)(2,1)S(1)} %collective-permute-done.3.near_ref, ...), custom_call_target="tpu_custom_call" | custom-call | flops 536870912 | bytes 786432 | tf_op jit(solution)/shard_map/owner/pallas_call | solution.py:356
  35.0 3.5 %all-to-all-start.1 = ((bf16[32,16,256]{2,1,0:T(8,128)(2,1)}), bf16[32,16,256]{2,1,0:T(8,128)(2,1)S(1)}, u32[]{:S(2)}, u32[]{:S(2)}) async-start(bf16[32,16,256]{2,1,0:T(8,128)(2,1)} %bitcast.4), calls=%async_computation.1 | async-start | bytes 524288 | tf_op jit(solution)/shard_map/all_to_all | solution.py:372
  38.5 1.8 %collective-permute-start = (f32[2,64,256]{2,1,0:T(8,128)S(1)}, f32[2,64,256]{2,1,0:T(8,128)S(1)}, u32[]{:S(2)}, u32[]{:S(2)}) collective-permute-start(f32[2,64,256]{2,1,0:T(8,128)S(1)} %get-tuple-element.11), channel_id=1, source_target_pairs={{0,2},{1,3},{2,0},{3,1},{4,6},{5,7},{6,4},{7,5},{8,10},{9,11},{10,... | collective-permute-start | bytes 393224 | tf_op jit(solution)/shard_map/ppermute | solution.py:299
  40.3 0.0 collective-permute-start.1
  40.3 6.2 %collective-permute-done.across_ref = f32[2,64,256]{2,1,0:T(8,128)S(1)} collective-permute-done((f32[2,64,256]{2,1,0:T(8,128)S(1)}, f32[2,64,256]{2,1,0:T(8,128)S(1)}, u32[]{:S(2)}, u32[]{:S(2)}) %collective-permute-start) | collective-permute-done | bytes 131104 | tf_op jit(solution)/shard_map/ppermute | solution.py:299
  46.5 0.0 collective-permute-start.2
  46.5 0.0 collective-permute-done.1.near_ref
  46.5 1.2 %collective-permute-done.2.far_ref = f32[64,256]{1,0:T(8,128)S(1)} collective-permute-done((f32[64,256]{1,0:T(8,128)S(1)}, f32[64,256]{1,0:T(8,128)S(1)}, u32[]{:S(2)}, u32[]{:S(2)}) %collective-permute-start.2) | collective-permute-done | bytes 65568 | tf_op jit(solution)/shard_map/ppermute | solution.py:299
  47.8 0.7 %join.1 = f32[64,1024]{1,0:T(8,128)} custom-call(f32[64,256]{1,0:T(8,128)S(1)} %get-tuple-element.10.here_ref, f32[2,64,256]{2,1,0:T(8,128)S(1)} %collective-permute-done.across_ref, f32[64,256]{1,0:T(8,128)S(1)} %collective-permute-done.1.near_ref, f32[64,256]{1,0:T(8,128)S(1)} %collective-permute-done.2.far_ref), custom_call_target="tpu_custom_call" | custom-call | tf_op jit(solution)/shard_map/join/pallas_call | solution.py:373
  48.5 0.6 %all-to-all-done.1.got_ref = bf16[32,16,256]{2,1,0:T(8,128)(2,1)S(1)} async-done(((bf16[32,16,256]{2,1,0:T(8,128)(2,1)}), bf16[32,16,256]{2,1,0:T(8,128)(2,1)S(1)}, u32[]{:S(2)}, u32[]{:S(2)}) %all-to-all-start.1) | async-done | bytes 262176 | tf_op jit(solution)/shard_map/all_to_all | solution.py:372
  49.1 0.0 copy-done
  49.1 0.7 %finish.1 = f32[16,1024]{1,0:T(8,128)} custom-call(bf16[32,16,256]{2,1,0:T(8,128)(2,1)S(1)} %all-to-all-done.1.got_ref, f32[16,128]{1,0:T(8,128)S(1)} %get-tuple-element.17.count_ref, f32[16,1024]{1,0:T(8,128)S(1)} %copy-done), custom_call_target="tpu_custom_call" | custom-call | tf_op jit(solution)/shard_map/finish/pallas_call | solution.py:381
  (1 shorter events, 0.0 us)
Async XLA Ops:
  5.0 25.2 %all-to-all-start = ((bf16[32,80,128]{2,1,0:T(8,128)(2,1)}), bf16[32,80,128]{2,1,0:T(8,128)(2,1)S(1)}, u32[]{:S(2)}, u32[]{:S(2)}) async-start(bf16[32,80,128]{2,1,0:T(8,128)(2,1)} %bitcast.1), calls=%async_computation | async-start | bytes 1310720 | tf_op jit(solution)/shard_map/all_to_all | solution.py:314
  17.3 2.0 %collective-permute-start.3 = (bf16[2,512,256]{2,1,0:T(8,128)(2,1)S(1)}, bf16[2,512,256]{2,1,0:T(8,128)(2,1)S(1)}, u32[]{:S(2)}, u32[]{:S(2)}) collective-permute-start(bf16[2,512,256]{2,1,0:T(8,128)(2,1)S(1)} %get-tuple-element.15), channel_id=1, source_target_pairs={{0,1},{1,0},{2,3},{3,2},{4,5},{5,4},{6,7},{7,6},{8,9},{9,8},{10,11... | collective-permute-start | bytes 1572872 | tf_op jit(solution)/shard_map/ppermute | solution.py:299
  19.3 12.3 %collective-permute-start.4 = (bf16[512,256]{1,0:T(8,128)(2,1)S(1)}, bf16[512,256]{1,0:T(8,128)(2,1)S(1)}, u32[]{:S(2)}, u32[]{:S(2)}) collective-permute-start(bf16[512,256]{1,0:T(8,128)(2,1)S(1)} %fusion), channel_id=1, source_target_pairs={{0,2},{1,3},{2,0},{3,1},{4,6},{5,7},{6,4},{7,5},{8,10},{9,11},{10,... | collective-permute-start | bytes 786440 | tf_op jit(solution)/shard_map/ppermute | solution.py:299
  31.6 17.5 %copy-start = (f32[16,1024]{1,0:T(8,128)S(1)}, f32[16,1024]{1,0:T(8,128)}, u32[]{:S(2)}) copy-start(f32[16,1024]{1,0:T(8,128)} %old_ref.1) | copy-start | bytes 196612
  35.0 14.1 %all-to-all-start.1 = ((bf16[32,16,256]{2,1,0:T(8,128)(2,1)}), bf16[32,16,256]{2,1,0:T(8,128)(2,1)S(1)}, u32[]{:S(2)}, u32[]{:S(2)}) async-start(bf16[32,16,256]{2,1,0:T(8,128)(2,1)} %bitcast.4), calls=%async_computation.1 | async-start | bytes 524288 | tf_op jit(solution)/shard_map/all_to_all | solution.py:372
  38.5 8.0 %collective-permute-start = (f32[2,64,256]{2,1,0:T(8,128)S(1)}, f32[2,64,256]{2,1,0:T(8,128)S(1)}, u32[]{:S(2)}, u32[]{:S(2)}) collective-permute-start(f32[2,64,256]{2,1,0:T(8,128)S(1)} %get-tuple-element.11), channel_id=1, source_target_pairs={{0,2},{1,3},{2,0},{3,1},{4,6},{5,7},{6,4},{7,5},{8,10},{9,11},{10,... | collective-permute-start | bytes 393224 | tf_op jit(solution)/shard_map/ppermute | solution.py:299
  40.3 6.2 %collective-permute-start.1 = (f32[64,256]{1,0:T(8,128)S(1)}, f32[64,256]{1,0:T(8,128)S(1)}, u32[]{:S(2)}, u32[]{:S(2)}) collective-permute-start(f32[64,256]{1,0:T(8,128)S(1)} %get-tuple-element.12), channel_id=1, source_target_pairs={{0,1},{1,0},{2,3},{3,2},{4,5},{5,4},{6,7},{7,6},{8,9},{9,8},{10,11... | collective-permute-start | bytes 196616 | tf_op jit(solution)/shard_map/ppermute | solution.py:299
  46.5 1.3 %collective-permute-start.2 = (f32[64,256]{1,0:T(8,128)S(1)}, f32[64,256]{1,0:T(8,128)S(1)}, u32[]{:S(2)}, u32[]{:S(2)}) collective-permute-start(f32[64,256]{1,0:T(8,128)S(1)} %slice_bitcast_fusion), channel_id=1, source_target_pairs={{0,1},{1,0},{2,3},{3,2},{4,5},{5,4},{6,7},{7,6},{8,9},{9,8},{10,11... | collective-permute-start | bytes 196616 | tf_op jit(solution)/shard_map/ppermute | solution.py:299

commit v3 on v2

--- a/solution.py
+++ b/solution.py
@@ -111,29 +111,28 @@
     slot_length = dot_rows(rows(length_ref), video_of_slot)
     slot_cluster = dot_rows(rows(cluster_ref), video_of_slot)
     back = (longest - 1 - iota((longest, slots), 0)).astype(f32)
-    slot_codes = jnp.where(back < slot_length, slot_codes, 2.0 * EXACT).astype(bf16)
-    slot_cluster = jnp.where(slot_length > 0, slot_cluster, -1.0).astype(bf16)
-    lane = iota((slots, owners * LANES), 1)
-    place_owner, place_lane = lane // LANES, lane % LANES
-    wanted = iota((slots, owners * LANES), 0) - place_owner * capacity
-    code_lane = me * capacity
-    cluster_lane = lax.rem(me + 1, cents) * capacity
-    count_lane = lax.rem(me + 2, cents) * capacity
-    inside = (wanted >= 0) & (wanted < capacity)
-    place_codes = (inside & (place_lane == wanted + code_lane)).astype(f32).astype(bf16)
-    place_cluster = (inside & (place_lane == wanted + cluster_lane)).astype(f32).astype(bf16)
-    notes = dot(slot_codes, place_codes) + dot(slot_cluster, place_cluster)
-    counts = dot(code_matches(code_ref, code_total), jnp.ones((frame_count, LANES), bf16))
+    slot_codes = jnp.where(back < slot_length, slot_codes, 2.0 * EXACT)
+    slot_cluster = jnp.where(slot_length > 0, slot_cluster, -1.0)
     part = code_total // (owners * cents)
-    note_lane = iota((part, LANES), 1)
-    counted = (note_lane >= count_lane) & (note_lane < count_lane + capacity)
+    high = code_ref[...] // part
+    high_match = (iota((owners * cents, frame_count), 0) == high).astype(f32).astype(bf16)
+    low_match = (iota((part, frame_count), 0) + high * part == code_ref[...]).astype(f32)
+    counts = dot_rows(low_match.astype(bf16), high_match)
+    segment = iota((part, LANES), 1) // capacity
+    code_segment, cluster_segment = me, lax.rem(me + 1, cents)
+    counted = segment == lax.rem(me + 2, cents)
     for owner in range(owners):
+        tile, place = divmod(owner * capacity, LANES)
+        lanes = slice(tile * LANES, (tile + 1) * LANES)
+        turn = lax.rem(code_segment * capacity + LANES - place, LANES)
+        codes = pltpu.roll(slot_codes[:, lanes], turn, 1)
+        turn = lax.rem(cluster_segment * capacity + LANES - place, LANES)
+        cluster = pltpu.roll(slot_cluster[:, lanes], turn, 1)
+        note = jnp.where(segment == code_segment, codes, cluster)
         for cent in range(cents):
-            at = (owner * cents + cent) * part
-            note = jnp.where(
-                counted, counts[at : at + part], notes[:, owner * LANES : (owner + 1) * LANES]
-            )
-            send_ref[owner, cent, 2 * capacity :, :] = note.astype(bf16)
+            at = owner * cents + cent
+            count = jnp.broadcast_to(counts[:, at : at + 1], (part, LANES))
+            send_ref[owner, cent, 2 * capacity :, :] = jnp.where(counted, count, note).astype(bf16)
     weight = 1.0 / jnp.maximum(length, 1.0)
     copies[-1].wait()
     half = share // 2
@@ -203,7 +202,7 @@
     return jnp.concatenate(picks, axis=1)
 
 
-def coarse_kernel(sizes, got_ref, old_hbm, across_ref, here_ref, beside_ref, anchor_ref, old_ref, new_ref, sems):
+def owner_kernel(sizes, got_ref, old_hbm, keep_ref, near_ref, far_ref, code_ref, count_ref, across_ref, here_ref, beside_ref, old_ref, new_ref, sems):
     owners, cents, capacity, longest, code_total = sizes
     me = lax.axis_index("cent")
     clusters, share = old_ref.shape
@@ -216,46 +215,55 @@
     number = jnp.concatenate([number] * (share // LANES), axis=1)
     copies[0].wait()
     new = (sums + old_ref[...].astype(f32)) / (number + 1.0)
-    anchor_ref[...] = new.astype(bf16)
     new_ref[...] = new
+    anchor = new.astype(bf16)
+    bits = longest.bit_length()
+    digits = 30 // bits
+    block = -(-code_total // digits)
+    block = -(-block // 16) * 16
+    segment = iota((longest, LANES), 1) // capacity
+    count = jnp.zeros((longest, LANES), f32)
+    word_row = iota((block, LANES), 0)
+    slot_counts = []
+    for owner in range(owners):
+        codes = jnp.zeros((longest, LANES), f32)
+        for cent in range(cents):
+            note = got_ref[owner * cents + cent, 2 * capacity :, :].astype(f32)
+            codes = jnp.where(segment == cent, note, codes)
+            count = count + jnp.where(segment == (cent + 2) % cents, note, 0.0)
+        codes = codes.astype(jnp.int32) + EXACT
+        place = jnp.where(codes < code_total, codes, -1)
+        one = jnp.ones((longest, LANES), jnp.int32)
+        for digit in range(1, -(-code_total // block)):
+            above = (codes >= digit * block) & (codes < code_total)
+            place = place - jnp.where(above, block, 0)
+            one = jnp.where(above, 1 << (bits * digit), one)
+        words = jnp.zeros((block, LANES), jnp.int32)
+        for row in range(longest):
+            words = words + jnp.where(word_row == place[row : row + 1], one[row : row + 1], 0)
+        held = []
+        for digit in range(-(-code_total // block)):
+            height = min(block, code_total - digit * block)
+            word = words[:height] >> (bits * digit) & ((1 << bits) - 1)
+            held.append(word.astype(f32).astype(bf16))
+        slot_counts.append(jnp.concatenate(held, axis=0))
+    for step in range(cents.bit_length() - 1):
+        count = count + pltpu.roll(count, capacity << step, 1)
+    count_ref[...] = count
+    slot_count = jnp.concatenate(slot_counts, axis=1)
+    cluster_count = dot_rows(slot_count, pick)
+    high = jnp.floor(cluster_count * (1.0 / EXACT))
+    low = cluster_count - high * EXACT
+    moved = dot(low.astype(bf16), anchor) + EXACT * dot(high.astype(bf16), anchor)
+    total = keep_ref[0] + near_ref[0].astype(f32) + far_ref[...].astype(f32)
+    total = total + (dot(slot_count, rows) - moved)
+    code_ref[...] = total.astype(bf16)
     quarter = clusters // cents
     rows_of = lambda step: new_ref[pl.ds(pl.multiple_of((me ^ step) * quarter, quarter), quarter), :]
     across_ref[0] = rows_of(2)
     across_ref[1] = rows_of(3)
     here_ref[...] = rows_of(0)
     beside_ref[...] = rows_of(1)
-
-
-def owner_kernel(sizes, got_ref, anchor_ref, keep_ref, near_ref, far_ref, code_ref, count_ref):
-    owners, cents, capacity, longest, code_total = sizes
-    segment = iota((longest, LANES), 1) // capacity
-    count = jnp.zeros((longest, LANES), f32)
-    slot_counts = []
-    code_row = (iota((code_total, LANES), 0) - EXACT).astype(f32).astype(bf16)
-    for owner in range(owners):
-        codes = jnp.zeros((longest, LANES), f32)
-        for cent in range(cents):
-            note = got_ref[owner * cents + cent, 2 * capacity :, :].astype(f32)
-            codes = jnp.where(segment == cent, note, codes)
-            count = count + jnp.where(segment == (cent + 2) % cents, note, 0.0)
-        codes = codes.astype(bf16)
-        held = jnp.zeros((code_total, LANES), bf16)
-        for row in range(longest):
-            held = held + ones_where(code_row == codes[row : row + 1])
-        slot_counts.append(held)
-    for step in range(cents.bit_length() - 1):
-        count = count + pltpu.roll(count, capacity << step, 1)
-    count_ref[...] = count
-    slot_count = jnp.concatenate(slot_counts, axis=1)
-    pick = cluster_picks(sizes, got_ref, anchor_ref.shape[0])
-    anchor = anchor_ref[...]
-    cluster_count = dot_rows(slot_count, pick)
-    high = jnp.floor(cluster_count * (1.0 / EXACT))
-    low = cluster_count - high * EXACT
-    moved = dot(low.astype(bf16), anchor) + EXACT * dot(high.astype(bf16), anchor)
-    total = keep_ref[0] + near_ref[0].astype(f32) + far_ref[...].astype(f32)
-    total = total + (dot(slot_count, slot_rows(got_ref, capacity)) - moved)
-    code_ref[...] = total.astype(bf16)
 
 
 def finish_kernel(sizes, got_ref, count_ref, old_ref, out_ref):
@@ -334,41 +342,26 @@
     near = swap(give, 1)
     far = swap((keep[1] + near[1].astype(f32)).astype(bf16), 2)
     piece = jax.ShapeDtypeStruct((quarter, share), f32)
-    across, here, beside, anchor = pl.pallas_call(
-        functools.partial(coarse_kernel, sizes),
+    sums, count, across, here, beside = pl.pallas_call(
+        functools.partial(owner_kernel, sizes),
         out_shape=(
+            jax.ShapeDtypeStruct((code_total, share), bf16),
+            jax.ShapeDtypeStruct((part, LANES), f32),
             jax.ShapeDtypeStruct((2, quarter, share), f32),
             piece,
             piece,
-            jax.ShapeDtypeStruct((clusters, share), bf16),
-        ),
-        in_specs=[vmem, hbm],
-        out_specs=(vmem,) * 4,
+        ),
+        in_specs=[vmem, hbm, vmem, vmem, vmem],
+        out_specs=(vmem,) * 5,
         scratch_shapes=[
             pltpu.VMEM((clusters, share), bf16),
             pltpu.VMEM((clusters, share), f32),
             pltpu.SemaphoreType.DMA((1,)),
         ],
         compiler_params=params,
-        name="coarse",
-    )(got, stay(old_coarse))
+        name="owner",
+    )(got, stay(old_coarse), keep, near, far)
     across = swap(across, 2)
-    sums, count = pl.pallas_call(
-        functools.partial(owner_kernel, sizes),
-        out_shape=(
-            jax.ShapeDtypeStruct((code_total, share), bf16),
-            jax.ShapeDtypeStruct((part, LANES), f32),
-        ),
-        in_specs=[vmem] * 5,
-        out_specs=(vmem, vmem),
-        compiler_params=params,
-        cost_estimate=pl.CostEstimate(
-            flops=4 * code_total * devices * capacity * share,
-            bytes_accessed=6 * code_total * share,
-            transcendentals=0,
-        ),
-        name="owner",
-    )(got, anchor, keep, near, far)
     last = lax.all_to_all(sums.reshape(devices, part, share), ("dp", "cent"), 0, 0, tiled=True)
     new_coarse = pl.pallas_call(
         join_kernel,

time: 50.1 us -> 49 us (0.978)
  Pallas kernels: 15.5 us -> 13.2 us
  starting transfers between devices: 14.8 us -> 16 us
    all_to_all x1, waiting for transfers between devices: 9.04 us -> 0.8 us  [summed_body(): lax.all_to_all(send.reshape(devices, chunk, share // 2), ('dp', 'cent'),...]
    ppermute x5, waiting for transfers between devices: 9.08 us -> 17.3 us  [summed_body(): lax.ppermute(array, 'cent', [(index, index ^ bit) for index in range(cent...]
    pallas_call x1 -> x0, Pallas kernels: 1.4 us -> none  [summed_body(): pl.pallas_call(functools.partial(coarse_kernel, sizes), out_shape=(jax.Sh...]
    all_to_all x1, starting transfers between devices: 3.51 us -> 4.72 us  [summed_body(): lax.all_to_all(sums.reshape(devices, part, share), ('dp', 'cent'), 0, 0,...]
    pallas_call x1, Pallas kernels: 4.33 us -> 3.33 us  [summed_body(): pl.pallas_call(functools.partial(pool_kernel, sizes), out_shape=jax.Shape...]
  transfers between devices with their start and end apart: 7 -> 7, of which waited for: 5 -> 6; matrix products, arithmetic and copies ran while one was open for 0% -> 0% of each run, Pallas kernels for 14% -> 12%
where the time goes in v3:
time: 49 us; the launch traced here: 48.6 us
  waiting for transfers between devices  18.7 us (38%)
  starting transfers between devices  16 us (33%)
  Pallas kernels  13.2 us (27%)
  between operations  0.7 us (1%)
    ppermute x5, waiting for transfers between devices, summed_body(): lax.ppermute(array, 'cent', [(index, index ^ bit) for index in range(cent...  17.3 us
    all_to_all x1, starting transfers between devices, summed_body(): lax.all_to_all(send.reshape(devices, chunk, share // 2), ('dp', 'cent'),...  7.3 us
    pallas_call x1, Pallas kernels, summed_body(): pl.pallas_call(functools.partial(code_kernel, sizes), out_shape=(jax.Shap...  5 us
    all_to_all x1, starting transfers between devices, summed_body(): lax.all_to_all(sums.reshape(devices, part, share), ('dp', 'cent'), 0, 0,...  4.72 us
    ppermute x5, starting transfers between devices, summed_body(): lax.ppermute(array, 'cent', [(index, index ^ bit) for index in range(cent...  4 us
    pallas_call x1, Pallas kernels, summed_body(): pl.pallas_call(functools.partial(owner_kernel, sizes), out_shape=(jax.Sha...  3.43 us
    pallas_call x1, Pallas kernels, summed_body(): pl.pallas_call(functools.partial(pool_kernel, sizes), out_shape=jax.Shape...  3.33 us
  transfers between devices with their start and end apart: 7, of which 6 were waited for; matrix products, arithmetic and copies ran while one was open for 0% of the time, Pallas kernels for 12%

profile of v3, /device:TPU:0, one launch (start us, length us, event | category | flops | bytes accessed | tf_op | source)
XLA Modules:
  0.0 48.6 jit_solution(14359877703625598287)
XLA Ops:
  0.6 3.3 %pool.1.pooled_ref = bf16[8,4,80,128]{3,2,1,0:T(8,128)(2,1)} custom-call(s32[1,128]{1,0:T(1,128)} %length_hbm.3, s32[1,128]{1,0:T(1,128)} %owner_hbm.3, s32[1,128]{1,0:T(1,128)} %cluster_hbm.1, s32[1,1024]{1,0:T(1,128)} %bitcast.7, bf16[1024,1024]{1,0:T(8,128)(2,1)} %frames_hbm.3), custom_call_target="tpu_custom_call" | custom-call | tf_op jit(solution)/shard_map/pool/pallas_call | solution.py:313
  4.0 7.3 %all-to-all-start = ((bf16[32,80,128]{2,1,0:T(8,128)(2,1)}), bf16[32,80,128]{2,1,0:T(8,128)(2,1)S(1)}, u32[]{:S(2)}, u32[]{:S(2)}) async-start(bf16[32,80,128]{2,1,0:T(8,128)(2,1)} %bitcast.1), calls=%async_computation | async-start | bytes 1310720 | tf_op jit(solution)/shard_map/all_to_all | solution.py:322
  11.3 5.0 %codes.1 = (f32[2,512,256]{2,1,0:T(8,128)S(1)}, bf16[2,512,256]{2,1,0:T(8,128)(2,1)S(1)}) custom-call(s32[1,128]{1,0:T(1,128)} %length_hbm.3, s32[1,128]{1,0:T(1,128)} %owner_hbm.3, s32[1,1024]{1,0:T(1,128)} %bitcast.8, bf16[1024,1024]{1,0:T(8,128)(2,1)} %frames_hbm.3, bf16[8,4,80,128]{3,2,1,0:T(8,128)(2,1)} %pool.1.pooled_ref), custom_call_target="tpu_custom_call" | custom-call | flops 1610612736 | bytes 6291456 | tf_op jit(solution)/shard_map/codes/pallas_call | solution.py:325
  16.3 0.3 collective-permute-start
  16.6 1.7 %collective-permute-done.near_ref = bf16[2,512,256]{2,1,0:T(8,128)(2,1)S(1)} collective-permute-done((bf16[2,512,256]{2,1,0:T(8,128)(2,1)S(1)}, bf16[2,512,256]{2,1,0:T(8,128)(2,1)S(1)}, u32[]{:S(2)}, u32[]{:S(2)}) %collective-permute-start) | collective-permute-done | bytes 524320 | tf_op jit(solution)/shard_map/ppermute | solution.py:307
  18.3 0.1 fusion
  18.3 0.0 copy-start
  18.3 1.8 %collective-permute-start.1 = (bf16[512,256]{1,0:T(8,128)(2,1)S(1)}, bf16[512,256]{1,0:T(8,128)(2,1)S(1)}, u32[]{:S(2)}, u32[]{:S(2)}) collective-permute-start(bf16[512,256]{1,0:T(8,128)(2,1)S(1)} %fusion), channel_id=1, source_target_pairs={{0,2},{1,3},{2,0},{3,1},{4,6},{5,7},{6,4},{7,5},{8,10},{9,11},{10,... | collective-permute-start | bytes 786440 | tf_op jit(solution)/shard_map/ppermute | solution.py:307
  20.2 8.2 %collective-permute-done.1.far_ref = bf16[512,256]{1,0:T(8,128)(2,1)S(1)} collective-permute-done((bf16[512,256]{1,0:T(8,128)(2,1)S(1)}, bf16[512,256]{1,0:T(8,128)(2,1)S(1)}, u32[]{:S(2)}, u32[]{:S(2)}) %collective-permute-start.1) | collective-permute-done | bytes 262176 | tf_op jit(solution)/shard_map/ppermute | solution.py:307
  28.4 0.8 %all-to-all-done.got_ref = bf16[32,80,128]{2,1,0:T(8,128)(2,1)S(1)} async-done(((bf16[32,80,128]{2,1,0:T(8,128)(2,1)}), bf16[32,80,128]{2,1,0:T(8,128)(2,1)S(1)}, u32[]{:S(2)}, u32[]{:S(2)}) %all-to-all-start) | async-done | bytes 655392 | tf_op jit(solution)/shard_map/all_to_all | solution.py:322
  29.2 3.4 %owner.1 = (bf16[512,256]{1,0:T(8,128)(2,1)}, f32[16,128]{1,0:T(8,128)S(1)}, f32[2,64,256]{2,1,0:T(8,128)S(1)}, f32[64,256]{1,0:T(8,128)S(1)}, f32[64,256]{1,0:T(8,128)S(1)}) custom-call(bf16[32,80,128]{2,1,0:T(8,128)(2,1)S(1)} %all-to-all-done.got_ref, bf16[256,1024]{1,0:T(8,128)(2,1)} %old_hbm.1, f32[2,512,256]{2,1,0:T(8,128)S(1)} %get-tuple-element.9.keep_ref, ...), custom_call_target="tpu_custom_call" | custom-call | tf_op jit(solution)/shard_map/owner/pallas_call | solution.py:345
  32.6 4.7 %all-to-all-start.1 = ((bf16[32,16,256]{2,1,0:T(8,128)(2,1)}), bf16[32,16,256]{2,1,0:T(8,128)(2,1)S(1)}, u32[]{:S(2)}, u32[]{:S(2)}) async-start(bf16[32,16,256]{2,1,0:T(8,128)(2,1)} %bitcast.4), calls=%async_computation.1 | async-start | bytes 524288 | tf_op jit(solution)/shard_map/all_to_all | solution.py:365
  37.4 1.8 %collective-permute-start.2 = (f32[2,64,256]{2,1,0:T(8,128)S(1)}, f32[2,64,256]{2,1,0:T(8,128)S(1)}, u32[]{:S(2)}, u32[]{:S(2)}) collective-permute-start(f32[2,64,256]{2,1,0:T(8,128)S(1)} %get-tuple-element.12), channel_id=1, source_target_pairs={{0,2},{1,3},{2,0},{3,1},{4,6},{5,7},{6,4},{7,5},{8,10},{9,11},{10,... | collective-permute-start | bytes 393224 | tf_op jit(solution)/shard_map/ppermute | solution.py:307
  39.2 0.0 collective-permute-start.3
  39.2 6.2 %collective-permute-done.2.across_ref = f32[2,64,256]{2,1,0:T(8,128)S(1)} collective-permute-done((f32[2,64,256]{2,1,0:T(8,128)S(1)}, f32[2,64,256]{2,1,0:T(8,128)S(1)}, u32[]{:S(2)}, u32[]{:S(2)}) %collective-permute-start.2) | collective-permute-done | bytes 131104 | tf_op jit(solution)/shard_map/ppermute | solution.py:307
  45.4 0.0 collective-permute-start.4
  45.4 0.0 collective-permute-done.3.near_ref
  45.4 1.2 %collective-permute-done.4.far_ref = f32[64,256]{1,0:T(8,128)S(1)} collective-permute-done((f32[64,256]{1,0:T(8,128)S(1)}, f32[64,256]{1,0:T(8,128)S(1)}, u32[]{:S(2)}, u32[]{:S(2)}) %collective-permute-start.4) | collective-permute-done | bytes 65568 | tf_op jit(solution)/shard_map/ppermute | solution.py:307
  46.7 0.7 %join.1 = f32[64,1024]{1,0:T(8,128)} custom-call(f32[64,256]{1,0:T(8,128)S(1)} %get-tuple-element.11.here_ref, f32[2,64,256]{2,1,0:T(8,128)S(1)} %collective-permute-done.2.across_ref, f32[64,256]{1,0:T(8,128)S(1)} %collective-permute-done.3.near_ref, f32[64,256]{1,0:T(8,128)S(1)} %collective-permute-done.4.far_ref), custom_call_target="tpu_custom_call" | custom-call | tf_op jit(solution)/shard_map/join/pallas_call | solution.py:366
  47.4 0.6 %all-to-all-done.1.got_ref = bf16[32,16,256]{2,1,0:T(8,128)(2,1)S(1)} async-done(((bf16[32,16,256]{2,1,0:T(8,128)(2,1)}), bf16[32,16,256]{2,1,0:T(8,128)(2,1)S(1)}, u32[]{:S(2)}, u32[]{:S(2)}) %all-to-all-start.1) | async-done | bytes 262176 | tf_op jit(solution)/shard_map/all_to_all | solution.py:365
  48.0 0.0 copy-done
  48.0 0.7 %finish.1 = f32[16,1024]{1,0:T(8,128)} custom-call(bf16[32,16,256]{2,1,0:T(8,128)(2,1)S(1)} %all-to-all-done.1.got_ref, f32[16,128]{1,0:T(8,128)S(1)} %get-tuple-element.15.count_ref, f32[16,1024]{1,0:T(8,128)S(1)} %copy-done), custom_call_target="tpu_custom_call" | custom-call | tf_op jit(solution)/shard_map/finish/pallas_call | solution.py:374
  (1 shorter events, 0.0 us)
Async XLA Ops:
  4.0 25.2 %all-to-all-start = ((bf16[32,80,128]{2,1,0:T(8,128)(2,1)}), bf16[32,80,128]{2,1,0:T(8,128)(2,1)S(1)}, u32[]{:S(2)}, u32[]{:S(2)}) async-start(bf16[32,80,128]{2,1,0:T(8,128)(2,1)} %bitcast.1), calls=%async_computation | async-start | bytes 1310720 | tf_op jit(solution)/shard_map/all_to_all | solution.py:322
  16.3 2.0 %collective-permute-start = (bf16[2,512,256]{2,1,0:T(8,128)(2,1)S(1)}, bf16[2,512,256]{2,1,0:T(8,128)(2,1)S(1)}, u32[]{:S(2)}, u32[]{:S(2)}) collective-permute-start(bf16[2,512,256]{2,1,0:T(8,128)(2,1)S(1)} %get-tuple-element.10), channel_id=1, source_target_pairs={{0,1},{1,0},{2,3},{3,2},{4,5},{5,4},{6,7},{7,6},{8,9},{9,8},{10,11... | collective-permute-start | bytes 1572872 | tf_op jit(solution)/shard_map/ppermute | solution.py:307
  18.3 29.6 %copy-start = (f32[16,1024]{1,0:T(8,128)S(1)}, f32[16,1024]{1,0:T(8,128)}, u32[]{:S(2)}) copy-start(f32[16,1024]{1,0:T(8,128)} %old_ref.1) | copy-start | bytes 196612
  18.3 10.1 %collective-permute-start.1 = (bf16[512,256]{1,0:T(8,128)(2,1)S(1)}, bf16[512,256]{1,0:T(8,128)(2,1)S(1)}, u32[]{:S(2)}, u32[]{:S(2)}) collective-permute-start(bf16[512,256]{1,0:T(8,128)(2,1)S(1)} %fusion), channel_id=1, source_target_pairs={{0,2},{1,3},{2,0},{3,1},{4,6},{5,7},{6,4},{7,5},{8,10},{9,11},{10,... | collective-permute-start | bytes 786440 | tf_op jit(solution)/shard_map/ppermute | solution.py:307
  32.6 15.3 %all-to-all-start.1 = ((bf16[32,16,256]{2,1,0:T(8,128)(2,1)}), bf16[32,16,256]{2,1,0:T(8,128)(2,1)S(1)}, u32[]{:S(2)}, u32[]{:S(2)}) async-start(bf16[32,16,256]{2,1,0:T(8,128)(2,1)} %bitcast.4), calls=%async_computation.1 | async-start | bytes 524288 | tf_op jit(solution)/shard_map/all_to_all | solution.py:365
  37.4 8.0 %collective-permute-start.2 = (f32[2,64,256]{2,1,0:T(8,128)S(1)}, f32[2,64,256]{2,1,0:T(8,128)S(1)}, u32[]{:S(2)}, u32[]{:S(2)}) collective-permute-start(f32[2,64,256]{2,1,0:T(8,128)S(1)} %get-tuple-element.12), channel_id=1, source_target_pairs={{0,2},{1,3},{2,0},{3,1},{4,6},{5,7},{6,4},{7,5},{8,10},{9,11},{10,... | collective-permute-start | bytes 393224 | tf_op jit(solution)/shard_map/ppermute | solution.py:307
  39.2 6.2 %collective-permute-start.3 = (f32[64,256]{1,0:T(8,128)S(1)}, f32[64,256]{1,0:T(8,128)S(1)}, u32[]{:S(2)}, u32[]{:S(2)}) collective-permute-start(f32[64,256]{1,0:T(8,128)S(1)} %get-tuple-element.13), channel_id=1, source_target_pairs={{0,1},{1,0},{2,3},{3,2},{4,5},{5,4},{6,7},{7,6},{8,9},{9,8},{10,11... | collective-permute-start | bytes 196616 | tf_op jit(solution)/shard_map/ppermute | solution.py:307
  45.4 1.3 %collective-permute-start.4 = (f32[64,256]{1,0:T(8,128)S(1)}, f32[64,256]{1,0:T(8,128)S(1)}, u32[]{:S(2)}, u32[]{:S(2)}) collective-permute-start(f32[64,256]{1,0:T(8,128)S(1)} %slice_bitcast_fusion), channel_id=1, source_target_pairs={{0,1},{1,0},{2,3},{3,2},{4,5},{5,4},{6,7},{7,6},{8,9},{9,8},{10,11... | collective-permute-start | bytes 196616 | tf_op jit(solution)/shard_map/ppermute | solution.py:307

commit v4 on v3

--- a/solution.py
+++ b/solution.py
@@ -76,11 +76,22 @@
     return (iota((code_total, frame_count), 0) == code_ref[...]).astype(f32).astype(bf16)
 
 
-def pool_kernel(sizes, length_hbm, owner_hbm, cluster_hbm, code_hbm, frames_hbm, send_ref, *scratch):
+def pool_kernel(
+    sizes,
+    length_hbm,
+    owner_hbm,
+    cluster_hbm,
+    code_hbm,
+    frames_hbm,
+    send_hbm,
+    pooled_ref,
+    member_ref,
+    *scratch,
+):
     owners, cents, capacity, longest, code_total = sizes
-    length_ref, owner_ref, cluster_ref, code_ref, frames_ref, sems = scratch
+    length_ref, owner_ref, cluster_ref, code_ref, frames_ref, send_ref, sems, out_sems = scratch
     copies = fetch(
-        (length_hbm, owner_hbm, cluster_hbm, code_hbm, frames_hbm), scratch[:-1], sems
+        (length_hbm, owner_hbm, cluster_hbm, code_hbm, frames_hbm), scratch[:5], sems
     )
     me = lax.axis_index("cent")
     frame_count, features = frames_hbm.shape
@@ -91,6 +102,7 @@
     video_of_slot, first, length, member = member_of_slots(
         length_ref, owner_ref, owners, capacity, frame_count
     )
+    member_ref[...] = member
     code = (code_ref[...] - EXACT).astype(f32)
     shifted = pltpu.roll(
         jnp.broadcast_to(code, (longest, frame_count)),
@@ -118,62 +130,70 @@
     high_match = (iota((owners * cents, frame_count), 0) == high).astype(f32).astype(bf16)
     low_match = (iota((part, frame_count), 0) + high * part == code_ref[...]).astype(f32)
     counts = dot_rows(low_match.astype(bf16), high_match)
-    segment = iota((part, LANES), 1) // capacity
-    code_segment, cluster_segment = me, lax.rem(me + 1, cents)
-    counted = segment == lax.rem(me + 2, cents)
+    half = part // 2
+    lane = iota((half, LANES), 1)
+    segment = lane // capacity
+    last_codes, cluster_place, count_place = (
+        segment == lax.rem(me + step, cents) for step in range(1, 4)
+    )
+    front = lane % capacity < capacity // 2
     for owner in range(owners):
         tile, place = divmod(owner * capacity, LANES)
         lanes = slice(tile * LANES, (tile + 1) * LANES)
-        turn = lax.rem(code_segment * capacity + LANES - place, LANES)
-        codes = pltpu.roll(slot_codes[:, lanes], turn, 1)
-        turn = lax.rem(cluster_segment * capacity + LANES - place, LANES)
-        cluster = pltpu.roll(slot_cluster[:, lanes], turn, 1)
-        note = jnp.where(segment == code_segment, codes, cluster)
+        turned = lambda value, step: pltpu.roll(
+            value, lax.rem((me + step) * capacity + LANES - place, LANES), 1
+        )
+        codes = turned(slot_codes[:half, lanes], 0)
+        codes = jnp.where(last_codes, turned(slot_codes[half:, lanes], 1), codes)
+        note = jnp.where(cluster_place, turned(slot_cluster[:half, lanes], 2), codes)
         for cent in range(cents):
             at = owner * cents + cent
-            count = jnp.broadcast_to(counts[:, at : at + 1], (part, LANES))
-            send_ref[owner, cent, 2 * capacity :, :] = jnp.where(counted, count, note).astype(bf16)
+            spread = lambda value: jnp.broadcast_to(value, (half, LANES))
+            count = jnp.where(
+                front, spread(counts[:half, at : at + 1]), spread(counts[half:, at : at + 1])
+            )
+            send_ref[owner, cent, 2 * capacity :, :] = jnp.where(count_place, count, note).astype(
+                bf16
+            )
     weight = 1.0 / jnp.maximum(length, 1.0)
     copies[-1].wait()
     half = share // 2
+    out = []
     for cent in range(cents):
         sums = dot(member, frames_ref[:, cent * share : (cent + 1) * share])
         for side in range(2):
             pooled = (sums[:, side * half : (side + 1) * half] * weight).astype(bf16)
+            at = cent * share + side * half
+            pooled_ref[:, at : at + half] = pooled
             send_ref[:, cent, side * capacity : (side + 1) * capacity, :] = pooled.reshape(
                 owners, capacity, half
             )
-
-
-def code_kernel(sizes, length_hbm, owner_hbm, code_hbm, frames_hbm, pooled_ref, keep_ref, give_ref, *scratch):
+        out.append(
+            pltpu.make_async_copy(send_ref.at[:, cent], send_hbm.at[:, cent], out_sems.at[cent])
+        )
+        out[-1].start()
+    for copy in out:
+        copy.wait()
+
+
+def code_kernel(
+    sizes, code_hbm, frames_hbm, pooled_ref, member_ref, keep_ref, give_ref, code_ref, frames_ref, sems
+):
     owners, cents, capacity, longest, code_total = sizes
-    length_ref, owner_ref, code_ref, frames_ref, sems = scratch
-    copies = fetch((length_hbm, owner_hbm, code_hbm, frames_hbm), scratch[:-1], sems)
+    copies = fetch((code_hbm, frames_hbm), (code_ref, frames_ref), sems)
     me = lax.axis_index("cent")
-    for copy in copies[:-1]:
-        copy.wait()
-    frame_count, features = frames_hbm.shape
-    share = features // cents
-    slots = owners * capacity
-    half = share // 2
-    _, _, _, member = member_of_slots(length_ref, owner_ref, owners, capacity, frame_count)
+    share = frames_hbm.shape[1] // cents
+    copies[0].wait()
     matches = code_matches(code_ref, code_total)
-    slot_counts = dot_rows(matches, member).astype(bf16)
-    copies[-1].wait()
+    slot_counts = dot_rows(matches, member_ref[...]).astype(bf16)
+    copies[1].wait()
     for step in range(cents):
-        cent = me ^ step
-        columns = pl.ds(pl.multiple_of(cent * share, share), share)
-        sums = dot(matches, frames_ref[:, columns])
-        for side in range(2):
-            pooled = pooled_ref[:, cent, side * capacity : (side + 1) * capacity, :].reshape(
-                slots, half
-            )
-            lanes = slice(side * half, (side + 1) * half)
-            centred = sums[:, lanes] - dot(slot_counts, pooled)
-            if step % 2:
-                give_ref[step // 2, :, lanes] = centred.astype(bf16)
-            else:
-                keep_ref[step // 2, :, lanes] = centred
+        columns = pl.ds(pl.multiple_of((me ^ step) * share, share), share)
+        centred = dot(matches, frames_ref[:, columns]) - dot(slot_counts, pooled_ref[:, columns])
+        if step % 2:
+            give_ref[step // 2] = centred.astype(bf16)
+        else:
+            keep_ref[step // 2] = centred
 
 
 def slot_rows(got_ref, capacity):
@@ -187,28 +207,40 @@
     )
 
 
-def cluster_picks(sizes, got_ref, clusters):
-    owners, cents, capacity, longest, code_total = sizes
-    segment = iota((longest, LANES), 1) // capacity
-    cluster_row = iota((clusters, LANES), 0).astype(f32).astype(bf16)
-    picks = []
-    for owner in range(owners):
-        cluster = jnp.zeros((longest, LANES), f32)
-        for cent in range(cents):
-            note = got_ref[owner * cents + cent, 2 * capacity :, :].astype(f32)
-            cluster = jnp.where(segment == (cent + 1) % cents, note, cluster)
-        cluster = pltpu.roll(cluster, LANES - capacity, 1).astype(bf16)
-        picks.append(ones_where(cluster_row == cluster[0:1]))
-    return jnp.concatenate(picks, axis=1)
-
-
-def owner_kernel(sizes, got_ref, old_hbm, keep_ref, near_ref, far_ref, code_ref, count_ref, across_ref, here_ref, beside_ref, old_ref, new_ref, sems):
+def owner_kernel(sizes, got_ref, old_hbm, keep_ref, near_ref, far_ref, code_hbm, count_ref, across_ref, here_ref, beside_ref, old_ref, new_ref, code_ref, sems, out_sems):
     owners, cents, capacity, longest, code_total = sizes
     me = lax.axis_index("cent")
     clusters, share = old_ref.shape
     columns = pl.ds(pl.multiple_of(me * share, share), share)
     copies = fetch((old_hbm.at[:, columns],), (old_ref,), sems)
-    pick = cluster_picks(sizes, got_ref, clusters)
+    half = longest // 2
+    lane = iota((half, LANES), 1)
+    segment = lane // capacity
+    zeros = jnp.zeros((half, LANES), f32)
+    count = zeros
+    cluster_row = iota((clusters, LANES), 0).astype(f32).astype(bf16)
+    picks, code_tiles = [], []
+    for owner in range(owners):
+        front, back, cluster = zeros, zeros, zeros
+        for cent in range(cents):
+            note = got_ref[owner * cents + cent, 2 * capacity :, :].astype(f32)
+            placed = [segment == (cent + step) % cents for step in range(4)]
+            front = jnp.where(placed[0], note, front)
+            back = jnp.where(placed[1], note, back)
+            cluster = jnp.where(placed[2], note, cluster)
+            count = count + jnp.where(placed[3], note, 0.0)
+        back = pltpu.roll(back, LANES - capacity, 1)
+        cluster = pltpu.roll(cluster, LANES - 2 * capacity, 1).astype(bf16)
+        picks.append(ones_where(cluster_row == cluster[0:1]))
+        code_tiles.append(jnp.concatenate([front, back], axis=0))
+    for step in range(cents.bit_length() - 1):
+        count = count + pltpu.roll(count, capacity << step, 1)
+    other = pltpu.roll(count, capacity // 2, 1)
+    first = lane % capacity < capacity // 2
+    count_ref[...] = jnp.concatenate(
+        [jnp.where(first, count, other), jnp.where(first, other, count)], axis=0
+    )
+    pick = jnp.concatenate(picks, axis=1)
     rows = slot_rows(got_ref, capacity)
     sums = dot(pick, rows)
     number = dot(pick, jnp.ones((rows.shape[0], LANES), bf16))
@@ -221,16 +253,9 @@
     digits = 30 // bits
     block = -(-code_total // digits)
     block = -(-block // 16) * 16
-    segment = iota((longest, LANES), 1) // capacity
-    count = jnp.zeros((longest, LANES), f32)
     word_row = iota((block, LANES), 0)
     slot_counts = []
-    for owner in range(owners):
-        codes = jnp.zeros((longest, LANES), f32)
-        for cent in range(cents):
-            note = got_ref[owner * cents + cent, 2 * capacity :, :].astype(f32)
-            codes = jnp.where(segment == cent, note, codes)
-            count = count + jnp.where(segment == (cent + 2) % cents, note, 0.0)
+    for codes in code_tiles:
         codes = codes.astype(jnp.int32) + EXACT
         place = jnp.where(codes < code_total, codes, -1)
         one = jnp.ones((longest, LANES), jnp.int32)
@@ -247,23 +272,28 @@
             word = words[:height] >> (bits * digit) & ((1 << bits) - 1)
             held.append(word.astype(f32).astype(bf16))
         slot_counts.append(jnp.concatenate(held, axis=0))
-    for step in range(cents.bit_length() - 1):
-        count = count + pltpu.roll(count, capacity << step, 1)
-    count_ref[...] = count
     slot_count = jnp.concatenate(slot_counts, axis=1)
     cluster_count = dot_rows(slot_count, pick)
     high = jnp.floor(cluster_count * (1.0 / EXACT))
     low = cluster_count - high * EXACT
     moved = dot(low.astype(bf16), anchor) + EXACT * dot(high.astype(bf16), anchor)
-    total = keep_ref[0] + near_ref[0].astype(f32) + far_ref[...].astype(f32)
-    total = total + (dot(slot_count, rows) - moved)
-    code_ref[...] = total.astype(bf16)
+    out = []
+    height = code_total // 2
+    for side in range(2):
+        part = slice(side * height, (side + 1) * height)
+        total = keep_ref[0, part] + near_ref[0, part].astype(f32) + far_ref[part].astype(f32)
+        total = total + (dot(slot_count[part], rows) - moved[part])
+        code_ref[part] = total.astype(bf16)
+        out.append(pltpu.make_async_copy(code_ref.at[part], code_hbm.at[part], out_sems.at[side]))
+        out[-1].start()
     quarter = clusters // cents
     rows_of = lambda step: new_ref[pl.ds(pl.multiple_of((me ^ step) * quarter, quarter), quarter), :]
     across_ref[0] = rows_of(2)
     across_ref[1] = rows_of(3)
     here_ref[...] = rows_of(0)
     beside_ref[...] = rows_of(1)
+    for copy in out:
+        copy.wait()
 
 
 def finish_kernel(sizes, got_ref, count_ref, old_ref, out_ref):
@@ -302,7 +332,8 @@
     vmem = pl.BlockSpec(memory_space=pltpu.VMEM)
     hbm = pl.BlockSpec(memory_space=pltpu.HBM)
     params = pltpu.CompilerParams(vmem_limit_bytes=32 * 1024 * 1024)
-    chunk = 2 * capacity + longest
+    chunk = 2 * capacity + longest // 2
+    slots = owners * capacity
     stay = lambda array: pltpu.with_memory_space_constraint(array, pltpu.HBM)
     swap = lambda array, bit: lax.ppermute(
         array, "cent", [(index, index ^ bit) for index in range(cents)]
@@ -310,12 +341,22 @@
     row = lambda length: pltpu.VMEM((1, length), jnp.int32)
     frames_scratch = [row(frame_count), pltpu.VMEM((frame_count, features), bf16)]
     quarter = clusters // cents
-    send = pl.pallas_call(
+    send, pooled, member = pl.pallas_call(
         functools.partial(pool_kernel, sizes),
-        out_shape=jax.ShapeDtypeStruct((owners, cents, chunk, share // 2), bf16),
+        out_shape=(
+            jax.ShapeDtypeStruct((owners, cents, chunk, share // 2), bf16),
+            jax.ShapeDtypeStruct((slots, features), bf16),
+            jax.ShapeDtypeStruct((slots, frame_count), bf16),
+        ),
         in_specs=[hbm] * 5,
-        out_specs=vmem,
-        scratch_shapes=[row(videos)] * 3 + frames_scratch + [pltpu.SemaphoreType.DMA((5,))],
+        out_specs=(hbm, vmem, vmem),
+        scratch_shapes=[row(videos)] * 3
+        + frames_scratch
+        + [
+            pltpu.VMEM((owners, cents, chunk, share // 2), bf16),
+            pltpu.SemaphoreType.DMA((5,)),
+            pltpu.SemaphoreType.DMA((cents,)),
+        ],
         compiler_params=params,
         name="pool",
     )(*map(stay, (video_length, video_owner, video_cluster, frame_code, frames)))
@@ -328,9 +369,9 @@
             jax.ShapeDtypeStruct((cents // 2, code_total, share), f32),
             jax.ShapeDtypeStruct((cents // 2, code_total, share), bf16),
         ),
-        in_specs=[hbm] * 4 + [vmem],
+        in_specs=[hbm] * 2 + [vmem] * 2,
         out_specs=(vmem, vmem),
-        scratch_shapes=[row(videos)] * 2 + frames_scratch + [pltpu.SemaphoreType.DMA((4,))],
+        scratch_shapes=frames_scratch + [pltpu.SemaphoreType.DMA((2,))],
         compiler_params=params,
         cost_estimate=pl.CostEstimate(
             flops=3 * code_total * frame_count * features,
@@ -338,7 +379,7 @@
             transcendentals=0,
         ),
         name="codes",
-    )(*map(stay, (video_length, video_owner, frame_code, frames)), send)
+    )(stay(frame_code), stay(frames), pooled, member)
     near = swap(give, 1)
     far = swap((keep[1] + near[1].astype(f32)).astype(bf16), 2)
     piece = jax.ShapeDtypeStruct((quarter, share), f32)
@@ -352,11 +393,13 @@
             piece,
         ),
         in_specs=[vmem, hbm, vmem, vmem, vmem],
-        out_specs=(vmem,) * 5,
+        out_specs=(hbm,) + (vmem,) * 4,
         scratch_shapes=[
             pltpu.VMEM((clusters, share), bf16),
             pltpu.VMEM((clusters, share), f32),
+            pltpu.VMEM((code_total, share), bf16),
             pltpu.SemaphoreType.DMA((1,)),
+            pltpu.SemaphoreType.DMA((2,)),
         ],
         compiler_params=params,
         name="owner",

time: 49 us -> 47.9 us (0.978)
  Pallas kernels: 13.2 us -> 11.8 us
  waiting for transfers between devices: 18.7 us -> 19.2 us
    pallas_call x1, Pallas kernels: 5 us -> 3.31 us  [summed_body(): pl.pallas_call(functools.partial(code_kernel, sizes), out_shape=(jax.Shap...]
  transfers between devices with their start and end apart: 7 -> 7, of which waited for: 6 -> 6; matrix products, arithmetic and copies ran while one was open for 0% -> 0% of each run, Pallas kernels for 12% -> 8%
where the time goes in v4:
time: 47.9 us; the launch traced here: 47.5 us
  waiting for transfers between devices  19.2 us (40%)
  starting transfers between devices  15.8 us (33%)
  Pallas kernels  11.8 us (25%)
  between operations  0.7 us (1%)
    ppermute x5, waiting for transfers between devices, summed_body(): lax.ppermute(array, 'cent', [(index, index ^ bit) for index in range(cent...  17.7 us
    all_to_all x1, starting transfers between devices, summed_body(): lax.all_to_all(send.reshape(devices, chunk, share // 2), ('dp', 'cent'),...  7.3 us
    all_to_all x1, starting transfers between devices, summed_body(): lax.all_to_all(sums.reshape(devices, part, share), ('dp', 'cent'), 0, 0,...  4.49 us
    ppermute x5, starting transfers between devices, summed_body(): lax.ppermute(array, 'cent', [(index, index ^ bit) for index in range(cent...  4 us
    pallas_call x1, Pallas kernels, summed_body(): pl.pallas_call(functools.partial(owner_kernel, sizes), out_shape=(jax.Sha...  3.79 us
    pallas_call x1, Pallas kernels, summed_body(): pl.pallas_call(functools.partial(code_kernel, sizes), out_shape=(jax.Shap...  3.31 us
    pallas_call x1, Pallas kernels, summed_body(): pl.pallas_call(functools.partial(pool_kernel, sizes), out_shape=(jax.Shap...  3.3 us
  transfers between devices with their start and end apart: 7, of which 6 were waited for; matrix products, arithmetic and copies ran while one was open for 0% of the time, Pallas kernels for 8%

profile of v4, /device:TPU:0, one launch (start us, length us, event | category | flops | bytes accessed | tf_op | source)
XLA Modules:
  0.0 47.5 jit_solution(11982424947451376989)
XLA Ops:
  0.6 3.3 %pool.1 = (bf16[8,4,72,128]{3,2,1,0:T(8,128)(2,1)}, bf16[256,1024]{1,0:T(8,128)(2,1)S(1)}, bf16[256,1024]{1,0:T(8,128)(2,1)S(1)}) custom-call(s32[1,128]{1,0:T(1,128)} %length_hbm.1, s32[1,128]{1,0:T(1,128)} %owner_hbm.1, s32[1,128]{1,0:T(1,128)} %cluster_hbm.1, s32[1,1024]{1,0:T(1,128)} %bitcast.7, bf16[1024,1024]{1,0:T(8,128)(2,1)} %frames_hbm.3), custom_call_target="tpu_custom_call" | custom-call | tf_op jit(solution)/shard_map/pool/pallas_call | solution.py:344
  3.9 7.3 %all-to-all-start = ((bf16[32,72,128]{2,1,0:T(8,128)(2,1)}), bf16[32,72,128]{2,1,0:T(8,128)(2,1)S(1)}, u32[]{:S(2)}, u32[]{:S(2)}) async-start(bf16[32,72,128]{2,1,0:T(8,128)(2,1)} %bitcast.1), calls=%async_computation | async-start | bytes 1179648 | tf_op jit(solution)/shard_map/all_to_all | solution.py:363
  11.3 3.3 %codes.1 = (f32[2,512,256]{2,1,0:T(8,128)S(1)}, bf16[2,512,256]{2,1,0:T(8,128)(2,1)S(1)}) custom-call(s32[1,1024]{1,0:T(1,128)} %bitcast.8, bf16[1024,1024]{1,0:T(8,128)(2,1)} %frames_hbm.3, bf16[256,1024]{1,0:T(8,128)(2,1)S(1)} %get-tuple-element.13.pooled_ref, bf16[256,1024]{1,0:T(8,128)(2,1)S(1)} %get-tuple-element.14.member_ref), custom_call_target="tpu_custom_call" | custom-call | flops 1610612736 | bytes 6291456 | tf_op jit(solution)/shard_map/codes/pallas_call | solution.py:366
  14.6 0.3 collective-permute-start
  14.9 1.7 %collective-permute-done.near_ref = bf16[2,512,256]{2,1,0:T(8,128)(2,1)S(1)} collective-permute-done((bf16[2,512,256]{2,1,0:T(8,128)(2,1)S(1)}, bf16[2,512,256]{2,1,0:T(8,128)(2,1)S(1)}, u32[]{:S(2)}, u32[]{:S(2)}) %collective-permute-start) | collective-permute-done | bytes 524320 | tf_op jit(solution)/shard_map/ppermute | solution.py:338
  16.5 0.1 fusion
  16.6 0.0 copy-start
  16.6 1.8 %collective-permute-start.1 = (bf16[512,256]{1,0:T(8,128)(2,1)S(1)}, bf16[512,256]{1,0:T(8,128)(2,1)S(1)}, u32[]{:S(2)}, u32[]{:S(2)}) collective-permute-start(bf16[512,256]{1,0:T(8,128)(2,1)S(1)} %fusion), channel_id=1, source_target_pairs={{0,2},{1,3},{2,0},{3,1},{4,6},{5,7},{6,4},{7,5},{8,10},{9,11},{10,... | collective-permute-start | bytes 786440 | tf_op jit(solution)/shard_map/ppermute | solution.py:338
  18.5 8.6 %collective-permute-done.1.far_ref = bf16[512,256]{1,0:T(8,128)(2,1)S(1)} collective-permute-done((bf16[512,256]{1,0:T(8,128)(2,1)S(1)}, bf16[512,256]{1,0:T(8,128)(2,1)S(1)}, u32[]{:S(2)}, u32[]{:S(2)}) %collective-permute-start.1) | collective-permute-done | bytes 262176 | tf_op jit(solution)/shard_map/ppermute | solution.py:338
  27.0 1.0 %all-to-all-done.got_ref = bf16[32,72,128]{2,1,0:T(8,128)(2,1)S(1)} async-done(((bf16[32,72,128]{2,1,0:T(8,128)(2,1)}), bf16[32,72,128]{2,1,0:T(8,128)(2,1)S(1)}, u32[]{:S(2)}, u32[]{:S(2)}) %all-to-all-start) | async-done | bytes 589856 | tf_op jit(solution)/shard_map/all_to_all | solution.py:363
  28.0 3.8 %owner.1 = (bf16[512,256]{1,0:T(8,128)(2,1)}, f32[16,128]{1,0:T(8,128)S(1)}, f32[2,64,256]{2,1,0:T(8,128)S(1)}, f32[64,256]{1,0:T(8,128)S(1)}, f32[64,256]{1,0:T(8,128)S(1)}) custom-call(bf16[32,72,128]{2,1,0:T(8,128)(2,1)S(1)} %all-to-all-done.got_ref, bf16[256,1024]{1,0:T(8,128)(2,1)} %old_hbm.1, f32[2,512,256]{2,1,0:T(8,128)S(1)} %get-tuple-element.15.keep_ref, ...), custom_call_target="tpu_custom_call" | custom-call | tf_op jit(solution)/shard_map/owner/pallas_call | solution.py:386
  31.8 4.5 %all-to-all-start.1 = ((bf16[32,16,256]{2,1,0:T(8,128)(2,1)}), bf16[32,16,256]{2,1,0:T(8,128)(2,1)S(1)}, u32[]{:S(2)}, u32[]{:S(2)}) async-start(bf16[32,16,256]{2,1,0:T(8,128)(2,1)} %bitcast.4), calls=%async_computation.1 | async-start | bytes 524288 | tf_op jit(solution)/shard_map/all_to_all | solution.py:408
  36.3 1.8 %collective-permute-start.2 = (f32[2,64,256]{2,1,0:T(8,128)S(1)}, f32[2,64,256]{2,1,0:T(8,128)S(1)}, u32[]{:S(2)}, u32[]{:S(2)}) collective-permute-start(f32[2,64,256]{2,1,0:T(8,128)S(1)} %get-tuple-element.18), channel_id=1, source_target_pairs={{0,2},{1,3},{2,0},{3,1},{4,6},{5,7},{6,4},{7,5},{8,10},{9,11},{10,... | collective-permute-start | bytes 393224 | tf_op jit(solution)/shard_map/ppermute | solution.py:338
  38.1 0.0 collective-permute-start.3
  38.1 6.2 %collective-permute-done.2.across_ref = f32[2,64,256]{2,1,0:T(8,128)S(1)} collective-permute-done((f32[2,64,256]{2,1,0:T(8,128)S(1)}, f32[2,64,256]{2,1,0:T(8,128)S(1)}, u32[]{:S(2)}, u32[]{:S(2)}) %collective-permute-start.2) | collective-permute-done | bytes 131104 | tf_op jit(solution)/shard_map/ppermute | solution.py:338
  44.3 0.0 collective-permute-start.4
  44.3 0.0 collective-permute-done.3.near_ref
  44.3 1.2 %collective-permute-done.4.far_ref = f32[64,256]{1,0:T(8,128)S(1)} collective-permute-done((f32[64,256]{1,0:T(8,128)S(1)}, f32[64,256]{1,0:T(8,128)S(1)}, u32[]{:S(2)}, u32[]{:S(2)}) %collective-permute-start.4) | collective-permute-done | bytes 65568 | tf_op jit(solution)/shard_map/ppermute | solution.py:338
  45.6 0.7 %join.1 = f32[64,1024]{1,0:T(8,128)} custom-call(f32[64,256]{1,0:T(8,128)S(1)} %get-tuple-element.17.here_ref, f32[2,64,256]{2,1,0:T(8,128)S(1)} %collective-permute-done.2.across_ref, f32[64,256]{1,0:T(8,128)S(1)} %collective-permute-done.3.near_ref, f32[64,256]{1,0:T(8,128)S(1)} %collective-permute-done.4.far_ref), custom_call_target="tpu_custom_call" | custom-call | tf_op jit(solution)/shard_map/join/pallas_call | solution.py:409
  46.3 0.6 %all-to-all-done.1.got_ref = bf16[32,16,256]{2,1,0:T(8,128)(2,1)S(1)} async-done(((bf16[32,16,256]{2,1,0:T(8,128)(2,1)}), bf16[32,16,256]{2,1,0:T(8,128)(2,1)S(1)}, u32[]{:S(2)}, u32[]{:S(2)}) %all-to-all-start.1) | async-done | bytes 262176 | tf_op jit(solution)/shard_map/all_to_all | solution.py:408
  46.9 0.0 copy-done
  46.9 0.7 %finish.1 = f32[16,1024]{1,0:T(8,128)} custom-call(bf16[32,16,256]{2,1,0:T(8,128)(2,1)S(1)} %all-to-all-done.1.got_ref, f32[16,128]{1,0:T(8,128)S(1)} %get-tuple-element.21.count_ref, f32[16,1024]{1,0:T(8,128)S(1)} %copy-done), custom_call_target="tpu_custom_call" | custom-call | tf_op jit(solution)/shard_map/finish/pallas_call | solution.py:417
  (1 shorter events, 0.0 us)
Async XLA Ops:
  3.9 24.0 %all-to-all-start = ((bf16[32,72,128]{2,1,0:T(8,128)(2,1)}), bf16[32,72,128]{2,1,0:T(8,128)(2,1)S(1)}, u32[]{:S(2)}, u32[]{:S(2)}) async-start(bf16[32,72,128]{2,1,0:T(8,128)(2,1)} %bitcast.1), calls=%async_computation | async-start | bytes 1179648 | tf_op jit(solution)/shard_map/all_to_all | solution.py:363
  14.6 2.0 %collective-permute-start = (bf16[2,512,256]{2,1,0:T(8,128)(2,1)S(1)}, bf16[2,512,256]{2,1,0:T(8,128)(2,1)S(1)}, u32[]{:S(2)}, u32[]{:S(2)}) collective-permute-start(bf16[2,512,256]{2,1,0:T(8,128)(2,1)S(1)} %get-tuple-element.16), channel_id=1, source_target_pairs={{0,1},{1,0},{2,3},{3,2},{4,5},{5,4},{6,7},{7,6},{8,9},{9,8},{10,11... | collective-permute-start | bytes 1572872 | tf_op jit(solution)/shard_map/ppermute | solution.py:338
  16.6 30.3 %copy-start = (f32[16,1024]{1,0:T(8,128)S(1)}, f32[16,1024]{1,0:T(8,128)}, u32[]{:S(2)}) copy-start(f32[16,1024]{1,0:T(8,128)} %old_ref.1) | copy-start | bytes 196612
  16.6 10.4 %collective-permute-start.1 = (bf16[512,256]{1,0:T(8,128)(2,1)S(1)}, bf16[512,256]{1,0:T(8,128)(2,1)S(1)}, u32[]{:S(2)}, u32[]{:S(2)}) collective-permute-start(bf16[512,256]{1,0:T(8,128)(2,1)S(1)} %fusion), channel_id=1, source_target_pairs={{0,2},{1,3},{2,0},{3,1},{4,6},{5,7},{6,4},{7,5},{8,10},{9,11},{10,... | collective-permute-start | bytes 786440 | tf_op jit(solution)/shard_map/ppermute | solution.py:338
  31.8 15.1 %all-to-all-start.1 = ((bf16[32,16,256]{2,1,0:T(8,128)(2,1)}), bf16[32,16,256]{2,1,0:T(8,128)(2,1)S(1)}, u32[]{:S(2)}, u32[]{:S(2)}) async-start(bf16[32,16,256]{2,1,0:T(8,128)(2,1)} %bitcast.4), calls=%async_computation.1 | async-start | bytes 524288 | tf_op jit(solution)/shard_map/all_to_all | solution.py:408
  36.3 8.0 %collective-permute-start.2 = (f32[2,64,256]{2,1,0:T(8,128)S(1)}, f32[2,64,256]{2,1,0:T(8,128)S(1)}, u32[]{:S(2)}, u32[]{:S(2)}) collective-permute-start(f32[2,64,256]{2,1,0:T(8,128)S(1)} %get-tuple-element.18), channel_id=1, source_target_pairs={{0,2},{1,3},{2,0},{3,1},{4,6},{5,7},{6,4},{7,5},{8,10},{9,11},{10,... | collective-permute-start | bytes 393224 | tf_op jit(solution)/shard_map/ppermute | solution.py:338
  38.1 6.2 %collective-permute-start.3 = (f32[64,256]{1,0:T(8,128)S(1)}, f32[64,256]{1,0:T(8,128)S(1)}, u32[]{:S(2)}, u32[]{:S(2)}) collective-permute-start(f32[64,256]{1,0:T(8,128)S(1)} %get-tuple-element.19), channel_id=1, source_target_pairs={{0,1},{1,0},{2,3},{3,2},{4,5},{5,4},{6,7},{7,6},{8,9},{9,8},{10,11... | collective-permute-start | bytes 196616 | tf_op jit(solution)/shard_map/ppermute | solution.py:338
  44.3 1.3 %collective-permute-start.4 = (f32[64,256]{1,0:T(8,128)S(1)}, f32[64,256]{1,0:T(8,128)S(1)}, u32[]{:S(2)}, u32[]{:S(2)}) collective-permute-start(f32[64,256]{1,0:T(8,128)S(1)} %slice_bitcast_fusion), channel_id=1, source_target_pairs={{0,1},{1,0},{2,3},{3,2},{4,5},{5,4},{6,7},{7,6},{8,9},{9,8},{10,11... | collective-permute-start | bytes 196616 | tf_op jit(solution)/shard_map/ppermute | solution.py:338

commit v5 on v4

--- a/solution.py
+++ b/solution.py
@@ -176,24 +176,49 @@
         copy.wait()
 
 
-def code_kernel(
-    sizes, code_hbm, frames_hbm, pooled_ref, member_ref, keep_ref, give_ref, code_ref, frames_ref, sems
+def give_kernel(
+    sizes,
+    code_hbm,
+    frames_hbm,
+    pooled_ref,
+    member_ref,
+    give_ref,
+    matches_ref,
+    counts_ref,
+    code_ref,
+    frames_ref,
+    sems,
 ):
     owners, cents, capacity, longest, code_total = sizes
     copies = fetch((code_hbm, frames_hbm), (code_ref, frames_ref), sems)
     me = lax.axis_index("cent")
     share = frames_hbm.shape[1] // cents
     copies[0].wait()
-    matches = code_matches(code_ref, code_total)
-    slot_counts = dot_rows(matches, member_ref[...]).astype(bf16)
+    matches_ref[...] = code_matches(code_ref, code_total)
+    counts_ref[...] = dot_rows(matches_ref[...], member_ref[...]).astype(bf16)
     copies[1].wait()
-    for step in range(cents):
+    for step in range(1, cents, 2):
         columns = pl.ds(pl.multiple_of((me ^ step) * share, share), share)
-        centred = dot(matches, frames_ref[:, columns]) - dot(slot_counts, pooled_ref[:, columns])
-        if step % 2:
-            give_ref[step // 2] = centred.astype(bf16)
-        else:
-            keep_ref[step // 2] = centred
+        sums = dot(matches_ref[...], frames_ref[:, columns])
+        give_ref[step // 2] = (sums - dot(counts_ref[...], pooled_ref[:, columns])).astype(bf16)
+
+
+def keep_kernel(sizes, frames_hbm, pooled_ref, matches_ref, counts_ref, keep_ref, frames_ref, sems):
+    owners, cents, capacity, longest, code_total = sizes
+    me = lax.axis_index("cent")
+    share = frames_hbm.shape[1] // cents
+    spans = [
+        pl.ds(pl.multiple_of((me ^ step) * share, share), share) for step in range(0, cents, 2)
+    ]
+    copies = fetch(
+        [frames_hbm.at[:, span] for span in spans],
+        [frames_ref.at[at] for at in range(cents // 2)],
+        sems,
+    )
+    for at, span in enumerate(spans):
+        removed = dot(counts_ref[...], pooled_ref[:, span])
+        copies[at].wait()
+        keep_ref[at] = dot(matches_ref[...], frames_ref[at]) - removed
 
 
 def slot_rows(got_ref, capacity):
@@ -207,7 +232,7 @@
     )
 
 
-def owner_kernel(sizes, got_ref, old_hbm, keep_ref, near_ref, far_ref, code_hbm, count_ref, across_ref, here_ref, beside_ref, old_ref, new_ref, code_ref, sems, out_sems):
+def owner_kernel(sizes, got_ref, old_hbm, code_ref, count_ref, here_ref, beside_ref, across_ref, diagonal_ref, old_ref, new_ref, sems):
     owners, cents, capacity, longest, code_total = sizes
     me = lax.axis_index("cent")
     clusters, share = old_ref.shape
@@ -277,23 +302,11 @@
     high = jnp.floor(cluster_count * (1.0 / EXACT))
     low = cluster_count - high * EXACT
     moved = dot(low.astype(bf16), anchor) + EXACT * dot(high.astype(bf16), anchor)
-    out = []
-    height = code_total // 2
-    for side in range(2):
-        part = slice(side * height, (side + 1) * height)
-        total = keep_ref[0, part] + near_ref[0, part].astype(f32) + far_ref[part].astype(f32)
-        total = total + (dot(slot_count[part], rows) - moved[part])
-        code_ref[part] = total.astype(bf16)
-        out.append(pltpu.make_async_copy(code_ref.at[part], code_hbm.at[part], out_sems.at[side]))
-        out[-1].start()
+    code_ref[...] = dot(slot_count, rows) - moved
     quarter = clusters // cents
     rows_of = lambda step: new_ref[pl.ds(pl.multiple_of((me ^ step) * quarter, quarter), quarter), :]
-    across_ref[0] = rows_of(2)
-    across_ref[1] = rows_of(3)
-    here_ref[...] = rows_of(0)
-    beside_ref[...] = rows_of(1)
-    for copy in out:
-        copy.wait()
+    for step, ref in enumerate((here_ref, beside_ref, across_ref, diagonal_ref)):
+        ref[...] = rows_of(step)
 
 
 def finish_kernel(sizes, got_ref, count_ref, old_ref, out_ref):
@@ -308,11 +321,11 @@
         out_ref[:, lanes] = (total + code_prior * old_ref[:, lanes]) / prior
 
 
-def join_kernel(here_ref, across_ref, near_ref, far_ref, out_ref):
+def join_kernel(here_ref, beside_ref, across_ref, diagonal_ref, out_ref):
     me = lax.axis_index("cent")
     share = here_ref.shape[1]
-    for step, value in enumerate((here_ref[...], near_ref[...], across_ref[0], far_ref[...])):
-        out_ref[:, pl.ds(pl.multiple_of((me ^ step) * share, share), share)] = value
+    for step, ref in enumerate((here_ref, beside_ref, across_ref, diagonal_ref)):
+        out_ref[:, pl.ds(pl.multiple_of((me ^ step) * share, share), share)] = ref[...]
 
 
 def summed_body(frames, video_length, video_owner, video_cluster, frame_code, old_coarse, old_codes):
@@ -363,48 +376,63 @@
     got = lax.all_to_all(
         send.reshape(devices, chunk, share // 2), ("dp", "cent"), 0, 0, tiled=True
     )
-    keep, give = pl.pallas_call(
-        functools.partial(code_kernel, sizes),
+    table = (cents // 2, code_total, share)
+    give, matches, slot_counts = pl.pallas_call(
+        functools.partial(give_kernel, sizes),
         out_shape=(
-            jax.ShapeDtypeStruct((cents // 2, code_total, share), f32),
-            jax.ShapeDtypeStruct((cents // 2, code_total, share), bf16),
+            jax.ShapeDtypeStruct(table, bf16),
+            jax.ShapeDtypeStruct((code_total, frame_count), bf16),
+            jax.ShapeDtypeStruct((code_total, slots), bf16),
         ),
         in_specs=[hbm] * 2 + [vmem] * 2,
-        out_specs=(vmem, vmem),
+        out_specs=(vmem,) * 3,
         scratch_shapes=frames_scratch + [pltpu.SemaphoreType.DMA((2,))],
         compiler_params=params,
         cost_estimate=pl.CostEstimate(
-            flops=3 * code_total * frame_count * features,
-            bytes_accessed=6 * frame_count * features,
+            flops=2 * code_total * frame_count * features,
+            bytes_accessed=4 * frame_count * features,
             transcendentals=0,
         ),
-        name="codes",
+        name="give",
     )(stay(frame_code), stay(frames), pooled, member)
     near = swap(give, 1)
+    keep = pl.pallas_call(
+        functools.partial(keep_kernel, sizes),
+        out_shape=jax.ShapeDtypeStruct(table, f32),
+        in_specs=[hbm] + [vmem] * 3,
+        out_specs=vmem,
+        scratch_shapes=[
+            pltpu.VMEM((cents // 2, frame_count, share), bf16),
+            pltpu.SemaphoreType.DMA((cents // 2,)),
+        ],
+        compiler_params=params,
+        cost_estimate=pl.CostEstimate(
+            flops=2 * code_total * frame_count * features,
+            bytes_accessed=4 * frame_count * features,
+            transcendentals=0,
+        ),
+        name="keep",
+    )(stay(frames), pooled, matches, slot_counts)
     far = swap((keep[1] + near[1].astype(f32)).astype(bf16), 2)
     piece = jax.ShapeDtypeStruct((quarter, share), f32)
-    sums, count, across, here, beside = pl.pallas_call(
+    sums, count, here, beside, across, diagonal = pl.pallas_call(
         functools.partial(owner_kernel, sizes),
         out_shape=(
-            jax.ShapeDtypeStruct((code_total, share), bf16),
+            jax.ShapeDtypeStruct((code_total, share), f32),
             jax.ShapeDtypeStruct((part, LANES), f32),
-            jax.ShapeDtypeStruct((2, quarter, share), f32),
-            piece,
-            piece,
-        ),
-        in_specs=[vmem, hbm, vmem, vmem, vmem],
-        out_specs=(hbm,) + (vmem,) * 4,
+        )
+        + (piece,) * cents,
+        in_specs=[vmem, hbm],
+        out_specs=(vmem,) * (2 + cents),
         scratch_shapes=[
             pltpu.VMEM((clusters, share), bf16),
             pltpu.VMEM((clusters, share), f32),
-            pltpu.VMEM((code_total, share), bf16),
             pltpu.SemaphoreType.DMA((1,)),
-            pltpu.SemaphoreType.DMA((2,)),
         ],
         compiler_params=params,
         name="owner",
-    )(got, stay(old_coarse), keep, near, far)
-    across = swap(across, 2)
+    )(got, stay(old_coarse))
+    sums = (sums + (keep[0] + near[0].astype(f32) + far.astype(f32))).astype(bf16)
     last = lax.all_to_all(sums.reshape(devices, part, share), ("dp", "cent"), 0, 0, tiled=True)
     new_coarse = pl.pallas_call(
         join_kernel,
@@ -413,7 +441,7 @@
         out_specs=vmem,
         compiler_params=params,
         name="join",
-    )(here, across, swap(beside, 1), swap(across[1], 1))
+    )(here, swap(beside, 1), swap(across, 2), swap(diagonal, 3))
     new_codes = pl.pallas_call(
         functools.partial(finish_kernel, sizes),
         out_shape=jax.ShapeDtypeStruct((part, features), f32),

time: 47.9 us -> 46.6 us (0.973)
  waiting for transfers between devices: 19.2 us -> 17.3 us
  starting transfers between devices: 15.8 us -> 14.7 us
  Pallas kernels: 11.8 us -> 12.7 us
  other arithmetic: 0.06 us -> 0.87 us
    ppermute x5, waiting for transfers between devices: 17.7 us -> 5.35 us  [summed_body(): lax.ppermute(array, 'cent', [(index, index ^ bit) for index in range(cent...]
    all_to_all x1, waiting for transfers between devices: 0.95 us -> 9.48 us  [summed_body(): lax.all_to_all(send.reshape(devices, chunk, share // 2), ('dp', 'cent'),...]
    all_to_all x1, waiting for transfers between devices: 0.58 us -> 2.52 us  [summed_body(): lax.all_to_all(sums.reshape(devices, part, share), ('dp', 'cent'), 0, 0,...]
    pallas_call x1 -> x2, Pallas kernels: 3.31 us -> 5.09 us  [the longest x1 2.62 us: summed_body(): pl.pallas_call(functools.partial(give_kernel, sizes), out_shape=(jax.Shap...]
    all_to_all x1, starting transfers between devices: 4.49 us -> 3.28 us  [summed_body(): lax.all_to_all(sums.reshape(devices, part, share), ('dp', 'cent'), 0, 0,...]
    pallas_call x1, Pallas kernels: 3.79 us -> 2.86 us  [summed_body(): pl.pallas_call(functools.partial(owner_kernel, sizes), out_shape=(jax.Sha...]
    convert_element_type x0 -> x1, other arithmetic: none -> 0.81 us  [summed_body(): (sums + (keep[0] + near[0].astype(f32) + far.astype(f32))).astype(bf16)]
  transfers between devices with their start and end apart: 7 -> 7, of which waited for: 6 -> 4; matrix products, arithmetic and copies ran while one was open for 0% -> 0% of each run, Pallas kernels for 8% -> 19%
where the time goes in v5:
time: 46.6 us; the launch traced here: 46.3 us
  waiting for transfers between devices  17.3 us (37%)
  starting transfers between devices  14.7 us (32%)
  Pallas kernels  12.7 us (27%)
  other arithmetic  0.87 us (2%)
  between operations  0.72 us (2%)
    all_to_all x1, waiting for transfers between devices, summed_body(): lax.all_to_all(send.reshape(devices, chunk, share // 2), ('dp', 'cent'),...  9.48 us
    all_to_all x1, starting transfers between devices, summed_body(): lax.all_to_all(send.reshape(devices, chunk, share // 2), ('dp', 'cent'),...  7.3 us
    ppermute x5, waiting for transfers between devices, summed_body(): lax.ppermute(array, 'cent', [(index, index ^ bit) for index in range(cent...  5.35 us
    ppermute x5, starting transfers between devices, summed_body(): lax.ppermute(array, 'cent', [(index, index ^ bit) for index in range(cent...  4.07 us
    pallas_call x1, Pallas kernels, summed_body(): pl.pallas_call(functools.partial(pool_kernel, sizes), out_shape=(jax.Shap...  3.3 us
    all_to_all x1, starting transfers between devices, summed_body(): lax.all_to_all(sums.reshape(devices, part, share), ('dp', 'cent'), 0, 0,...  3.28 us
    pallas_call x1, Pallas kernels, summed_body(): pl.pallas_call(functools.partial(owner_kernel, sizes), out_shape=(jax.Sha...  2.86 us
    pallas_call x1, Pallas kernels, summed_body(): pl.pallas_call(functools.partial(give_kernel, sizes), out_shape=(jax.Shap...  2.62 us
  transfers between devices with their start and end apart: 7, of which 4 were waited for; matrix products, arithmetic and copies ran while one was open for 0% of the time, Pallas kernels for 19%

profile of v5, /device:TPU:0, one launch (start us, length us, event | category | flops | bytes accessed | tf_op | source)
XLA Modules:
  0.0 46.3 jit_solution(18001685322177081754)
XLA Ops:
  0.6 3.3 %pool.1 = (bf16[8,4,72,128]{3,2,1,0:T(8,128)(2,1)}, bf16[256,1024]{1,0:T(8,128)(2,1)S(1)}, bf16[256,1024]{1,0:T(8,128)(2,1)S(1)}) custom-call(s32[1,128]{1,0:T(1,128)} %length_hbm.1, s32[1,128]{1,0:T(1,128)} %owner_hbm.1, s32[1,128]{1,0:T(1,128)} %cluster_hbm.1, s32[1,1024]{1,0:T(1,128)} %bitcast.13, bf16[1024,1024]{1,0:T(8,128)(2,1)} %frames_hbm.5), custom_call_target="tpu_custom_call" | custom-call | tf_op jit(solution)/shard_map/pool/pallas_call | solution.py:357
  3.9 7.3 %all-to-all-start = ((bf16[32,72,128]{2,1,0:T(8,128)(2,1)}), bf16[32,72,128]{2,1,0:T(8,128)(2,1)S(1)}, u32[]{:S(2)}, u32[]{:S(2)}) async-start(bf16[32,72,128]{2,1,0:T(8,128)(2,1)} %bitcast.1), calls=%async_computation | async-start | bytes 1179648 | tf_op jit(solution)/shard_map/all_to_all | solution.py:376
  11.3 2.6 %give.1 = (bf16[2,512,256]{2,1,0:T(8,128)(2,1)S(1)}, bf16[512,1024]{1,0:T(8,128)(2,1)S(1)}, bf16[512,256]{1,0:T(8,128)(2,1)S(1)}) custom-call(s32[1,1024]{1,0:T(1,128)} %bitcast.14, bf16[1024,1024]{1,0:T(8,128)(2,1)} %frames_hbm.5, bf16[256,1024]{1,0:T(8,128)(2,1)S(1)} %get-tuple-element.20.pooled_ref, bf16[256,1024]{1,0:T(8,128)(2,1)S(1)} %get-tuple-element.21.member_ref), custom_call_target="tpu_custom_call" | custom-call | flops 1073741824 | bytes 4194304 | tf_op jit(solution)/shard_map/give/pallas_call | solution.py:380
  13.9 0.3 collective-permute-start.3
  14.2 2.5 %keep.1 = f32[2,512,256]{2,1,0:T(8,128)S(1)} custom-call(bf16[1024,1024]{1,0:T(8,128)(2,1)} %frames_hbm.5, bf16[256,1024]{1,0:T(8,128)(2,1)S(1)} %get-tuple-element.20.pooled_ref, bf16[512,1024]{1,0:T(8,128)(2,1)S(1)} %get-tuple-element.22.matches_ref, bf16[512,256]{1,0:T(8,128)(2,1)S(1)} %get-tuple-element.23.counts_ref), custom_call_target="tpu_custom_call" | custom-call | flops 1073741824 | bytes 4194304 | tf_op jit(solution)/shard_map/keep/pallas_call | solution.py:399
  16.7 0.0 collective-permute-done.3
  16.7 0.1 fusion.5
  16.8 0.0 copy-start
  16.8 1.8 %collective-permute-start.4 = (bf16[512,256]{1,0:T(8,128)(2,1)S(1)}, bf16[512,256]{1,0:T(8,128)(2,1)S(1)}, u32[]{:S(2)}, u32[]{:S(2)}) collective-permute-start(bf16[512,256]{1,0:T(8,128)(2,1)S(1)} %fusion.5), channel_id=1, source_target_pairs={{0,2},{1,3},{2,0},{3,1},{4,6},{5,7},{6,4},{7,5},{8,10},{9,11},{10,... | collective-permute-start | bytes 786440 | tf_op jit(solution)/shard_map/ppermute | solution.py:351
  18.5 9.5 %all-to-all-done.got_ref = bf16[32,72,128]{2,1,0:T(8,128)(2,1)S(1)} async-done(((bf16[32,72,128]{2,1,0:T(8,128)(2,1)}), bf16[32,72,128]{2,1,0:T(8,128)(2,1)S(1)}, u32[]{:S(2)}, u32[]{:S(2)}) %all-to-all-start) | async-done | bytes 589856 | tf_op jit(solution)/shard_map/all_to_all | solution.py:376
  28.0 2.9 %owner.1 = (f32[512,256]{1,0:T(8,128)S(1)}, f32[16,128]{1,0:T(8,128)S(1)}, f32[64,256]{1,0:T(8,128)S(1)}, f32[64,256]{1,0:T(8,128)S(1)}, f32[64,256]{1,0:T(8,128)S(1)}, /*index=5*/f32[64,256]{1,0:T(8,128)S(1)}) custom-call(bf16[32,72,128]{2,1,0:T(8,128)(2,1)S(1)} %all-to-all-done.got_ref, bf16[256,1024]{1,0:T(8,128)(2,1)} %old_hbm.1), custom_call_target="tpu_custom_call" | custom-call | tf_op jit(solution)/shard_map/owner/pallas_call | solution.py:418
  30.9 0.0 collective-permute-done.4
  30.9 0.8 %fusion.4 = bf16[512,256]{1,0:T(8,128)(2,1)} fusion(f32[512,256]{1,0:T(8,128)S(1)} %get-tuple-element.19, f32[2,512,256]{2,1,0:T(8,128)S(1)} %keep.1, bf16[512,256]{1,0:T(8,128)(2,1)S(1)} %collective-permute-done.4, bf16[2,512,256]{2,1,0:T(8,128)(2,1)S(1)} %collective-permute-done.3), kind=kLoop, calls=%fused_computation.6 | loop fusion | flops 786432 | bytes 1835008 | tf_op jit(solution)/shard_map/convert_element_type | solution.py:435
  31.7 3.3 %all-to-all-start.1 = ((bf16[32,16,256]{2,1,0:T(8,128)(2,1)}), bf16[32,16,256]{2,1,0:T(8,128)(2,1)S(1)}, u32[]{:S(2)}, u32[]{:S(2)}) async-start(bf16[32,16,256]{2,1,0:T(8,128)(2,1)} %bitcast.4), calls=%async_computation.1 | async-start | bytes 524288 | tf_op jit(solution)/shard_map/all_to_all | solution.py:436
  35.0 0.3 collective-permute-start
  35.3 1.7 %collective-permute-start.1 = (f32[64,256]{1,0:T(8,128)S(1)}, f32[64,256]{1,0:T(8,128)S(1)}, u32[]{:S(2)}, u32[]{:S(2)}) collective-permute-start(f32[64,256]{1,0:T(8,128)S(1)} %get-tuple-element.17), channel_id=1, source_target_pairs={{0,2},{1,3},{2,0},{3,1},{4,6},{5,7},{6,4},{7,5},{8,10},{9,11},{10,... | collective-permute-start | bytes 196616 | tf_op jit(solution)/shard_map/ppermute | solution.py:351
  37.0 0.0 collective-permute-start.2
  37.0 0.0 collective-permute-done.beside_ref
  37.0 4.8 %collective-permute-done.1.across_ref = f32[64,256]{1,0:T(8,128)S(1)} collective-permute-done((f32[64,256]{1,0:T(8,128)S(1)}, f32[64,256]{1,0:T(8,128)S(1)}, u32[]{:S(2)}, u32[]{:S(2)}) %collective-permute-start.1) | collective-permute-done | bytes 65568 | tf_op jit(solution)/shard_map/ppermute | solution.py:351
  41.8 0.5 %collective-permute-done.2.diagonal_ref = f32[64,256]{1,0:T(8,128)S(1)} collective-permute-done((f32[64,256]{1,0:T(8,128)S(1)}, f32[64,256]{1,0:T(8,128)S(1)}, u32[]{:S(2)}, u32[]{:S(2)}) %collective-permute-start.2) | collective-permute-done | bytes 65568 | tf_op jit(solution)/shard_map/ppermute | solution.py:351
  42.3 0.7 %join.1 = f32[64,1024]{1,0:T(8,128)} custom-call(f32[64,256]{1,0:T(8,128)S(1)} %get-tuple-element.15.here_ref, f32[64,256]{1,0:T(8,128)S(1)} %collective-permute-done.beside_ref, f32[64,256]{1,0:T(8,128)S(1)} %collective-permute-done.1.across_ref, f32[64,256]{1,0:T(8,128)S(1)} %collective-permute-done.2.diagonal_ref), custom_call_target="tpu_custom_call" | custom-call | tf_op jit(solution)/shard_map/join/pallas_call | solution.py:437
  43.1 2.5 %all-to-all-done.1.got_ref = bf16[32,16,256]{2,1,0:T(8,128)(2,1)S(1)} async-done(((bf16[32,16,256]{2,1,0:T(8,128)(2,1)}), bf16[32,16,256]{2,1,0:T(8,128)(2,1)S(1)}, u32[]{:S(2)}, u32[]{:S(2)}) %all-to-all-start.1) | async-done | bytes 262176 | tf_op jit(solution)/shard_map/all_to_all | solution.py:436
  45.6 0.0 copy-done
  45.6 0.7 %finish.1 = f32[16,1024]{1,0:T(8,128)} custom-call(bf16[32,16,256]{2,1,0:T(8,128)(2,1)S(1)} %all-to-all-done.1.got_ref, f32[16,128]{1,0:T(8,128)S(1)} %get-tuple-element.25.count_ref, f32[16,1024]{1,0:T(8,128)S(1)} %copy-done), custom_call_target="tpu_custom_call" | custom-call | tf_op jit(solution)/shard_map/finish/pallas_call | solution.py:445
Async XLA Ops:
  3.9 24.1 %all-to-all-start = ((bf16[32,72,128]{2,1,0:T(8,128)(2,1)}), bf16[32,72,128]{2,1,0:T(8,128)(2,1)S(1)}, u32[]{:S(2)}, u32[]{:S(2)}) async-start(bf16[32,72,128]{2,1,0:T(8,128)(2,1)} %bitcast.1), calls=%async_computation | async-start | bytes 1179648 | tf_op jit(solution)/shard_map/all_to_all | solution.py:376
  13.9 2.8 %collective-permute-start.3 = (bf16[2,512,256]{2,1,0:T(8,128)(2,1)S(1)}, bf16[2,512,256]{2,1,0:T(8,128)(2,1)S(1)}, u32[]{:S(2)}, u32[]{:S(2)}) collective-permute-start(bf16[2,512,256]{2,1,0:T(8,128)(2,1)S(1)} %get-tuple-element.24), channel_id=1, source_target_pairs={{0,1},{1,0},{2,3},{3,2},{4,5},{5,4},{6,7},{7,6},{8,9},{9,8},{10,11... | collective-permute-start | bytes 1572872 | tf_op jit(solution)/shard_map/ppermute | solution.py:351
  16.8 28.8 %copy-start = (f32[16,1024]{1,0:T(8,128)S(1)}, f32[16,1024]{1,0:T(8,128)}, u32[]{:S(2)}) copy-start(f32[16,1024]{1,0:T(8,128)} %old_ref.1) | copy-start | bytes 196612
  16.8 14.1 %collective-permute-start.4 = (bf16[512,256]{1,0:T(8,128)(2,1)S(1)}, bf16[512,256]{1,0:T(8,128)(2,1)S(1)}, u32[]{:S(2)}, u32[]{:S(2)}) collective-permute-start(bf16[512,256]{1,0:T(8,128)(2,1)S(1)} %fusion.5), channel_id=1, source_target_pairs={{0,2},{1,3},{2,0},{3,1},{4,6},{5,7},{6,4},{7,5},{8,10},{9,11},{10,... | collective-permute-start | bytes 786440 | tf_op jit(solution)/shard_map/ppermute | solution.py:351
  31.7 13.9 %all-to-all-start.1 = ((bf16[32,16,256]{2,1,0:T(8,128)(2,1)}), bf16[32,16,256]{2,1,0:T(8,128)(2,1)S(1)}, u32[]{:S(2)}, u32[]{:S(2)}) async-start(bf16[32,16,256]{2,1,0:T(8,128)(2,1)} %bitcast.4), calls=%async_computation.1 | async-start | bytes 524288 | tf_op jit(solution)/shard_map/all_to_all | solution.py:436
  35.0 2.0 %collective-permute-start = (f32[64,256]{1,0:T(8,128)S(1)}, f32[64,256]{1,0:T(8,128)S(1)}, u32[]{:S(2)}, u32[]{:S(2)}) collective-permute-start(f32[64,256]{1,0:T(8,128)S(1)} %get-tuple-element.16), channel_id=1, source_target_pairs={{0,1},{1,0},{2,3},{3,2},{4,5},{5,4},{6,7},{7,6},{8,9},{9,8},{10,11... | collective-permute-start | bytes 196616 | tf_op jit(solution)/shard_map/ppermute | solution.py:351
  35.3 6.5 %collective-permute-start.1 = (f32[64,256]{1,0:T(8,128)S(1)}, f32[64,256]{1,0:T(8,128)S(1)}, u32[]{:S(2)}, u32[]{:S(2)}) collective-permute-start(f32[64,256]{1,0:T(8,128)S(1)} %get-tuple-element.17), channel_id=1, source_target_pairs={{0,2},{1,3},{2,0},{3,1},{4,6},{5,7},{6,4},{7,5},{8,10},{9,11},{10,... | collective-permute-start | bytes 196616 | tf_op jit(solution)/shard_map/ppermute | solution.py:351
  37.0 5.4 %collective-permute-start.2 = (f32[64,256]{1,0:T(8,128)S(1)}, f32[64,256]{1,0:T(8,128)S(1)}, u32[]{:S(2)}, u32[]{:S(2)}) collective-permute-start(f32[64,256]{1,0:T(8,128)S(1)} %get-tuple-element.18), channel_id=1, source_target_pairs={{0,3},{1,2},{2,1},{3,0},{4,7},{5,6},{6,5},{7,4},{8,11},{9,10},{10,... | collective-permute-start | bytes 196616 | tf_op jit(solution)/shard_map/ppermute | solution.py:351

commit v6 on v5

--- a/solution.py
+++ b/solution.py
@@ -232,12 +232,10 @@
     )
 
 
-def owner_kernel(sizes, got_ref, old_hbm, code_ref, count_ref, here_ref, beside_ref, across_ref, diagonal_ref, old_ref, new_ref, sems):
+def owner_kernel(sizes, got_ref, old_ref, code_ref, count_ref, here_ref, beside_ref, across_ref, diagonal_ref, new_ref):
     owners, cents, capacity, longest, code_total = sizes
     me = lax.axis_index("cent")
     clusters, share = old_ref.shape
-    columns = pl.ds(pl.multiple_of(me * share, share), share)
-    copies = fetch((old_hbm.at[:, columns],), (old_ref,), sems)
     half = longest // 2
     lane = iota((half, LANES), 1)
     segment = lane // capacity
@@ -270,7 +268,6 @@
     sums = dot(pick, rows)
     number = dot(pick, jnp.ones((rows.shape[0], LANES), bf16))
     number = jnp.concatenate([number] * (share // LANES), axis=1)
-    copies[0].wait()
     new = (sums + old_ref[...].astype(f32)) / (number + 1.0)
     new_ref[...] = new
     anchor = new.astype(bf16)
@@ -415,6 +412,8 @@
     )(stay(frames), pooled, matches, slot_counts)
     far = swap((keep[1] + near[1].astype(f32)).astype(bf16), 2)
     piece = jax.ShapeDtypeStruct((quarter, share), f32)
+    first = lax.axis_index("cent") * share
+    old_part = lax.dynamic_slice_in_dim(old_coarse, first, share, 1)
     sums, count, here, beside, across, diagonal = pl.pallas_call(
         functools.partial(owner_kernel, sizes),
         out_shape=(
@@ -422,16 +421,12 @@
             jax.ShapeDtypeStruct((part, LANES), f32),
         )
         + (piece,) * cents,
-        in_specs=[vmem, hbm],
+        in_specs=[vmem, vmem],
         out_specs=(vmem,) * (2 + cents),
-        scratch_shapes=[
-            pltpu.VMEM((clusters, share), bf16),
-            pltpu.VMEM((clusters, share), f32),
-            pltpu.SemaphoreType.DMA((1,)),
-        ],
+        scratch_shapes=[pltpu.VMEM((clusters, share), f32)],
         compiler_params=params,
         name="owner",
-    )(got, stay(old_coarse))
+    )(got, old_part)
     sums = (sums + (keep[0] + near[0].astype(f32) + far.astype(f32))).astype(bf16)
     last = lax.all_to_all(sums.reshape(devices, part, share), ("dp", "cent"), 0, 0, tiled=True)
     new_coarse = pl.pallas_call(

time: 46.6 us -> 45.6 us (0.979)
  Pallas kernels: 12.7 us -> 11.7 us
  other arithmetic: 0.87 us -> 1.56 us
  waiting for transfers between devices: 17.3 us -> 16.7 us
    pallas_call x1, Pallas kernels: 2.86 us -> 1.83 us  [summed_body(): pl.pallas_call(functools.partial(owner_kernel, sizes), out_shape=(jax.Sha...]
    convert_element_type x1, other arithmetic: 0.06 us -> 0.76 us  [summed_body(): far = swap((keep[1] + near[1].astype(f32)).astype(bf16), 2)]
    all_to_all x1, waiting for transfers between devices: 9.48 us -> 8.85 us  [summed_body(): lax.all_to_all(send.reshape(devices, chunk, share // 2), ('dp', 'cent'),...]
  transfers between devices with their start and end apart: 7 -> 7, of which waited for: 4 -> 4; matrix products, arithmetic and copies ran while one was open for 0% -> 2% of each run, Pallas kernels for 19% -> 17%
where the time goes in v6:
time: 45.6 us; the launch traced here: 45.3 us
  waiting for transfers between devices  16.7 us (37%)
  starting transfers between devices  14.6 us (32%)
  Pallas kernels  11.7 us (26%)
  other arithmetic  1.56 us (3%)
  between operations  0.71 us (2%)
    all_to_all x1, waiting for transfers between devices, summed_body(): lax.all_to_all(send.reshape(devices, chunk, share // 2), ('dp', 'cent'),...  8.85 us
    all_to_all x1, starting transfers between devices, summed_body(): lax.all_to_all(send.reshape(devices, chunk, share // 2), ('dp', 'cent'),...  7.3 us
    ppermute x5, waiting for transfers between devices, summed_body(): lax.ppermute(array, 'cent', [(index, index ^ bit) for index in range(cent...  5.35 us
    ppermute x5, starting transfers between devices, summed_body(): lax.ppermute(array, 'cent', [(index, index ^ bit) for index in range(cent...  4 us
    pallas_call x1, Pallas kernels, summed_body(): pl.pallas_call(functools.partial(pool_kernel, sizes), out_shape=(jax.Shap...  3.37 us
    all_to_all x1, starting transfers between devices, summed_body(): lax.all_to_all(sums.reshape(devices, part, share), ('dp', 'cent'), 0, 0,...  3.31 us
    pallas_call x1, Pallas kernels, summed_body(): pl.pallas_call(functools.partial(give_kernel, sizes), out_shape=(jax.Shap...  2.62 us
    all_to_all x1, waiting for transfers between devices, summed_body(): lax.all_to_all(sums.reshape(devices, part, share), ('dp', 'cent'), 0, 0,...  2.52 us
  transfers between devices with their start and end apart: 7, of which 4 were waited for; matrix products, arithmetic and copies ran while one was open for 2% of the time, Pallas kernels for 17%

profile of v6, /device:TPU:0, one launch (start us, length us, event | category | flops | bytes accessed | tf_op | source)
XLA Modules:
  0.0 45.3 jit_solution(18108964689145015248)
XLA Ops:
  0.6 0.0 copy-start
  0.6 3.4 %pool.1 = (bf16[8,4,72,128]{3,2,1,0:T(8,128)(2,1)}, bf16[256,1024]{1,0:T(8,128)(2,1)S(1)}, bf16[256,1024]{1,0:T(8,128)(2,1)S(1)}) custom-call(s32[1,128]{1,0:T(1,128)} %length_hbm.1, s32[1,128]{1,0:T(1,128)} %owner_hbm.1, s32[1,128]{1,0:T(1,128)} %cluster_hbm.1, s32[1,1024]{1,0:T(1,128)} %bitcast.13, bf16[1024,1024]{1,0:T(8,128)(2,1)} %frames_hbm.5), custom_call_target="tpu_custom_call" | custom-call | tf_op jit(solution)/shard_map/pool/pallas_call | solution.py:354
  4.0 7.3 %all-to-all-start = ((bf16[32,72,128]{2,1,0:T(8,128)(2,1)}), bf16[32,72,128]{2,1,0:T(8,128)(2,1)S(1)}, u32[]{:S(2)}, u32[]{:S(2)}) async-start(bf16[32,72,128]{2,1,0:T(8,128)(2,1)} %bitcast.1), calls=%async_computation | async-start | bytes 1179648 | tf_op jit(solution)/shard_map/all_to_all | solution.py:373
  11.3 2.6 %give.1 = (bf16[2,512,256]{2,1,0:T(8,128)(2,1)S(1)}, bf16[512,1024]{1,0:T(8,128)(2,1)S(1)}, bf16[512,256]{1,0:T(8,128)(2,1)S(1)}) custom-call(s32[1,1024]{1,0:T(1,128)} %bitcast.14, bf16[1024,1024]{1,0:T(8,128)(2,1)} %frames_hbm.5, bf16[256,1024]{1,0:T(8,128)(2,1)S(1)} %get-tuple-element.20.pooled_ref, bf16[256,1024]{1,0:T(8,128)(2,1)S(1)} %get-tuple-element.21.member_ref), custom_call_target="tpu_custom_call" | custom-call | flops 1073741824 | bytes 4194304 | tf_op jit(solution)/shard_map/give/pallas_call | solution.py:377
  14.0 0.3 collective-permute-start.3
  14.3 2.5 %keep.1 = f32[2,512,256]{2,1,0:T(8,128)S(1)} custom-call(bf16[1024,1024]{1,0:T(8,128)(2,1)} %frames_hbm.5, bf16[256,1024]{1,0:T(8,128)(2,1)S(1)} %get-tuple-element.20.pooled_ref, bf16[512,1024]{1,0:T(8,128)(2,1)S(1)} %get-tuple-element.22.matches_ref, bf16[512,256]{1,0:T(8,128)(2,1)S(1)} %get-tuple-element.23.counts_ref), custom_call_target="tpu_custom_call" | custom-call | flops 1073741824 | bytes 4194304 | tf_op jit(solution)/shard_map/keep/pallas_call | solution.py:396
  16.8 0.0 collective-permute-done.3
  16.8 0.8 %fusion.5 = bf16[512,256]{1,0:T(8,128)(2,1)} fusion(f32[2,512,256]{2,1,0:T(8,128)S(1)} %keep.1, bf16[2,512,256]{2,1,0:T(8,128)(2,1)S(1)} %collective-permute-done.3), kind=kLoop, calls=%fused_computation.7 | loop fusion | flops 393216 | bytes 1048576 | tf_op jit(solution)/shard_map/convert_element_type | solution.py:413
  17.5 0.0 copy-start.1
  17.5 1.7 %collective-permute-start.4 = (bf16[512,256]{1,0:T(8,128)(2,1)}, bf16[512,256]{1,0:T(8,128)(2,1)S(1)}, u32[]{:S(2)}, u32[]{:S(2)}) collective-permute-start(bf16[512,256]{1,0:T(8,128)(2,1)} %fusion.5), channel_id=1, source_target_pairs={{0,2},{1,3},{2,0},{3,1},{4,6},{5,7},{6,4},{7,5},{8,10},{9,11},{10,... | collective-permute-start | bytes 786440 | tf_op jit(solution)/shard_map/ppermute | solution.py:348
  19.2 0.0 copy-done
  19.2 8.8 %all-to-all-done.got_ref = bf16[32,72,128]{2,1,0:T(8,128)(2,1)S(1)} async-done(((bf16[32,72,128]{2,1,0:T(8,128)(2,1)}), bf16[32,72,128]{2,1,0:T(8,128)(2,1)S(1)}, u32[]{:S(2)}, u32[]{:S(2)}) %all-to-all-start) | async-done | bytes 589856 | tf_op jit(solution)/shard_map/all_to_all | solution.py:373
  28.1 1.8 %owner.1 = (f32[512,256]{1,0:T(8,128)S(1)}, f32[16,128]{1,0:T(8,128)S(1)}, f32[64,256]{1,0:T(8,128)S(1)}, f32[64,256]{1,0:T(8,128)S(1)}, f32[64,256]{1,0:T(8,128)S(1)}, /*index=5*/f32[64,256]{1,0:T(8,128)S(1)}) custom-call(bf16[32,72,128]{2,1,0:T(8,128)(2,1)S(1)} %all-to-all-done.got_ref, bf16[256,256]{1,0:T(8,128)(2,1)S(1)} %constant_dynamic-slice_fusion.old_ref), custom_call_target="tpu_custom_call" | custom-call | tf_op jit(solution)/shard_map/owner/pallas_call | solution.py:417
  29.9 0.0 collective-permute-done.4
  29.9 0.8 %fusion.4 = bf16[512,256]{1,0:T(8,128)(2,1)} fusion(f32[512,256]{1,0:T(8,128)S(1)} %get-tuple-element.19, f32[2,512,256]{2,1,0:T(8,128)S(1)} %keep.1, bf16[512,256]{1,0:T(8,128)(2,1)S(1)} %collective-permute-done.4, bf16[2,512,256]{2,1,0:T(8,128)(2,1)S(1)} %collective-permute-done.3), kind=kLoop, calls=%fused_computation.6 | loop fusion | flops 786432 | bytes 1835008 | tf_op jit(solution)/shard_map/convert_element_type | solution.py:430
  30.7 3.3 %all-to-all-start.1 = ((bf16[32,16,256]{2,1,0:T(8,128)(2,1)}), bf16[32,16,256]{2,1,0:T(8,128)(2,1)S(1)}, u32[]{:S(2)}, u32[]{:S(2)}) async-start(bf16[32,16,256]{2,1,0:T(8,128)(2,1)} %bitcast.4), calls=%async_computation.1 | async-start | bytes 524288 | tf_op jit(solution)/shard_map/all_to_all | solution.py:431
  34.0 0.3 collective-permute-start
  34.4 1.7 %collective-permute-start.1 = (f32[64,256]{1,0:T(8,128)S(1)}, f32[64,256]{1,0:T(8,128)S(1)}, u32[]{:S(2)}, u32[]{:S(2)}) collective-permute-start(f32[64,256]{1,0:T(8,128)S(1)} %get-tuple-element.17), channel_id=1, source_target_pairs={{0,2},{1,3},{2,0},{3,1},{4,6},{5,7},{6,4},{7,5},{8,10},{9,11},{10,... | collective-permute-start | bytes 196616 | tf_op jit(solution)/shard_map/ppermute | solution.py:348
  36.0 0.0 collective-permute-start.2
  36.1 0.0 collective-permute-done.beside_ref
  36.1 4.8 %collective-permute-done.1.across_ref = f32[64,256]{1,0:T(8,128)S(1)} collective-permute-done((f32[64,256]{1,0:T(8,128)S(1)}, f32[64,256]{1,0:T(8,128)S(1)}, u32[]{:S(2)}, u32[]{:S(2)}) %collective-permute-start.1) | collective-permute-done | bytes 65568 | tf_op jit(solution)/shard_map/ppermute | solution.py:348
  40.9 0.5 %collective-permute-done.2.diagonal_ref = f32[64,256]{1,0:T(8,128)S(1)} collective-permute-done((f32[64,256]{1,0:T(8,128)S(1)}, f32[64,256]{1,0:T(8,128)S(1)}, u32[]{:S(2)}, u32[]{:S(2)}) %collective-permute-start.2) | collective-permute-done | bytes 65568 | tf_op jit(solution)/shard_map/ppermute | solution.py:348
  41.4 0.7 %join.1 = f32[64,1024]{1,0:T(8,128)} custom-call(f32[64,256]{1,0:T(8,128)S(1)} %get-tuple-element.15.here_ref, f32[64,256]{1,0:T(8,128)S(1)} %collective-permute-done.beside_ref, f32[64,256]{1,0:T(8,128)S(1)} %collective-permute-done.1.across_ref, f32[64,256]{1,0:T(8,128)S(1)} %collective-permute-done.2.diagonal_ref), custom_call_target="tpu_custom_call" | custom-call | tf_op jit(solution)/shard_map/join/pallas_call | solution.py:432
  42.1 2.5 %all-to-all-done.1.got_ref = bf16[32,16,256]{2,1,0:T(8,128)(2,1)S(1)} async-done(((bf16[32,16,256]{2,1,0:T(8,128)(2,1)}), bf16[32,16,256]{2,1,0:T(8,128)(2,1)S(1)}, u32[]{:S(2)}, u32[]{:S(2)}) %all-to-all-start.1) | async-done | bytes 262176 | tf_op jit(solution)/shard_map/all_to_all | solution.py:431
  44.6 0.0 copy-done.1
  44.6 0.7 %finish.1 = f32[16,1024]{1,0:T(8,128)} custom-call(bf16[32,16,256]{2,1,0:T(8,128)(2,1)S(1)} %all-to-all-done.1.got_ref, f32[16,128]{1,0:T(8,128)S(1)} %get-tuple-element.25.count_ref, f32[16,1024]{1,0:T(8,128)S(1)} %copy-done.1), custom_call_target="tpu_custom_call" | custom-call | tf_op jit(solution)/shard_map/finish/pallas_call | solution.py:440
  (1 shorter events, 0.0 us)
Async XLA Ops:
  0.6 18.6 %copy-start = (bf16[256,1024]{1,0:T(8,128)(2,1)S(1)}, bf16[256,1024]{1,0:T(8,128)(2,1)}, u32[]{:S(2)}) copy-start(bf16[256,1024]{1,0:T(8,128)(2,1)} %param.12) | copy-start | bytes 1572868
  4.0 24.1 %all-to-all-start = ((bf16[32,72,128]{2,1,0:T(8,128)(2,1)}), bf16[32,72,128]{2,1,0:T(8,128)(2,1)S(1)}, u32[]{:S(2)}, u32[]{:S(2)}) async-start(bf16[32,72,128]{2,1,0:T(8,128)(2,1)} %bitcast.1), calls=%async_computation | async-start | bytes 1179648 | tf_op jit(solution)/shard_map/all_to_all | solution.py:373
  14.0 2.8 %collective-permute-start.3 = (bf16[2,512,256]{2,1,0:T(8,128)(2,1)S(1)}, bf16[2,512,256]{2,1,0:T(8,128)(2,1)S(1)}, u32[]{:S(2)}, u32[]{:S(2)}) collective-permute-start(bf16[2,512,256]{2,1,0:T(8,128)(2,1)S(1)} %get-tuple-element.24), channel_id=1, source_target_pairs={{0,1},{1,0},{2,3},{3,2},{4,5},{5,4},{6,7},{7,6},{8,9},{9,8},{10,11... | collective-permute-start | bytes 1572872 | tf_op jit(solution)/shard_map/ppermute | solution.py:348
  17.5 27.1 %copy-start.1 = (f32[16,1024]{1,0:T(8,128)S(1)}, f32[16,1024]{1,0:T(8,128)}, u32[]{:S(2)}) copy-start(f32[16,1024]{1,0:T(8,128)} %old_ref.1) | copy-start | bytes 196612
  17.5 12.4 %collective-permute-start.4 = (bf16[512,256]{1,0:T(8,128)(2,1)}, bf16[512,256]{1,0:T(8,128)(2,1)S(1)}, u32[]{:S(2)}, u32[]{:S(2)}) collective-permute-start(bf16[512,256]{1,0:T(8,128)(2,1)} %fusion.5), channel_id=1, source_target_pairs={{0,2},{1,3},{2,0},{3,1},{4,6},{5,7},{6,4},{7,5},{8,10},{9,11},{10,... | collective-permute-start | bytes 786440 | tf_op jit(solution)/shard_map/ppermute | solution.py:348
  30.7 13.9 %all-to-all-start.1 = ((bf16[32,16,256]{2,1,0:T(8,128)(2,1)}), bf16[32,16,256]{2,1,0:T(8,128)(2,1)S(1)}, u32[]{:S(2)}, u32[]{:S(2)}) async-start(bf16[32,16,256]{2,1,0:T(8,128)(2,1)} %bitcast.4), calls=%async_computation.1 | async-start | bytes 524288 | tf_op jit(solution)/shard_map/all_to_all | solution.py:431
  34.0 2.0 %collective-permute-start = (f32[64,256]{1,0:T(8,128)S(1)}, f32[64,256]{1,0:T(8,128)S(1)}, u32[]{:S(2)}, u32[]{:S(2)}) collective-permute-start(f32[64,256]{1,0:T(8,128)S(1)} %get-tuple-element.16), channel_id=1, source_target_pairs={{0,1},{1,0},{2,3},{3,2},{4,5},{5,4},{6,7},{7,6},{8,9},{9,8},{10,11... | collective-permute-start | bytes 196616 | tf_op jit(solution)/shard_map/ppermute | solution.py:348
  34.4 6.5 %collective-permute-start.1 = (f32[64,256]{1,0:T(8,128)S(1)}, f32[64,256]{1,0:T(8,128)S(1)}, u32[]{:S(2)}, u32[]{:S(2)}) collective-permute-start(f32[64,256]{1,0:T(8,128)S(1)} %get-tuple-element.17), channel_id=1, source_target_pairs={{0,2},{1,3},{2,0},{3,1},{4,6},{5,7},{6,4},{7,5},{8,10},{9,11},{10,... | collective-permute-start | bytes 196616 | tf_op jit(solution)/shard_map/ppermute | solution.py:348
  36.0 5.4 %collective-permute-start.2 = (f32[64,256]{1,0:T(8,128)S(1)}, f32[64,256]{1,0:T(8,128)S(1)}, u32[]{:S(2)}, u32[]{:S(2)}) collective-permute-start(f32[64,256]{1,0:T(8,128)S(1)} %get-tuple-element.18), channel_id=1, source_target_pairs={{0,3},{1,2},{2,1},{3,0},{4,7},{5,6},{6,5},{7,4},{8,11},{9,10},{10,... | collective-permute-start | bytes 196616 | tf_op jit(solution)/shard_map/ppermute | solution.py:348

commit v7 on v6

--- a/solution.py
+++ b/solution.py
@@ -85,7 +85,8 @@
     frames_hbm,
     send_hbm,
     pooled_ref,
-    member_ref,
+    matches_ref,
+    counts_ref,
     *scratch,
 ):
     owners, cents, capacity, longest, code_total = sizes
@@ -102,7 +103,6 @@
     video_of_slot, first, length, member = member_of_slots(
         length_ref, owner_ref, owners, capacity, frame_count
     )
-    member_ref[...] = member
     code = (code_ref[...] - EXACT).astype(f32)
     shifted = pltpu.roll(
         jnp.broadcast_to(code, (longest, frame_count)),
@@ -172,35 +172,27 @@
             pltpu.make_async_copy(send_ref.at[:, cent], send_hbm.at[:, cent], out_sems.at[cent])
         )
         out[-1].start()
+    matches_ref[...] = code_matches(code_ref, code_total)
+    counts_ref[...] = dot_rows(matches_ref[...], member).astype(bf16)
     for copy in out:
         copy.wait()
 
 
 def give_kernel(
-    sizes,
-    code_hbm,
-    frames_hbm,
-    pooled_ref,
-    member_ref,
-    give_ref,
-    matches_ref,
-    counts_ref,
-    code_ref,
-    frames_ref,
-    sems,
+    sizes, frames_hbm, pooled_ref, matches_ref, counts_ref, give_ref, frames_ref, sems
 ):
     owners, cents, capacity, longest, code_total = sizes
-    copies = fetch((code_hbm, frames_hbm), (code_ref, frames_ref), sems)
     me = lax.axis_index("cent")
     share = frames_hbm.shape[1] // cents
+    copies = fetch((frames_hbm,), (frames_ref,), sems)
+    spans = [
+        pl.ds(pl.multiple_of((me ^ step) * share, share), share) for step in range(1, cents, 2)
+    ]
+    removed = [dot(counts_ref[...], pooled_ref[:, span]) for span in spans]
     copies[0].wait()
-    matches_ref[...] = code_matches(code_ref, code_total)
-    counts_ref[...] = dot_rows(matches_ref[...], member_ref[...]).astype(bf16)
-    copies[1].wait()
-    for step in range(1, cents, 2):
-        columns = pl.ds(pl.multiple_of((me ^ step) * share, share), share)
-        sums = dot(matches_ref[...], frames_ref[:, columns])
-        give_ref[step // 2] = (sums - dot(counts_ref[...], pooled_ref[:, columns])).astype(bf16)
+    for at, span in enumerate(spans):
+        sums = dot(matches_ref[...], frames_ref[:, span])
+        give_ref[at] = (sums - removed[at]).astype(bf16)
 
 
 def keep_kernel(sizes, frames_hbm, pooled_ref, matches_ref, counts_ref, keep_ref, frames_ref, sems):
@@ -351,15 +343,16 @@
     row = lambda length: pltpu.VMEM((1, length), jnp.int32)
     frames_scratch = [row(frame_count), pltpu.VMEM((frame_count, features), bf16)]
     quarter = clusters // cents
-    send, pooled, member = pl.pallas_call(
+    send, pooled, matches, slot_counts = pl.pallas_call(
         functools.partial(pool_kernel, sizes),
         out_shape=(
             jax.ShapeDtypeStruct((owners, cents, chunk, share // 2), bf16),
             jax.ShapeDtypeStruct((slots, features), bf16),
-            jax.ShapeDtypeStruct((slots, frame_count), bf16),
+            jax.ShapeDtypeStruct((code_total, frame_count), bf16),
+            jax.ShapeDtypeStruct((code_total, slots), bf16),
         ),
         in_specs=[hbm] * 5,
-        out_specs=(hbm, vmem, vmem),
+        out_specs=(hbm, vmem, vmem, vmem),
         scratch_shapes=[row(videos)] * 3
         + frames_scratch
         + [
@@ -374,16 +367,12 @@
         send.reshape(devices, chunk, share // 2), ("dp", "cent"), 0, 0, tiled=True
     )
     table = (cents // 2, code_total, share)
-    give, matches, slot_counts = pl.pallas_call(
+    give = pl.pallas_call(
         functools.partial(give_kernel, sizes),
-        out_shape=(
-            jax.ShapeDtypeStruct(table, bf16),
-            jax.ShapeDtypeStruct((code_total, frame_count), bf16),
-            jax.ShapeDtypeStruct((code_total, slots), bf16),
-        ),
-        in_specs=[hbm] * 2 + [vmem] * 2,
-        out_specs=(vmem,) * 3,
-        scratch_shapes=frames_scratch + [pltpu.SemaphoreType.DMA((2,))],
+        out_shape=jax.ShapeDtypeStruct(table, bf16),
+        in_specs=[hbm] + [vmem] * 3,
+        out_specs=vmem,
+        scratch_shapes=[frames_scratch[1], pltpu.SemaphoreType.DMA((1,))],
         compiler_params=params,
         cost_estimate=pl.CostEstimate(
             flops=2 * code_total * frame_count * features,
@@ -391,7 +380,7 @@
             transcendentals=0,
         ),
         name="give",
-    )(stay(frame_code), stay(frames), pooled, member)
+    )(stay(frames), pooled, matches, slot_counts)
     near = swap(give, 1)
     keep = pl.pallas_call(
         functools.partial(keep_kernel, sizes),
@@ -410,7 +399,10 @@
         ),
         name="keep",
     )(stay(frames), pooled, matches, slot_counts)
-    far = swap((keep[1] + near[1].astype(f32)).astype(bf16), 2)
+    base, cross = lax.optimization_barrier(
+        (keep[0] + near[0].astype(f32), (keep[1] + near[1].astype(f32)).astype(bf16))
+    )
+    far = swap(cross, 2)
     piece = jax.ShapeDtypeStruct((quarter, share), f32)
     first = lax.axis_index("cent") * share
     old_part = lax.dynamic_slice_in_dim(old_coarse, first, share, 1)
@@ -427,7 +419,7 @@
         compiler_params=params,
         name="owner",
     )(got, old_part)
-    sums = (sums + (keep[0] + near[0].astype(f32) + far.astype(f32))).astype(bf16)
+    sums = (sums + (base + far.astype(f32))).astype(bf16)
     last = lax.all_to_all(sums.reshape(devices, part, share), ("dp", "cent"), 0, 0, tiled=True)
     new_coarse = pl.pallas_call(
         join_kernel,

time: 45.6 us -> 45.7 us (level)
  waiting for transfers between devices: 16.7 us -> 17.4 us
  other arithmetic: 1.56 us -> 0.89 us
    all_to_all x1, waiting for transfers between devices: 8.85 us -> 9.57 us  [summed_body(): lax.all_to_all(send.reshape(devices, chunk, share // 2), ('dp', 'cent'),...]
    convert_element_type x2, other arithmetic: 1.56 us -> 0.89 us  [the longest x1 0.78 us: summed_body(): sums = (sums + (base + far.astype(f32))).astype(bf16)]
  transfers between devices with their start and end apart: 7 -> 7, of which waited for: 4 -> 4; matrix products, arithmetic and copies ran while one was open for 2% -> 0% of each run, Pallas kernels for 17% -> 17%
where the time goes in v7:
time: 45.7 us; the launch traced here: 45.3 us
  waiting for transfers between devices  17.4 us (38%)
  starting transfers between devices  14.6 us (32%)
  Pallas kernels  11.6 us (25%)
  other arithmetic  0.89 us (2%)
  between operations  0.73 us (2%)
    all_to_all x1, waiting for transfers between devices, summed_body(): lax.all_to_all(send.reshape(devices, chunk, share // 2), ('dp', 'cent'),...  9.57 us
    all_to_all x1, starting transfers between devices, summed_body(): lax.all_to_all(send.reshape(devices, chunk, share // 2), ('dp', 'cent'),...  7.3 us
    ppermute x5, waiting for transfers between devices, summed_body(): lax.ppermute(array, 'cent', [(index, index ^ bit) for index in range(cent...  5.35 us
    ppermute x5, starting transfers between devices, summed_body(): lax.ppermute(array, 'cent', [(index, index ^ bit) for index in range(cent...  4.07 us
    pallas_call x1, Pallas kernels, summed_body(): pl.pallas_call(functools.partial(pool_kernel, sizes), out_shape=(jax.Shap...  3.44 us
    all_to_all x1, starting transfers between devices, summed_body(): lax.all_to_all(sums.reshape(devices, part, share), ('dp', 'cent'), 0, 0,...  3.27 us
    all_to_all x1, waiting for transfers between devices, summed_body(): lax.all_to_all(sums.reshape(devices, part, share), ('dp', 'cent'), 0, 0,...  2.52 us
    pallas_call x1, Pallas kernels, summed_body(): pl.pallas_call(functools.partial(keep_kernel, sizes), out_shape=jax.Shape...  2.47 us
  transfers between devices with their start and end apart: 7, of which 4 were waited for; matrix products, arithmetic and copies ran while one was open for 0% of the time, Pallas kernels for 17%

profile of v7, /device:TPU:0, one launch (start us, length us, event | category | flops | bytes accessed | tf_op | source)
XLA Modules:
  0.0 45.3 jit_solution(1864714482121676100)
XLA Ops:
  0.6 0.0 copy-start
  0.6 3.4 %pool.1 = (bf16[8,4,72,128]{3,2,1,0:T(8,128)(2,1)}, bf16[256,1024]{1,0:T(8,128)(2,1)S(1)}, bf16[512,1024]{1,0:T(8,128)(2,1)S(1)}, bf16[512,256]{1,0:T(8,128)(2,1)S(1)}) custom-call(s32[1,128]{1,0:T(1,128)} %length_hbm.1, s32[1,128]{1,0:T(1,128)} %owner_hbm.1, s32[1,128]{1,0:T(1,128)} %cluster_hbm.1, s32[1,1024]{1,0:T(1,128)} %bitcast.7, ...), custom_call_target="tpu_custom_call" | custom-call | tf_op jit(solution)/shard_map/pool/pallas_call | solution.py:346
  4.1 7.3 %all-to-all-start = ((bf16[32,72,128]{2,1,0:T(8,128)(2,1)}), bf16[32,72,128]{2,1,0:T(8,128)(2,1)S(1)}, u32[]{:S(2)}, u32[]{:S(2)}) async-start(bf16[32,72,128]{2,1,0:T(8,128)(2,1)} %bitcast.1), calls=%async_computation | async-start | bytes 1179648 | tf_op jit(solution)/shard_map/all_to_all | solution.py:366
  11.4 2.5 %give.1 = bf16[2,512,256]{2,1,0:T(8,128)(2,1)S(1)} custom-call(bf16[1024,1024]{1,0:T(8,128)(2,1)} %frames_hbm.5, bf16[256,1024]{1,0:T(8,128)(2,1)S(1)} %get-tuple-element.20.pooled_ref, bf16[512,1024]{1,0:T(8,128)(2,1)S(1)} %get-tuple-element.21.matches_ref, bf16[512,256]{1,0:T(8,128)(2,1)S(1)} %get-tuple-element.22.counts_ref), custom_call_target="tpu_custom_call" | custom-call | flops 1073741824 | bytes 4194304 | tf_op jit(solution)/shard_map/give/pallas_call | solution.py:370
  13.9 0.3 collective-permute-start.3
  14.2 2.5 %keep.1 = f32[2,512,256]{2,1,0:T(8,128)S(1)} custom-call(bf16[1024,1024]{1,0:T(8,128)(2,1)} %frames_hbm.5, bf16[256,1024]{1,0:T(8,128)(2,1)S(1)} %get-tuple-element.20.pooled_ref, bf16[512,1024]{1,0:T(8,128)(2,1)S(1)} %get-tuple-element.21.matches_ref, bf16[512,256]{1,0:T(8,128)(2,1)S(1)} %get-tuple-element.22.counts_ref), custom_call_target="tpu_custom_call" | custom-call | flops 1073741824 | bytes 4194304 | tf_op jit(solution)/shard_map/keep/pallas_call | solution.py:385
  16.7 0.0 collective-permute-done.3
  16.7 0.1 fusion.2
  16.8 0.0 copy-start.1
  16.8 1.8 %collective-permute-start.4 = (bf16[512,256]{1,0:T(8,128)(2,1)S(1)}, bf16[512,256]{1,0:T(8,128)(2,1)S(1)}, u32[]{:S(2)}, u32[]{:S(2)}) collective-permute-start(bf16[512,256]{1,0:T(8,128)(2,1)S(1)} %get-tuple-element.24), channel_id=1, source_target_pairs={{0,2},{1,3},{2,0},{3,1},{4,6},{5,7},{6,4},{7,5},{8,10},{9,11},{10,... | collective-permute-start | bytes 786440 | tf_op jit(solution)/shard_map/ppermute | solution.py:340
  18.6 0.0 copy-done
  18.6 9.6 %all-to-all-done.got_ref = bf16[32,72,128]{2,1,0:T(8,128)(2,1)S(1)} async-done(((bf16[32,72,128]{2,1,0:T(8,128)(2,1)}), bf16[32,72,128]{2,1,0:T(8,128)(2,1)S(1)}, u32[]{:S(2)}, u32[]{:S(2)}) %all-to-all-start) | async-done | bytes 589856 | tf_op jit(solution)/shard_map/all_to_all | solution.py:366
  28.2 1.8 %owner.1 = (f32[512,256]{1,0:T(8,128)S(1)}, f32[16,128]{1,0:T(8,128)S(1)}, f32[64,256]{1,0:T(8,128)S(1)}, f32[64,256]{1,0:T(8,128)S(1)}, f32[64,256]{1,0:T(8,128)S(1)}, /*index=5*/f32[64,256]{1,0:T(8,128)S(1)}) custom-call(bf16[32,72,128]{2,1,0:T(8,128)(2,1)S(1)} %all-to-all-done.got_ref, bf16[256,256]{1,0:T(8,128)(2,1)S(1)} %constant_dynamic-slice_fusion.old_ref), custom_call_target="tpu_custom_call" | custom-call | tf_op jit(solution)/shard_map/owner/pallas_call | solution.py:409
  30.0 0.0 collective-permute-done.4
  30.0 0.8 %add_convert_fusion = bf16[512,256]{1,0:T(8,128)(2,1)} fusion(f32[512,256]{1,0:T(8,128)S(1)} %get-tuple-element.19, f32[512,256]{1,0:T(8,128)S(1)} %get-tuple-element.23, bf16[512,256]{1,0:T(8,128)(2,1)S(1)} %collective-permute-done.4), kind=kLoop, calls=%fused_computation.4 | loop fusion | flops 524288 | bytes 1572864 | tf_op jit(solution)/shard_map/convert_element_type | solution.py:422
  30.8 3.3 %all-to-all-start.1 = ((bf16[32,16,256]{2,1,0:T(8,128)(2,1)}), bf16[32,16,256]{2,1,0:T(8,128)(2,1)S(1)}, u32[]{:S(2)}, u32[]{:S(2)}) async-start(bf16[32,16,256]{2,1,0:T(8,128)(2,1)} %bitcast.4), calls=%async_computation.1 | async-start | bytes 524288 | tf_op jit(solution)/shard_map/all_to_all | solution.py:423
  34.1 0.3 collective-permute-start
  34.4 1.7 %collective-permute-start.1 = (f32[64,256]{1,0:T(8,128)S(1)}, f32[64,256]{1,0:T(8,128)S(1)}, u32[]{:S(2)}, u32[]{:S(2)}) collective-permute-start(f32[64,256]{1,0:T(8,128)S(1)} %get-tuple-element.17), channel_id=1, source_target_pairs={{0,2},{1,3},{2,0},{3,1},{4,6},{5,7},{6,4},{7,5},{8,10},{9,11},{10,... | collective-permute-start | bytes 196616 | tf_op jit(solution)/shard_map/ppermute | solution.py:340
  36.1 0.0 collective-permute-start.2
  36.1 0.0 collective-permute-done.beside_ref
  36.1 4.8 %collective-permute-done.1.across_ref = f32[64,256]{1,0:T(8,128)S(1)} collective-permute-done((f32[64,256]{1,0:T(8,128)S(1)}, f32[64,256]{1,0:T(8,128)S(1)}, u32[]{:S(2)}, u32[]{:S(2)}) %collective-permute-start.1) | collective-permute-done | bytes 65568 | tf_op jit(solution)/shard_map/ppermute | solution.py:340
  40.9 0.5 %collective-permute-done.2.diagonal_ref = f32[64,256]{1,0:T(8,128)S(1)} collective-permute-done((f32[64,256]{1,0:T(8,128)S(1)}, f32[64,256]{1,0:T(8,128)S(1)}, u32[]{:S(2)}, u32[]{:S(2)}) %collective-permute-start.2) | collective-permute-done | bytes 65568 | tf_op jit(solution)/shard_map/ppermute | solution.py:340
  41.4 0.7 %join.1 = f32[64,1024]{1,0:T(8,128)} custom-call(f32[64,256]{1,0:T(8,128)S(1)} %get-tuple-element.15.here_ref, f32[64,256]{1,0:T(8,128)S(1)} %collective-permute-done.beside_ref, f32[64,256]{1,0:T(8,128)S(1)} %collective-permute-done.1.across_ref, f32[64,256]{1,0:T(8,128)S(1)} %collective-permute-done.2.diagonal_ref), custom_call_target="tpu_custom_call" | custom-call | tf_op jit(solution)/shard_map/join/pallas_call | solution.py:424
  42.1 2.5 %all-to-all-done.1.got_ref = bf16[32,16,256]{2,1,0:T(8,128)(2,1)S(1)} async-done(((bf16[32,16,256]{2,1,0:T(8,128)(2,1)}), bf16[32,16,256]{2,1,0:T(8,128)(2,1)S(1)}, u32[]{:S(2)}, u32[]{:S(2)}) %all-to-all-start.1) | async-done | bytes 262176 | tf_op jit(solution)/shard_map/all_to_all | solution.py:423
  44.7 0.0 copy-done.1
  44.7 0.7 %finish.1 = f32[16,1024]{1,0:T(8,128)} custom-call(bf16[32,16,256]{2,1,0:T(8,128)(2,1)S(1)} %all-to-all-done.1.got_ref, f32[16,128]{1,0:T(8,128)S(1)} %get-tuple-element.25.count_ref, f32[16,1024]{1,0:T(8,128)S(1)} %copy-done.1), custom_call_target="tpu_custom_call" | custom-call | tf_op jit(solution)/shard_map/finish/pallas_call | solution.py:432
  (1 shorter events, 0.0 us)
Async XLA Ops:
  0.6 17.9 %copy-start = (bf16[256,1024]{1,0:T(8,128)(2,1)S(1)}, bf16[256,1024]{1,0:T(8,128)(2,1)}, u32[]{:S(2)}) copy-start(bf16[256,1024]{1,0:T(8,128)(2,1)} %param.12) | copy-start | bytes 1572868
  4.1 24.1 %all-to-all-start = ((bf16[32,72,128]{2,1,0:T(8,128)(2,1)}), bf16[32,72,128]{2,1,0:T(8,128)(2,1)S(1)}, u32[]{:S(2)}, u32[]{:S(2)}) async-start(bf16[32,72,128]{2,1,0:T(8,128)(2,1)} %bitcast.1), calls=%async_computation | async-start | bytes 1179648 | tf_op jit(solution)/shard_map/all_to_all | solution.py:366
  13.9 2.8 %collective-permute-start.3 = (bf16[2,512,256]{2,1,0:T(8,128)(2,1)S(1)}, bf16[2,512,256]{2,1,0:T(8,128)(2,1)S(1)}, u32[]{:S(2)}, u32[]{:S(2)}) collective-permute-start(bf16[2,512,256]{2,1,0:T(8,128)(2,1)S(1)} %give.1), channel_id=1, source_target_pairs={{0,1},{1,0},{2,3},{3,2},{4,5},{5,4},{6,7},{7,6},{8,9},{9,8},{10,11... | collective-permute-start | bytes 1572872 | tf_op jit(solution)/shard_map/ppermute | solution.py:340
  16.8 27.9 %copy-start.1 = (f32[16,1024]{1,0:T(8,128)S(1)}, f32[16,1024]{1,0:T(8,128)}, u32[]{:S(2)}) copy-start(f32[16,1024]{1,0:T(8,128)} %old_ref.1) | copy-start | bytes 196612
  16.8 13.2 %collective-permute-start.4 = (bf16[512,256]{1,0:T(8,128)(2,1)S(1)}, bf16[512,256]{1,0:T(8,128)(2,1)S(1)}, u32[]{:S(2)}, u32[]{:S(2)}) collective-permute-start(bf16[512,256]{1,0:T(8,128)(2,1)S(1)} %get-tuple-element.24), channel_id=1, source_target_pairs={{0,2},{1,3},{2,0},{3,1},{4,6},{5,7},{6,4},{7,5},{8,10},{9,11},{10,... | collective-permute-start | bytes 786440 | tf_op jit(solution)/shard_map/ppermute | solution.py:340
  30.8 13.9 %all-to-all-start.1 = ((bf16[32,16,256]{2,1,0:T(8,128)(2,1)}), bf16[32,16,256]{2,1,0:T(8,128)(2,1)S(1)}, u32[]{:S(2)}, u32[]{:S(2)}) async-start(bf16[32,16,256]{2,1,0:T(8,128)(2,1)} %bitcast.4), calls=%async_computation.1 | async-start | bytes 524288 | tf_op jit(solution)/shard_map/all_to_all | solution.py:423
  34.1 2.0 %collective-permute-start = (f32[64,256]{1,0:T(8,128)S(1)}, f32[64,256]{1,0:T(8,128)S(1)}, u32[]{:S(2)}, u32[]{:S(2)}) collective-permute-start(f32[64,256]{1,0:T(8,128)S(1)} %get-tuple-element.16), channel_id=1, source_target_pairs={{0,1},{1,0},{2,3},{3,2},{4,5},{5,4},{6,7},{7,6},{8,9},{9,8},{10,11... | collective-permute-start | bytes 196616 | tf_op jit(solution)/shard_map/ppermute | solution.py:340
  34.4 6.5 %collective-permute-start.1 = (f32[64,256]{1,0:T(8,128)S(1)}, f32[64,256]{1,0:T(8,128)S(1)}, u32[]{:S(2)}, u32[]{:S(2)}) collective-permute-start(f32[64,256]{1,0:T(8,128)S(1)} %get-tuple-element.17), channel_id=1, source_target_pairs={{0,2},{1,3},{2,0},{3,1},{4,6},{5,7},{6,4},{7,5},{8,10},{9,11},{10,... | collective-permute-start | bytes 196616 | tf_op jit(solution)/shard_map/ppermute | solution.py:340
  36.1 5.4 %collective-permute-start.2 = (f32[64,256]{1,0:T(8,128)S(1)}, f32[64,256]{1,0:T(8,128)S(1)}, u32[]{:S(2)}, u32[]{:S(2)}) collective-permute-start(f32[64,256]{1,0:T(8,128)S(1)} %get-tuple-element.18), channel_id=1, source_target_pairs={{0,3},{1,2},{2,1},{3,0},{4,7},{5,6},{6,5},{7,4},{8,11},{9,10},{10,... | collective-permute-start | bytes 196616 | tf_op jit(solution)/shard_map/ppermute | solution.py:340

commit v8 on v6

--- a/solution.py
+++ b/solution.py
@@ -306,16 +306,21 @@
         ref[...] = rows_of(step)
 
 
-def finish_kernel(sizes, got_ref, count_ref, old_ref, out_ref):
+def finish_kernel(sizes, got_ref, count_ref, old_ref, out_hbm, out_ref, sems):
     owners, cents, capacity, longest, code_total = sizes
     share = got_ref.shape[2]
     prior = jnp.concatenate([count_ref[...] + code_prior] * (share // LANES), axis=1)
+    out = []
     for cent in range(cents):
         total = got_ref[cent].astype(f32)
         for owner in range(1, owners):
             total = total + got_ref[owner * cents + cent].astype(f32)
         lanes = slice(cent * share, (cent + 1) * share)
-        out_ref[:, lanes] = (total + code_prior * old_ref[:, lanes]) / prior
+        out_ref[cent] = (total + code_prior * old_ref[:, lanes]) / prior
+        out.append(pltpu.make_async_copy(out_ref.at[cent], out_hbm.at[:, lanes], sems.at[cent]))
+        out[-1].start()
+    for copy in out:
+        copy.wait()
 
 
 def join_kernel(here_ref, beside_ref, across_ref, diagonal_ref, out_ref):
@@ -441,7 +446,11 @@
         functools.partial(finish_kernel, sizes),
         out_shape=jax.ShapeDtypeStruct((part, features), f32),
         in_specs=[vmem] * 3,
-        out_specs=vmem,
+        out_specs=hbm,
+        scratch_shapes=[
+            pltpu.VMEM((cents, part, share), f32),
+            pltpu.SemaphoreType.DMA((cents,)),
+        ],
         compiler_params=params,
         name="finish",
     )(last, count, old_codes)

time: 45.6 us -> 45.7 us (level)
  no operation moved by 1% of the time
where the time goes in v8:
time: 45.7 us; the launch traced here: 45.3 us
  waiting for transfers between devices  16.7 us (37%)
  starting transfers between devices  14.6 us (32%)
  Pallas kernels  11.7 us (26%)
  other arithmetic  1.56 us (3%)
  between operations  0.71 us (2%)
    all_to_all x1, waiting for transfers between devices, summed_body(): lax.all_to_all(send.reshape(devices, chunk, share // 2), ('dp', 'cent'),...  8.85 us
    all_to_all x1, starting transfers between devices, summed_body(): lax.all_to_all(send.reshape(devices, chunk, share // 2), ('dp', 'cent'),...  7.3 us
    ppermute x5, waiting for transfers between devices, summed_body(): lax.ppermute(array, 'cent', [(index, index ^ bit) for index in range(cent...  5.35 us
    ppermute x5, starting transfers between devices, summed_body(): lax.ppermute(array, 'cent', [(index, index ^ bit) for index in range(cent...  4 us
    pallas_call x1, Pallas kernels, summed_body(): pl.pallas_call(functools.partial(pool_kernel, sizes), out_shape=(jax.Shap...  3.37 us
    all_to_all x1, starting transfers between devices, summed_body(): lax.all_to_all(sums.reshape(devices, part, share), ('dp', 'cent'), 0, 0,...  3.31 us
    pallas_call x1, Pallas kernels, summed_body(): pl.pallas_call(functools.partial(give_kernel, sizes), out_shape=(jax.Shap...  2.62 us
    all_to_all x1, waiting for transfers between devices, summed_body(): lax.all_to_all(sums.reshape(devices, part, share), ('dp', 'cent'), 0, 0,...  2.52 us
  transfers between devices with their start and end apart: 7, of which 4 were waited for; matrix products, arithmetic and copies ran while one was open for 2% of the time, Pallas kernels for 17%

profile of v8, /device:TPU:0, one launch (start us, length us, event | category | flops | bytes accessed | tf_op | source)
XLA Modules:
  0.0 45.3 jit_solution(9073997851329578802)
XLA Ops:
  0.6 0.0 copy-start
  0.6 3.4 %pool.1 = (bf16[8,4,72,128]{3,2,1,0:T(8,128)(2,1)}, bf16[256,1024]{1,0:T(8,128)(2,1)S(1)}, bf16[256,1024]{1,0:T(8,128)(2,1)S(1)}) custom-call(s32[1,128]{1,0:T(1,128)} %length_hbm.1, s32[1,128]{1,0:T(1,128)} %owner_hbm.1, s32[1,128]{1,0:T(1,128)} %cluster_hbm.1, s32[1,1024]{1,0:T(1,128)} %bitcast.13, bf16[1024,1024]{1,0:T(8,128)(2,1)} %frames_hbm.5), custom_call_target="tpu_custom_call" | custom-call | tf_op jit(solution)/shard_map/pool/pallas_call | solution.py:359
  4.0 7.3 %all-to-all-start = ((bf16[32,72,128]{2,1,0:T(8,128)(2,1)}), bf16[32,72,128]{2,1,0:T(8,128)(2,1)S(1)}, u32[]{:S(2)}, u32[]{:S(2)}) async-start(bf16[32,72,128]{2,1,0:T(8,128)(2,1)} %bitcast.1), calls=%async_computation | async-start | bytes 1179648 | tf_op jit(solution)/shard_map/all_to_all | solution.py:378
  11.3 2.6 %give.1 = (bf16[2,512,256]{2,1,0:T(8,128)(2,1)S(1)}, bf16[512,1024]{1,0:T(8,128)(2,1)S(1)}, bf16[512,256]{1,0:T(8,128)(2,1)S(1)}) custom-call(s32[1,1024]{1,0:T(1,128)} %bitcast.14, bf16[1024,1024]{1,0:T(8,128)(2,1)} %frames_hbm.5, bf16[256,1024]{1,0:T(8,128)(2,1)S(1)} %get-tuple-element.20.pooled_ref, bf16[256,1024]{1,0:T(8,128)(2,1)S(1)} %get-tuple-element.21.member_ref), custom_call_target="tpu_custom_call" | custom-call | flops 1073741824 | bytes 4194304 | tf_op jit(solution)/shard_map/give/pallas_call | solution.py:382
  14.0 0.3 collective-permute-start.3
  14.3 2.5 %keep.1 = f32[2,512,256]{2,1,0:T(8,128)S(1)} custom-call(bf16[1024,1024]{1,0:T(8,128)(2,1)} %frames_hbm.5, bf16[256,1024]{1,0:T(8,128)(2,1)S(1)} %get-tuple-element.20.pooled_ref, bf16[512,1024]{1,0:T(8,128)(2,1)S(1)} %get-tuple-element.22.matches_ref, bf16[512,256]{1,0:T(8,128)(2,1)S(1)} %get-tuple-element.23.counts_ref), custom_call_target="tpu_custom_call" | custom-call | flops 1073741824 | bytes 4194304 | tf_op jit(solution)/shard_map/keep/pallas_call | solution.py:401
  16.8 0.0 collective-permute-done.3
  16.8 0.8 %fusion.5 = bf16[512,256]{1,0:T(8,128)(2,1)} fusion(f32[2,512,256]{2,1,0:T(8,128)S(1)} %keep.1, bf16[2,512,256]{2,1,0:T(8,128)(2,1)S(1)} %collective-permute-done.3), kind=kLoop, calls=%fused_computation.7 | loop fusion | flops 393216 | bytes 1048576 | tf_op jit(solution)/shard_map/convert_element_type | solution.py:418
  17.5 0.0 copy-start.1
  17.5 1.7 %collective-permute-start.4 = (bf16[512,256]{1,0:T(8,128)(2,1)}, bf16[512,256]{1,0:T(8,128)(2,1)S(1)}, u32[]{:S(2)}, u32[]{:S(2)}) collective-permute-start(bf16[512,256]{1,0:T(8,128)(2,1)} %fusion.5), channel_id=1, source_target_pairs={{0,2},{1,3},{2,0},{3,1},{4,6},{5,7},{6,4},{7,5},{8,10},{9,11},{10,... | collective-permute-start | bytes 786440 | tf_op jit(solution)/shard_map/ppermute | solution.py:353
  19.2 0.0 copy-done
  19.2 8.8 %all-to-all-done.got_ref = bf16[32,72,128]{2,1,0:T(8,128)(2,1)S(1)} async-done(((bf16[32,72,128]{2,1,0:T(8,128)(2,1)}), bf16[32,72,128]{2,1,0:T(8,128)(2,1)S(1)}, u32[]{:S(2)}, u32[]{:S(2)}) %all-to-all-start) | async-done | bytes 589856 | tf_op jit(solution)/shard_map/all_to_all | solution.py:378
  28.1 1.8 %owner.1 = (f32[512,256]{1,0:T(8,128)S(1)}, f32[16,128]{1,0:T(8,128)S(1)}, f32[64,256]{1,0:T(8,128)S(1)}, f32[64,256]{1,0:T(8,128)S(1)}, f32[64,256]{1,0:T(8,128)S(1)}, /*index=5*/f32[64,256]{1,0:T(8,128)S(1)}) custom-call(bf16[32,72,128]{2,1,0:T(8,128)(2,1)S(1)} %all-to-all-done.got_ref, bf16[256,256]{1,0:T(8,128)(2,1)S(1)} %constant_dynamic-slice_fusion.old_ref), custom_call_target="tpu_custom_call" | custom-call | tf_op jit(solution)/shard_map/owner/pallas_call | solution.py:422
  29.9 0.0 collective-permute-done.4
  29.9 0.8 %fusion.4 = bf16[512,256]{1,0:T(8,128)(2,1)} fusion(f32[512,256]{1,0:T(8,128)S(1)} %get-tuple-element.19, f32[2,512,256]{2,1,0:T(8,128)S(1)} %keep.1, bf16[512,256]{1,0:T(8,128)(2,1)S(1)} %collective-permute-done.4, bf16[2,512,256]{2,1,0:T(8,128)(2,1)S(1)} %collective-permute-done.3), kind=kLoop, calls=%fused_computation.6 | loop fusion | flops 786432 | bytes 1835008 | tf_op jit(solution)/shard_map/convert_element_type | solution.py:435
  30.7 3.3 %all-to-all-start.1 = ((bf16[32,16,256]{2,1,0:T(8,128)(2,1)}), bf16[32,16,256]{2,1,0:T(8,128)(2,1)S(1)}, u32[]{:S(2)}, u32[]{:S(2)}) async-start(bf16[32,16,256]{2,1,0:T(8,128)(2,1)} %bitcast.4), calls=%async_computation.1 | async-start | bytes 524288 | tf_op jit(solution)/shard_map/all_to_all | solution.py:436
  34.0 0.3 collective-permute-start
  34.4 1.7 %collective-permute-start.1 = (f32[64,256]{1,0:T(8,128)S(1)}, f32[64,256]{1,0:T(8,128)S(1)}, u32[]{:S(2)}, u32[]{:S(2)}) collective-permute-start(f32[64,256]{1,0:T(8,128)S(1)} %get-tuple-element.17), channel_id=1, source_target_pairs={{0,2},{1,3},{2,0},{3,1},{4,6},{5,7},{6,4},{7,5},{8,10},{9,11},{10,... | collective-permute-start | bytes 196616 | tf_op jit(solution)/shard_map/ppermute | solution.py:353
  36.0 0.0 collective-permute-start.2
  36.1 0.0 collective-permute-done.beside_ref
  36.1 4.8 %collective-permute-done.1.across_ref = f32[64,256]{1,0:T(8,128)S(1)} collective-permute-done((f32[64,256]{1,0:T(8,128)S(1)}, f32[64,256]{1,0:T(8,128)S(1)}, u32[]{:S(2)}, u32[]{:S(2)}) %collective-permute-start.1) | collective-permute-done | bytes 65568 | tf_op jit(solution)/shard_map/ppermute | solution.py:353
  40.9 0.5 %collective-permute-done.2.diagonal_ref = f32[64,256]{1,0:T(8,128)S(1)} collective-permute-done((f32[64,256]{1,0:T(8,128)S(1)}, f32[64,256]{1,0:T(8,128)S(1)}, u32[]{:S(2)}, u32[]{:S(2)}) %collective-permute-start.2) | collective-permute-done | bytes 65568 | tf_op jit(solution)/shard_map/ppermute | solution.py:353
  41.4 0.7 %join.1 = f32[64,1024]{1,0:T(8,128)} custom-call(f32[64,256]{1,0:T(8,128)S(1)} %get-tuple-element.15.here_ref, f32[64,256]{1,0:T(8,128)S(1)} %collective-permute-done.beside_ref, f32[64,256]{1,0:T(8,128)S(1)} %collective-permute-done.1.across_ref, f32[64,256]{1,0:T(8,128)S(1)} %collective-permute-done.2.diagonal_ref), custom_call_target="tpu_custom_call" | custom-call | tf_op jit(solution)/shard_map/join/pallas_call | solution.py:437
  42.1 2.5 %all-to-all-done.1.got_ref = bf16[32,16,256]{2,1,0:T(8,128)(2,1)S(1)} async-done(((bf16[32,16,256]{2,1,0:T(8,128)(2,1)}), bf16[32,16,256]{2,1,0:T(8,128)(2,1)S(1)}, u32[]{:S(2)}, u32[]{:S(2)}) %all-to-all-start.1) | async-done | bytes 262176 | tf_op jit(solution)/shard_map/all_to_all | solution.py:436
  44.6 0.0 copy-done.1
  44.6 0.7 %finish.1 = f32[16,1024]{1,0:T(8,128)} custom-call(bf16[32,16,256]{2,1,0:T(8,128)(2,1)S(1)} %all-to-all-done.1.got_ref, f32[16,128]{1,0:T(8,128)S(1)} %get-tuple-element.25.count_ref, f32[16,1024]{1,0:T(8,128)S(1)} %copy-done.1), custom_call_target="tpu_custom_call" | custom-call | tf_op jit(solution)/shard_map/finish/pallas_call | solution.py:445
  (1 shorter events, 0.0 us)
Async XLA Ops:
  0.6 18.6 %copy-start = (bf16[256,1024]{1,0:T(8,128)(2,1)S(1)}, bf16[256,1024]{1,0:T(8,128)(2,1)}, u32[]{:S(2)}) copy-start(bf16[256,1024]{1,0:T(8,128)(2,1)} %param.12) | copy-start | bytes 1572868
  4.0 24.1 %all-to-all-start = ((bf16[32,72,128]{2,1,0:T(8,128)(2,1)}), bf16[32,72,128]{2,1,0:T(8,128)(2,1)S(1)}, u32[]{:S(2)}, u32[]{:S(2)}) async-start(bf16[32,72,128]{2,1,0:T(8,128)(2,1)} %bitcast.1), calls=%async_computation | async-start | bytes 1179648 | tf_op jit(solution)/shard_map/all_to_all | solution.py:378
  14.0 2.8 %collective-permute-start.3 = (bf16[2,512,256]{2,1,0:T(8,128)(2,1)S(1)}, bf16[2,512,256]{2,1,0:T(8,128)(2,1)S(1)}, u32[]{:S(2)}, u32[]{:S(2)}) collective-permute-start(bf16[2,512,256]{2,1,0:T(8,128)(2,1)S(1)} %get-tuple-element.24), channel_id=1, source_target_pairs={{0,1},{1,0},{2,3},{3,2},{4,5},{5,4},{6,7},{7,6},{8,9},{9,8},{10,11... | collective-permute-start | bytes 1572872 | tf_op jit(solution)/shard_map/ppermute | solution.py:353
  17.5 27.1 %copy-start.1 = (f32[16,1024]{1,0:T(8,128)S(1)}, f32[16,1024]{1,0:T(8,128)}, u32[]{:S(2)}) copy-start(f32[16,1024]{1,0:T(8,128)} %old_ref.1) | copy-start | bytes 196612
  17.5 12.4 %collective-permute-start.4 = (bf16[512,256]{1,0:T(8,128)(2,1)}, bf16[512,256]{1,0:T(8,128)(2,1)S(1)}, u32[]{:S(2)}, u32[]{:S(2)}) collective-permute-start(bf16[512,256]{1,0:T(8,128)(2,1)} %fusion.5), channel_id=1, source_target_pairs={{0,2},{1,3},{2,0},{3,1},{4,6},{5,7},{6,4},{7,5},{8,10},{9,11},{10,... | collective-permute-start | bytes 786440 | tf_op jit(solution)/shard_map/ppermute | solution.py:353
  30.7 13.9 %all-to-all-start.1 = ((bf16[32,16,256]{2,1,0:T(8,128)(2,1)}), bf16[32,16,256]{2,1,0:T(8,128)(2,1)S(1)}, u32[]{:S(2)}, u32[]{:S(2)}) async-start(bf16[32,16,256]{2,1,0:T(8,128)(2,1)} %bitcast.4), calls=%async_computation.1 | async-start | bytes 524288 | tf_op jit(solution)/shard_map/all_to_all | solution.py:436
  34.0 2.0 %collective-permute-start = (f32[64,256]{1,0:T(8,128)S(1)}, f32[64,256]{1,0:T(8,128)S(1)}, u32[]{:S(2)}, u32[]{:S(2)}) collective-permute-start(f32[64,256]{1,0:T(8,128)S(1)} %get-tuple-element.16), channel_id=1, source_target_pairs={{0,1},{1,0},{2,3},{3,2},{4,5},{5,4},{6,7},{7,6},{8,9},{9,8},{10,11... | collective-permute-start | bytes 196616 | tf_op jit(solution)/shard_map/ppermute | solution.py:353
  34.4 6.5 %collective-permute-start.1 = (f32[64,256]{1,0:T(8,128)S(1)}, f32[64,256]{1,0:T(8,128)S(1)}, u32[]{:S(2)}, u32[]{:S(2)}) collective-permute-start(f32[64,256]{1,0:T(8,128)S(1)} %get-tuple-element.17), channel_id=1, source_target_pairs={{0,2},{1,3},{2,0},{3,1},{4,6},{5,7},{6,4},{7,5},{8,10},{9,11},{10,... | collective-permute-start | bytes 196616 | tf_op jit(solution)/shard_map/ppermute | solution.py:353
  36.0 5.4 %collective-permute-start.2 = (f32[64,256]{1,0:T(8,128)S(1)}, f32[64,256]{1,0:T(8,128)S(1)}, u32[]{:S(2)}, u32[]{:S(2)}) collective-permute-start(f32[64,256]{1,0:T(8,128)S(1)} %get-tuple-element.18), channel_id=1, source_target_pairs={{0,3},{1,2},{2,1},{3,0},{4,7},{5,6},{6,5},{7,4},{8,11},{9,10},{10,... | collective-permute-start | bytes 196616 | tf_op jit(solution)/shard_map/ppermute | solution.py:353
